TPU v7x, 256 devices: a whole 4x4x8 slice. The times are simulated.
256 devices in a mesh: leaf: 128 (over x, y, z), sep: 2 (over core).
Axes of the slice: x: 4, y: 4, z: 8, core: 2. Of those that a mesh axis runs over, the one named last changes fastest.
Arguments:
- leaf_rhs: float32 [128, 16, 2048], P('leaf', None, 'sep'), may hold values from -6 to 6
- leaf_inverse: float32 [128, 2048, 2048], P('leaf', 'sep'), may hold values from -0.125 to 0.125
- skeleton_index: int32 [128, 3, 128], P('leaf'), may hold values from 0 to 2047, as said below
- leaf_coupling: float32 [128, 3, 128, 128], P('leaf'), may hold values from -0.046875 to 0.046875
- sep_rhs: float32 [7, 16, 128], replicated, may hold values from -6 to 6
- sep_inverse: float32 [7, 128, 128], replicated, may hold values from -0.5 to 0.5
- sep_parent: float32 [6, 128, 128], replicated, may hold values from -0.5 to 0.5
Outputs:
- leaf_solution: float32 [128, 16, 2048], P('leaf', None, 'sep')
- sep_solution: float32 [128, 3, 16, 128], P('leaf')
Inputs may be any that keep to these rules, and one draw needn't show every extreme that they name: `skeleton_index`: the 128 rows of one leaf and level are distinct.
All inputs are finite; a program needn't handle non-finite values.
Results may differ from a plain program's by a relative error of at most 0.0001.
Values sent between devices are 32-bit elements; how exact they have to be, the bound alone decides.
No kernel may reach another device: no remote copies, remote signals or barrier semaphores. Data moves between devices by JAX's collectives and lax.ppermute only.
A program may use at most 64 MiB of HBM per device.

v0:
```python
import jax
import jax.numpy as jnp
from jax import lax
from jax.sharding import PartitionSpec as P

HIGH = lax.Precision.HIGHEST


def from_partner(x, axis, bit):
    return lax.ppermute(x, axis, [(i, i ^ 1 << bit) for i in range(lax.axis_size(axis))])


def local(leaf_rhs, leaf_inverse, skeleton_index, leaf_coupling, sep_rhs, sep_inverse, sep_parent):
    n_leaf = lax.axis_size("leaf")
    my_leaf = lax.axis_index("leaf")
    my_side = lax.axis_index("sep")
    levels = skeleton_index.shape[1]
    width_k = sep_rhs.shape[2]
    count_sep = sep_rhs.shape[0]
    count_rhs = leaf_rhs.shape[1]
    half = leaf_rhs.shape[2]
    inverse = leaf_inverse[0]
    coupling = leaf_coupling[0]
    columns = inverse
    u_half = jnp.einsum(
        "nc,rc->nr", lax.all_gather(leaf_rhs[0], "sep", axis=1, tiled=True), columns, precision=HIGH
    )
    local_index = skeleton_index[0] - my_side * half
    inside = ((local_index >= 0) & (local_index < half)).astype(jnp.float32)
    safe_index = jnp.clip(local_index, 0, half - 1).reshape(-1)
    picked = u_half[:, safe_index].reshape(count_rhs, levels, width_k) * inside[None]
    term = jnp.einsum("ljk,nlk->lnj", coupling, picked, precision=HIGH)
    term = lax.psum(term, "sep")
    widths = [n_leaf // 2 ** (levels - 1 - level) for level in range(levels)]
    nodes = []
    for level in range(levels):
        offset = 2**levels - 2 ** (levels - level)
        nodes.append(offset + my_leaf // widths[level])
    slots = lax.broadcasted_iota(jnp.int32, (count_sep,), 0)
    table = jnp.zeros((count_sep, count_rhs, width_k), jnp.float32)
    for level in range(levels):
        marker = (slots == nodes[level]).astype(jnp.float32)
        table = table + marker[:, None, None] * term[level][None]
    table = lax.psum(table, "leaf")
    summed = [table[nodes[level]] for level in range(levels)]
    forward = []
    for level in range(levels):
        node = nodes[level]
        source = sep_rhs[node] - summed[level]
        if level > 0:
            child = nodes[level - 1]
            mine = jnp.einsum("jk,nk->nj", sep_parent[child], forward[-1], precision=HIGH)
            other = from_partner(mine, "leaf", widths[level - 1].bit_length() - 1)
            source = source - (mine + other)
        forward.append(jnp.einsum("jk,nk->nj", sep_inverse[node], source, precision=HIGH))
    backward = [None] * levels
    for level in reversed(range(levels)):
        target = forward[level]
        if level < levels - 1:
            target = target - jnp.einsum(
                "jk,nj->nk", sep_parent[nodes[level]], backward[level + 1], precision=HIGH
            )
        backward[level] = jnp.einsum("jk,nj->nk", sep_inverse[nodes[level]], target, precision=HIGH)
    solved = jnp.stack(backward, axis=0)
    correction = jnp.einsum("ljk,lnj->nlk", coupling, solved, precision=HIGH) * inside[None]
    adjusted = u_half.at[:, safe_index].add(-correction.reshape(count_rhs, levels * width_k))
    columns = inverse
    result = lax.psum_scatter(
        jnp.einsum("nr,rc->cn", adjusted, columns, precision=HIGH),
        "sep",
        scatter_dimension=0,
        tiled=True,
    )
    return (result.T[None], solved[None])


def solution(mesh):
    placed = (
        P("leaf", None, "sep"),
        P("leaf", "sep", None),
        P("leaf", None, None),
        P("leaf", None, None, None),
        P(),
        P(),
        P(),
    )
    return jax.shard_map(
        local,
        mesh=mesh,
        in_specs=placed,
        out_specs=(P("leaf", None, "sep"), P("leaf", None, None, None)),
        check_vma=False,
    )
```

profile of v0, /device:TPU:1, one launch (start us, length us, event | category | flops | bytes accessed | tf_op | source)
XLA Modules:
  0.0 752.7 jit_solution(18262284448915210104)
XLA Ops:
  7.3 0.8 and_convert_fusion
  8.0 0.7 fusion.65
  8.8 5.1 all-gather
  13.9 9.0 %fusion.2 = f32[16,1024]{0,1:T(8,128)S(1)} fusion(f32[1,1024,2048]{2,1,0:T(8,128)} %param.8, f32[1,16,2048]{2,1,0:T(8,128)S(1)} %all-gather), kind=kOutput, calls=%fused_computation.4 | convolution fusion | flops 402653184 | bytes 8585216 | tf_op jit(solution)/shard_map/nc,rc->nr/dot_general | solution.py:25
  22.9 1.1 gather_fusion
  24.2 0.4 fusion.10
  24.6 3.6 psum.14
  28.3 580.4 %psum.15 = f32[7,16,128]{2,1,0:T(8,128)S(1)} all-reduce(f32[7,16,128]{2,1,0:T(8,128)S(1)} %multiply_add_fusion), channel_id=1, replica_groups=mesh['leaf'=128,'sep'=2] {'leaf'}, use_global_device_ids=true, to_apply=%region_1.2 | all-reduce | flops 14336 | bytes 114688 | tf_op jit(solution)/shard_map/psum | solution.py:44
  608.7 0.9 fusion.28
  609.6 0.2 fusion.25
  609.9 2.8 collective-permute-done
  612.6 0.9 fusion.22
  613.5 0.2 fusion.18
  613.8 4.0 collective-permute-done.1
  617.8 0.9 fusion.15
  618.7 0.2 fusion.13
  618.9 0.2 convolution_subtract_fusion.1
  619.1 0.2 fusion.20
  619.2 0.2 convolution_subtract_fusion
  619.6 0.3 fusion.8
  620.0 2.8 scatter_fusion
  622.9 7.0 fusion.4
  629.9 0.6 fusion.41
  630.5 115.3 %reduce-scatter.2.cloned.1.call-done = f32[1024,16]{0,1:T(8,128)} async-done(((f32[2048,16]{0,1:T(8,128)}), f32[1024,16]{0,1:T(8,128)}) %reduce-scatter.2.cloned.1.call-update) | async-done | bytes 65552 | tf_op jit(solution)/shard_map/reduce_scatter | solution.py:68
  (20 shorter events, 0.6 us)
Async XLA Ops:
  7.2 601.5 %copy-start = (f32[7,128,128]{2,1,0:T(8,128)S(1)}, f32[7,128,128]{2,1,0:T(8,128)}, u32[]{:S(2)}) copy-start(f32[7,128,128]{2,1,0:T(8,128)} %param.12) | copy-start | bytes 1376260
  7.2 17.0 %copy-start.1 = (f32[1,3,128,128]{3,2,1,0:T(8,128)S(1)}, f32[1,3,128,128]{3,2,1,0:T(8,128)}, u32[]{:S(2)}) copy-start(f32[1,3,128,128]{3,2,1,0:T(8,128)} %param.10) | copy-start | bytes 589828
  7.2 602.4 %copy-start.2 = (f32[6,128,128]{2,1,0:T(8,128)S(1)}, f32[6,128,128]{2,1,0:T(8,128)}, u32[]{:S(2)}) copy-start(f32[6,128,128]{2,1,0:T(8,128)} %param.13) | copy-start | bytes 1179652
  7.2 738.6 %reduce-scatter.2.cloned.1.call-start = ((), (), s32[]{:S(2)}) async-start(), calls=%async_computation.1 | async-start | bytes 196608 | tf_op jit(solution)/shard_map/reduce_scatter | solution.py:68
  609.8 2.8 collective-permute-start
  613.7 4.1 collective-permute-start.1
Sparse Core Ops, SparseCore 0:
  630.0 115.7 reduce-scatter.1
where the time goes:
time: 753 us
  blocking collectives  589 us (78%)
  waiting for transfers between devices  122 us (16%)
  matrix products  20.7 us (3%)
  between operations  14.3 us (2%)
    psum x1, blocking collectives, local(): table = lax.psum(table, 'leaf')  580 us
    reduce_scatter x1, waiting for transfers between devices, local(): lax.psum_scatter(jnp.einsum('nr,rc->cn', adjusted, columns, precision=HIG...  115 us
  transfers between devices with their start and end apart: 3, of which 3 were waited for; matrix products, arithmetic and copies ran while one was open for 0% of the time, Pallas kernels for 0%

commit v1 on v0

v1 whole, which is shorter than its diff:
```python
import jax
import jax.numpy as jnp
from jax import lax
from jax.sharding import PartitionSpec as P

HIGH = lax.Precision.HIGHEST


def swap_core(x):
    return lax.ppermute(x, "sep", [(0, 1), (1, 0)])


def swap_leaf(x, mask):
    return lax.ppermute(x, "leaf", [(i, i ^ mask) for i in range(lax.axis_size("leaf"))])


def local(leaf_rhs, leaf_inverse, skeleton_index, leaf_coupling, sep_rhs, sep_inverse, sep_parent):
    n_leaf = lax.axis_size("leaf")
    my_leaf = lax.axis_index("leaf")
    my_side = lax.axis_index("sep")
    levels = skeleton_index.shape[1]
    width_k = sep_rhs.shape[2]
    count_rhs = leaf_rhs.shape[1]
    half = leaf_rhs.shape[2]
    inverse = leaf_inverse[0]
    coupling = leaf_coupling[0]
    mine = leaf_rhs[0]
    theirs = swap_core(mine)
    low = jnp.where(my_side == 0, mine, theirs)
    high = jnp.where(my_side == 0, theirs, mine)
    u_half = jnp.einsum(
        "nc,rc->nr", jnp.concatenate([low, high], axis=1), inverse, precision=HIGH
    )
    local_index = skeleton_index[0] - my_side * half
    inside = ((local_index >= 0) & (local_index < half)).astype(jnp.float32)
    safe_index = jnp.clip(local_index, 0, half - 1).reshape(-1)
    picked = u_half[:, safe_index].reshape(count_rhs, levels, width_k) * inside[None]
    term = jnp.einsum("ljk,nlk->lnj", coupling, picked, precision=HIGH)
    term = term + swap_core(term)
    for mask in (1, 2, 6, 8, 24):
        term = term + swap_leaf(term, mask)
    summed = [term[0]]
    upper = term[1:] + swap_leaf(term[1:], 32)
    summed.append(upper[0])
    summed.append(upper[1] + swap_leaf(upper[1], 96))
    nodes = []
    for level in range(levels):
        nodes.append(2**levels - 2 ** (levels - level) + my_leaf // (n_leaf // 2 ** (levels - 1 - level)))
    forward = []
    for level in range(levels):
        node = nodes[level]
        source = sep_rhs[node] - summed[level]
        if level > 0:
            child = nodes[level - 1]
            own = jnp.einsum("jk,nk->nj", sep_parent[child], forward[-1], precision=HIGH)
            source = source - (own + swap_leaf(own, 32 if level == 1 else 96))
        forward.append(jnp.einsum("jk,nk->nj", sep_inverse[node], source, precision=HIGH))
    backward = [None] * levels
    for level in reversed(range(levels)):
        target = forward[level]
        if level < levels - 1:
            target = target - jnp.einsum(
                "jk,nj->nk", sep_parent[nodes[level]], backward[level + 1], precision=HIGH
            )
        backward[level] = jnp.einsum("jk,nj->nk", sep_inverse[nodes[level]], target, precision=HIGH)
    solved = jnp.stack(backward, axis=0)
    correction = jnp.einsum("ljk,lnj->nlk", coupling, solved, precision=HIGH) * inside[None]
    adjusted = u_half.at[:, safe_index].add(-correction.reshape(count_rhs, levels * width_k))
    result = jnp.einsum("nr,rc->nc", adjusted, inverse, precision=HIGH)
    keep = jnp.where(my_side == 0, result[:, :half], result[:, half:])
    send = jnp.where(my_side == 0, result[:, half:], result[:, :half])
    return ((keep + swap_core(send))[None], solved[None])


def solution(mesh):
    placed = (
        P("leaf", None, "sep"),
        P("leaf", "sep", None),
        P("leaf", None, None),
        P("leaf", None, None, None),
        P(),
        P(),
        P(),
    )
    return jax.shard_map(
        local,
        mesh=mesh,
        in_specs=placed,
        out_specs=(P("leaf", None, "sep"), P("leaf", None, None, None)),
        check_vma=False,
    )
```

time: 753 us -> 68.4 us (0.09)
  blocking collectives: 589 us -> 0 us
  waiting for transfers between devices: 122 us -> 12.2 us
  starting transfers between devices: 0.1 us -> 27.1 us
  between operations: 14.3 us -> 0.8 us
    psum x2 -> x0, blocking collectives: 584 us -> none  [the longest x1 580 us: local(): table = lax.psum(table, 'leaf')]
    reduce_scatter x1 -> x0, waiting for transfers between devices: 115 us -> none  [local(): lax.psum_scatter(jnp.einsum('nr,rc->cn', adjusted, columns, precision=HIG...]
    ppermute x2 -> x12, starting transfers between devices: 0.07 us -> 27.1 us  [the longest x9 15.7 us: swap_leaf(): lax.ppermute(x, 'leaf', [(i, i ^ mask) for i in range(lax.axis_size('leaf...]
  transfers between devices with their start and end apart: 3 -> 12, of which waited for: 3 -> 8; matrix products, arithmetic and copies ran while one was open for 0% -> 6% of each run, Pallas kernels for 0% -> 0%
where the time goes in v1:
time: 68.4 us; the launch traced here: 68.1 us
  starting transfers between devices  27.1 us (40%)
  matrix products  20.1 us (29%)
  waiting for transfers between devices  12.2 us (18%)
  other arithmetic  6.55 us (10%)
  local copies, waits for them, and re-layouts  1.38 us (2%)
  between operations  0.8 us (1%)
    ppermute x9, starting transfers between devices, swap_leaf(): lax.ppermute(x, 'leaf', [(i, i ^ mask) for i in range(lax.axis_size('leaf...  15.7 us
    ppermute x3, starting transfers between devices, swap_core(): return lax.ppermute(x, 'sep', [(0, 1), (1, 0)])  11.4 us
    ppermute x9, waiting for transfers between devices, swap_leaf(): lax.ppermute(x, 'leaf', [(i, i ^ mask) for i in range(lax.axis_size('leaf...  10.8 us
    dot_general x1, matrix products, local(): jnp.einsum('nc,rc->nr', jnp.concatenate([low, high], axis=1), inverse, pr...  9.01 us
    dot_general x1, matrix products, local(): result = jnp.einsum('nr,rc->nc', adjusted, inverse, precision=HIGH)  6.41 us
    scatter-add x1, other arithmetic, local(): u_half.at[:, safe_index]  3.01 us
    dot_general x3, matrix products, local(): jnp.einsum('jk,nk->nj', sep_inverse[node], source, precision=HIGH)  2.61 us
    ppermute x3, waiting for transfers between devices, swap_core(): return lax.ppermute(x, 'sep', [(0, 1), (1, 0)])  1.37 us
  transfers between devices with their start and end apart: 12, of which 8 were waited for; matrix products, arithmetic and copies ran while one was open for 6% of the time, Pallas kernels for 0%

profile of v1, /device:TPU:1, one launch (start us, length us, event | category | flops | bytes accessed | tf_op | source)
XLA Modules:
  0.0 68.1 jit_solution(7275927669516521718)
XLA Ops:
  0.7 3.3 %collective-permute-start = (f32[16,1024]{1,0:T(8,128)}, f32[16,1024]{1,0:T(8,128)S(1)}, u32[]{:S(2)}, u32[]{:S(2)}) collective-permute-start(f32[16,1024]{1,0:T(8,128)} %bitcast.95), channel_id=1, source_target_pairs={{0,1},{1,0},{2,3},{3,2},{4,5},{5,4},{6,7},{7,6},{8,9},{9,8},{10,11... | collective-permute-start | bytes 196616 | tf_op jit(solution)/shard_map/ppermute | solution.py:10
  5.4 0.9 %broadcast_select_fusion.1 = (f32[16,1024]{1,0:T(8,128)S(1)}, f32[16,1024]{1,0:T(8,128)S(1)}) fusion(f32[16,1024]{1,0:T(8,128)S(1)} %collective-permute-done, pred[]{:T(512)S(6)} %eq.2, f32[1,16,1024]{2,1,0:T(8,128)} %param.7), kind=kLoop, calls=%fused_computation.48 | loop fusion | flops 32768 | bytes 262145 | tf_op jit(solution)/shard_map/jit(_where)/select_n | solution.py:29
  6.3 9.0 %fusion.2 = f32[16,1024]{0,1:T(8,128)S(1)} fusion(f32[1,1024,2048]{2,1,0:T(8,128)} %param.8, f32[16,1024]{1,0:T(8,128)S(1)} %get-tuple-element.3, f32[16,1024]{1,0:T(8,128)S(1)} %get-tuple-element.2), kind=kOutput, calls=%fused_computation.4 | convolution fusion | flops 402685952 | bytes 8585216 | tf_op jit(solution)/shard_map/nc,rc->nr/dot_general | solution.py:31
  15.3 1.1 %gather_fusion = f32[384,16]{1,0:T(8,128)S(1)} fusion(f32[16,1024]{0,1:T(8,128)S(1)} %fusion.2, s32[1024]{0:T(1024)S(1)} %pad_clamp_fusion), kind=kCustom, calls=%fused_computation | custom fusion | bytes 50688 | tf_op jit(solution)/shard_map/gather | solution.py:37
  17.1 1.1 %collective-permute-done.1 = f32[3,16,128]{2,1,0:T(8,128)S(1)} collective-permute-done((f32[3,16,128]{2,1,0:T(8,128)S(1)}, f32[3,16,128]{2,1,0:T(8,128)S(1)}, u32[]{:S(2)}, u32[]{:S(2)}) %collective-permute-start.1) | collective-permute-done | bytes 24608 | tf_op jit(solution)/shard_map/ppermute | solution.py:10
  18.2 2.7 %collective-permute-done.2 = f32[3,16,128]{2,1,0:T(8,128)S(1)} collective-permute-done((f32[3,16,128]{2,1,0:T(8,128)S(1)}, f32[3,16,128]{2,1,0:T(8,128)S(1)}, u32[]{:S(2)}, u32[]{:S(2)}) %collective-permute-start.2) | collective-permute-done | bytes 24608 | tf_op jit(solution)/shard_map/ppermute | solution.py:14
  20.9 1.4 %collective-permute-start.3 = (f32[3,16,128]{2,1,0:T(8,128)S(1)}, f32[3,16,128]{2,1,0:T(8,128)S(1)}, u32[]{:S(2)}, u32[]{:S(2)}) collective-permute-start(f32[3,16,128]{2,1,0:T(8,128)S(1)} %add.84), channel_id=1, source_target_pairs={{0,4},{2,6},{4,0},{6,2},{8,12},{10,14},{12,8},{14,10},{16,20},{18,... | collective-permute-start | bytes 73736 | tf_op jit(solution)/shard_map/ppermute | solution.py:14
  22.3 2.2 %collective-permute-done.3 = f32[3,16,128]{2,1,0:T(8,128)S(1)} collective-permute-done((f32[3,16,128]{2,1,0:T(8,128)S(1)}, f32[3,16,128]{2,1,0:T(8,128)S(1)}, u32[]{:S(2)}, u32[]{:S(2)}) %collective-permute-start.3) | collective-permute-done | bytes 24608 | tf_op jit(solution)/shard_map/ppermute | solution.py:14
  24.5 4.3 %collective-permute-start.4 = (f32[3,16,128]{2,1,0:T(8,128)S(1)}, f32[3,16,128]{2,1,0:T(8,128)S(1)}, u32[]{:S(2)}, u32[]{:S(2)}) collective-permute-start(f32[3,16,128]{2,1,0:T(8,128)S(1)} %add.85), channel_id=1, source_target_pairs={{0,12},{2,14},{4,8},{6,10},{8,4},{10,6},{12,0},{14,2},{16,28},{18,... | collective-permute-start | bytes 73736 | tf_op jit(solution)/shard_map/ppermute | solution.py:14
  28.8 1.3 %collective-permute-done.4 = f32[3,16,128]{2,1,0:T(8,128)S(1)} collective-permute-done((f32[3,16,128]{2,1,0:T(8,128)S(1)}, f32[3,16,128]{2,1,0:T(8,128)S(1)}, u32[]{:S(2)}, u32[]{:S(2)}) %collective-permute-start.4) | collective-permute-done | bytes 24608 | tf_op jit(solution)/shard_map/ppermute | solution.py:14
  30.1 1.3 %collective-permute-start.5 = (f32[3,16,128]{2,1,0:T(8,128)S(1)}, f32[3,16,128]{2,1,0:T(8,128)S(1)}, u32[]{:S(2)}, u32[]{:S(2)}) collective-permute-start(f32[3,16,128]{2,1,0:T(8,128)S(1)} %add.86), channel_id=1, source_target_pairs={{0,16},{2,18},{4,20},{6,22},{8,24},{10,26},{12,28},{14,30},{16,0},... | collective-permute-start | bytes 73736 | tf_op jit(solution)/shard_map/ppermute | solution.py:14
  31.4 1.5 %collective-permute-done.5 = f32[3,16,128]{2,1,0:T(8,128)S(1)} collective-permute-done((f32[3,16,128]{2,1,0:T(8,128)S(1)}, f32[3,16,128]{2,1,0:T(8,128)S(1)}, u32[]{:S(2)}, u32[]{:S(2)}) %collective-permute-start.5) | collective-permute-done | bytes 24608 | tf_op jit(solution)/shard_map/ppermute | solution.py:14
  32.9 2.7 %collective-permute-start.6 = (f32[3,16,128]{2,1,0:T(8,128)S(1)}, f32[3,16,128]{2,1,0:T(8,128)S(1)}, u32[]{:S(2)}, u32[]{:S(2)}) collective-permute-start(f32[3,16,128]{2,1,0:T(8,128)S(1)} %add.87), channel_id=1, source_target_pairs={{0,48},{2,50},{4,52},{6,54},{8,56},{10,58},{12,60},{14,62},{16,32}... | collective-permute-start | bytes 73736 | tf_op jit(solution)/shard_map/ppermute | solution.py:14
  35.6 1.2 %collective-permute-done.6 = f32[3,16,128]{2,1,0:T(8,128)S(1)} collective-permute-done((f32[3,16,128]{2,1,0:T(8,128)S(1)}, f32[3,16,128]{2,1,0:T(8,128)S(1)}, u32[]{:S(2)}, u32[]{:S(2)}) %collective-permute-start.6) | collective-permute-done | bytes 24608 | tf_op jit(solution)/shard_map/ppermute | solution.py:14
  36.9 1.3 %collective-permute-start.7 = (f32[2,16,128]{2,1,0:T(8,128)S(1)}, f32[2,16,128]{2,1,0:T(8,128)S(1)}, u32[]{:S(2)}, u32[]{:S(2)}) collective-permute-start(f32[2,16,128]{2,1,0:T(8,128)S(1)} %slice.31), channel_id=1, source_target_pairs={{0,64},{2,66},{4,68},{6,70},{8,72},{10,74},{12,76},{14,78},{16,80}... | collective-permute-start | bytes 49160 | tf_op jit(solution)/shard_map/ppermute | solution.py:14
  38.2 0.9 %fusion.27 = f32[16,128]{1,0:T(8,128)S(1)} fusion(f32[7,128,128]{2,1,0:T(8,128)S(1)} %copy-done, s32[]{:T(128)S(6)} %select_n.70, f32[3,16,128]{2,1,0:T(8,128)S(1)} %add.88, f32[7,16,128]{2,1,0:T(8,128)} %param.11), kind=kOutput, calls=%fused_computation.33 | convolution fusion | flops 3147776 | bytes 91136 | tf_op jit(solution)/shard_map/jk,nk->nj/dot_general | solution.py:57
  39.6 2.6 %collective-permute-start.9 = (f32[16,128]{1,0:T(8,128)S(1)}, f32[16,128]{1,0:T(8,128)S(1)}, u32[]{:S(2)}, u32[]{:S(2)}) collective-permute-start(f32[16,128]{1,0:T(8,128)S(1)} %slice_bitcast_fusion), channel_id=1, source_target_pairs={{0,192},{2,194},{4,196},{6,198},{8,200},{10,202},{12,204},{14,206}... | collective-permute-start | bytes 24584 | tf_op jit(solution)/shard_map/ppermute | solution.py:14
  42.2 0.9 %fusion.21 = f32[16,128]{1,0:T(8,128)S(1)} fusion(f32[7,128,128]{2,1,0:T(8,128)S(1)} %copy-done, s32[]{:T(128)S(6)} %select_n.72, f32[2,16,128]{2,1,0:T(8,128)S(1)} %slice_add_fusion, f32[16,128]{1,0:T(8,128)S(1)} %fusion.24, f32[16,128]{1,0:T(8,128)S(1)} %collective-permute-done.8, f32[7,16,128]{2,1,0:T(8,128)} %param.11), kind=kOutput, calls=%fused_computation.27 | convolution fusion | flops 3151872 | bytes 107520 | tf_op jit(solution)/shard_map/jk,nk->nj/dot_general | solution.py:57
  43.3 1.8 %collective-permute-start.10 = (f32[16,128]{1,0:T(8,128)S(1)}, f32[16,128]{1,0:T(8,128)S(1)}, u32[]{:S(2)}, u32[]{:S(2)}) collective-permute-start(f32[16,128]{1,0:T(8,128)S(1)} %fusion.17), channel_id=1, source_target_pairs={{0,192},{2,194},{4,196},{6,198},{8,200},{10,202},{12,204},{14,206}... | collective-permute-start | bytes 24584 | tf_op jit(solution)/shard_map/ppermute | solution.py:14
  45.1 1.9 %collective-permute-done.10 = f32[16,128]{1,0:T(8,128)S(1)} collective-permute-done((f32[16,128]{1,0:T(8,128)S(1)}, f32[16,128]{1,0:T(8,128)S(1)}, u32[]{:S(2)}, u32[]{:S(2)}) %collective-permute-start.10) | collective-permute-done | bytes 8224 | tf_op jit(solution)/shard_map/ppermute | solution.py:14
  47.0 0.9 %fusion.14 = f32[16,128]{1,0:T(8,128)S(1)} fusion(f32[7,128,128]{2,1,0:T(8,128)S(1)} %copy-done, s32[]{:T(128)S(6)} %select_n.75, f32[16,128]{1,0:T(8,128)S(1)} %fusion.17, f32[16,128]{1,0:T(8,128)S(1)} %collective-permute-done.10, f32[16,128]{1,0:T(8,128)S(1)} %collective-permute-done.9, f32[7,16,128]{2,1,0:T(8,128)} %param.11, ...), kind=kOutput, calls=%fused_computation.20 | convolution fusion | flops 3153920 | bytes 115712 | tf_op jit(solution)/shard_map/jk,nk->nj/dot_general | solution.py:57
  49.3 3.0 %scatter_fusion = f32[16,1024]{0,1:T(8,128)S(1)} fusion(f32[16,1024]{0,1:T(8,128)S(1)} %fusion.2, s32[384]{0:T(512)S(1)} %fusion.65, f32[384,16]{1,0:T(8,128)S(1)} %copy.16), kind=kCustom, calls=%fused_computation.1 | custom fusion | flops 6144 | bytes 75264 | tf_op jit(solution)/shard_map/scatter-add | solution.py:68
  52.3 6.4 %fusion = f32[16,2048]{1,0:T(8,128)S(1)} fusion(f32[16,1024]{0,1:T(8,128)S(1)} %scatter_fusion, f32[1,1024,2048]{2,1,0:T(8,128)} %param.8), kind=kOutput, calls=%fused_computation.2 | convolution fusion | flops 402653184 | bytes 8585216 | tf_op jit(solution)/shard_map/nr,rc->nc/dot_general | solution.py:69
  58.7 7.9 %collective-permute-start.11 = (f32[16,1024]{1,0:T(8,128)S(1)}, f32[16,1024]{1,0:T(8,128)S(1)}, u32[]{:S(2)}, u32[]{:S(2)}) collective-permute-start(f32[16,1024]{1,0:T(8,128)S(1)} %slice_select_fusion), channel_id=1, source_target_pairs={{0,1},{1,0},{2,3},{3,2},{4,5},{5,4},{6,7},{7,6},{8,9},{9,8},{10,11... | collective-permute-start | bytes 196616 | tf_op jit(solution)/shard_map/ppermute | solution.py:10
  (42 shorter events, 5.8 us)
Async XLA Ops:
  0.6 37.5 %copy-start = (f32[7,128,128]{2,1,0:T(8,128)S(1)}, f32[7,128,128]{2,1,0:T(8,128)}, u32[]{:S(2)}) copy-start(f32[7,128,128]{2,1,0:T(8,128)} %param.12) | copy-start | bytes 1376260
  0.6 15.9 %copy-start.1 = (f32[1,3,128,128]{3,2,1,0:T(8,128)S(1)}, f32[1,3,128,128]{3,2,1,0:T(8,128)}, u32[]{:S(2)}) copy-start(f32[1,3,128,128]{3,2,1,0:T(8,128)} %param.10) | copy-start | bytes 589828
  0.7 38.4 %copy-start.2 = (f32[6,128,128]{2,1,0:T(8,128)S(1)}, f32[6,128,128]{2,1,0:T(8,128)}, u32[]{:S(2)}) copy-start(f32[6,128,128]{2,1,0:T(8,128)} %param.13) | copy-start | bytes 1179652
  0.7 4.7 %collective-permute-start = (f32[16,1024]{1,0:T(8,128)}, f32[16,1024]{1,0:T(8,128)S(1)}, u32[]{:S(2)}, u32[]{:S(2)}) collective-permute-start(f32[16,1024]{1,0:T(8,128)} %bitcast.95), channel_id=1, source_target_pairs={{0,1},{1,0},{2,3},{3,2},{4,5},{5,4},{6,7},{7,6},{8,9},{9,8},{10,11... | collective-permute-start | bytes 196616 | tf_op jit(solution)/shard_map/ppermute | solution.py:10
  16.9 1.3 %collective-permute-start.1 = (f32[3,16,128]{2,1,0:T(8,128)S(1)}, f32[3,16,128]{2,1,0:T(8,128)S(1)}, u32[]{:S(2)}, u32[]{:S(2)}) collective-permute-start(f32[3,16,128]{2,1,0:T(8,128)S(1)} %fusion.7), channel_id=1, source_target_pairs={{0,1},{1,0},{2,3},{3,2},{4,5},{5,4},{6,7},{7,6},{8,9},{9,8},{10,11... | collective-permute-start | bytes 73736 | tf_op jit(solution)/shard_map/ppermute | solution.py:10
  18.2 2.7 %collective-permute-start.2 = (f32[3,16,128]{2,1,0:T(8,128)S(1)}, f32[3,16,128]{2,1,0:T(8,128)S(1)}, u32[]{:S(2)}, u32[]{:S(2)}) collective-permute-start(f32[3,16,128]{2,1,0:T(8,128)S(1)} %add.83), channel_id=1, source_target_pairs={{0,2},{2,0},{4,6},{6,4},{8,10},{10,8},{12,14},{14,12},{16,18},{18,... | collective-permute-start | bytes 73736 | tf_op jit(solution)/shard_map/ppermute | solution.py:14
  20.9 3.6 %collective-permute-start.3 = (f32[3,16,128]{2,1,0:T(8,128)S(1)}, f32[3,16,128]{2,1,0:T(8,128)S(1)}, u32[]{:S(2)}, u32[]{:S(2)}) collective-permute-start(f32[3,16,128]{2,1,0:T(8,128)S(1)} %add.84), channel_id=1, source_target_pairs={{0,4},{2,6},{4,0},{6,2},{8,12},{10,14},{12,8},{14,10},{16,20},{18,... | collective-permute-start | bytes 73736 | tf_op jit(solution)/shard_map/ppermute | solution.py:14
  24.5 5.6 %collective-permute-start.4 = (f32[3,16,128]{2,1,0:T(8,128)S(1)}, f32[3,16,128]{2,1,0:T(8,128)S(1)}, u32[]{:S(2)}, u32[]{:S(2)}) collective-permute-start(f32[3,16,128]{2,1,0:T(8,128)S(1)} %add.85), channel_id=1, source_target_pairs={{0,12},{2,14},{4,8},{6,10},{8,4},{10,6},{12,0},{14,2},{16,28},{18,... | collective-permute-start | bytes 73736 | tf_op jit(solution)/shard_map/ppermute | solution.py:14
  30.1 2.8 %collective-permute-start.5 = (f32[3,16,128]{2,1,0:T(8,128)S(1)}, f32[3,16,128]{2,1,0:T(8,128)S(1)}, u32[]{:S(2)}, u32[]{:S(2)}) collective-permute-start(f32[3,16,128]{2,1,0:T(8,128)S(1)} %add.86), channel_id=1, source_target_pairs={{0,16},{2,18},{4,20},{6,22},{8,24},{10,26},{12,28},{14,30},{16,0},... | collective-permute-start | bytes 73736 | tf_op jit(solution)/shard_map/ppermute | solution.py:14
  32.9 3.9 %collective-permute-start.6 = (f32[3,16,128]{2,1,0:T(8,128)S(1)}, f32[3,16,128]{2,1,0:T(8,128)S(1)}, u32[]{:S(2)}, u32[]{:S(2)}) collective-permute-start(f32[3,16,128]{2,1,0:T(8,128)S(1)} %add.87), channel_id=1, source_target_pairs={{0,48},{2,50},{4,52},{6,54},{8,56},{10,58},{12,60},{14,62},{16,32}... | collective-permute-start | bytes 73736 | tf_op jit(solution)/shard_map/ppermute | solution.py:14
  36.9 2.7 %collective-permute-start.7 = (f32[2,16,128]{2,1,0:T(8,128)S(1)}, f32[2,16,128]{2,1,0:T(8,128)S(1)}, u32[]{:S(2)}, u32[]{:S(2)}) collective-permute-start(f32[2,16,128]{2,1,0:T(8,128)S(1)} %slice.31), channel_id=1, source_target_pairs={{0,64},{2,66},{4,68},{6,70},{8,72},{10,74},{12,76},{14,78},{16,80}... | collective-permute-start | bytes 49160 | tf_op jit(solution)/shard_map/ppermute | solution.py:14
  39.3 2.9 %collective-permute-start.8 = (f32[16,128]{1,0:T(8,128)S(1)}, f32[16,128]{1,0:T(8,128)S(1)}, u32[]{:S(2)}, u32[]{:S(2)}) collective-permute-start(f32[16,128]{1,0:T(8,128)S(1)} %fusion.24), channel_id=1, source_target_pairs={{0,64},{2,66},{4,68},{6,70},{8,72},{10,74},{12,76},{14,78},{16,80}... | collective-permute-start | bytes 24584 | tf_op jit(solution)/shard_map/ppermute | solution.py:14
  39.6 5.5 %collective-permute-start.9 = (f32[16,128]{1,0:T(8,128)S(1)}, f32[16,128]{1,0:T(8,128)S(1)}, u32[]{:S(2)}, u32[]{:S(2)}) collective-permute-start(f32[16,128]{1,0:T(8,128)S(1)} %slice_bitcast_fusion), channel_id=1, source_target_pairs={{0,192},{2,194},{4,196},{6,198},{8,200},{10,202},{12,204},{14,206}... | collective-permute-start | bytes 24584 | tf_op jit(solution)/shard_map/ppermute | solution.py:14
  43.3 3.8 %collective-permute-start.10 = (f32[16,128]{1,0:T(8,128)S(1)}, f32[16,128]{1,0:T(8,128)S(1)}, u32[]{:S(2)}, u32[]{:S(2)}) collective-permute-start(f32[16,128]{1,0:T(8,128)S(1)} %fusion.17), channel_id=1, source_target_pairs={{0,192},{2,194},{4,196},{6,198},{8,200},{10,202},{12,204},{14,206}... | collective-permute-start | bytes 24584 | tf_op jit(solution)/shard_map/ppermute | solution.py:14
  58.7 8.8 %collective-permute-start.11 = (f32[16,1024]{1,0:T(8,128)S(1)}, f32[16,1024]{1,0:T(8,128)S(1)}, u32[]{:S(2)}, u32[]{:S(2)}) collective-permute-start(f32[16,1024]{1,0:T(8,128)S(1)} %slice_select_fusion), channel_id=1, source_target_pairs={{0,1},{1,0},{2,3},{3,2},{4,5},{5,4},{6,7},{7,6},{8,9},{9,8},{10,11... | collective-permute-start | bytes 196616 | tf_op jit(solution)/shard_map/ppermute | solution.py:10

commit v2 on v1

v2 whole, which is shorter than its diff:
```python
import functools

import jax
import jax.numpy as jnp
from jax import lax
from jax.experimental import pallas as pl
from jax.experimental.pallas import tpu as pltpu
from jax.sharding import PartitionSpec as P

F32, BF16 = jnp.float32, jnp.bfloat16
HIGH = lax.Precision.HIGHEST
MIB = 1 << 20
VMEM = pl.BlockSpec(memory_space=pltpu.VMEM)
SMEM = pl.BlockSpec(memory_space=pltpu.SMEM)
HBM = pl.BlockSpec(memory_space=pltpu.HBM)
NN = (((1,), (0,)), ((), ()))
NT = (((1,), (1,)), ((), ()))
TN = (((0,), (0,)), ((), ()))


def shape(*dims, dtype=F32):
    return jax.ShapeDtypeStruct(dims, dtype)


def dot(a, b, dims=NN):
    return lax.dot_general(a, b, dims, preferred_element_type=F32)


def full(a, b, dims=NN):
    return lax.dot_general(a, b, dims, precision=HIGH, preferred_element_type=F32)


def split(x):
    high = x.astype(BF16)
    return high, (x - high.astype(F32)).astype(BF16)


def product(a, split_b, dims=NN):
    ah, al = split(a)
    bh, bl = split_b
    rows = a.shape[0]
    both = dot(jnp.concatenate([ah, al], axis=0), bh, dims)
    return both[:rows] + both[rows:] + dot(ah, bl, dims)


def call(name, body, outs, ins, scratch=(), limit=24):
    return pl.pallas_call(
        body,
        out_shape=outs,
        in_specs=ins,
        out_specs=[VMEM] * len(outs),
        scratch_shapes=list(scratch),
        compiler_params=pltpu.CompilerParams(vmem_limit_bytes=limit * MIB),
        name=name,
    )


def load_columns(inverse_ref, first, steps, chunk, a_ref, sems):
    copies = []
    for s in range(steps):
        start = pl.multiple_of(first + s * chunk, chunk)
        copy = pltpu.make_async_copy(inverse_ref.at[:, pl.ds(start, chunk)], a_ref.at[s], sems.at[s])
        copy.start()
        copies.append(copy)
    return copies


def column_product(copies, chunk, x_ref, a_ref, ah_ref, al_ref):
    n = x_ref.shape[0]
    total = None
    for s, copy in enumerate(copies):
        xh, xl = split(x_ref[:, s * chunk:(s + 1) * chunk])
        x = jnp.concatenate([xh, xl], axis=0)
        copy.wait()
        ah, al = split(a_ref[s])
        ah_ref[s] = ah
        al_ref[s] = al
        part = dot(x, ah, NT) + dot(x, al, NT)
        total = part if total is None else total + part
    return total[:n] + total[n:]


def one_hot(index_ref, level, rows, first):
    row = lax.broadcasted_iota(jnp.int32, (rows, index_ref.shape[1]), 0) + first
    return jnp.where(row == index_ref[level:level + 1, :], 1.0, 0.0).astype(BF16)


def first_kernel(chunk, where_ref, x_ref, inverse_ref, out_ref, ah_ref, al_ref, a_ref, sems):
    half = x_ref.shape[1]
    copies = load_columns(inverse_ref, where_ref[0] * half, half // chunk, chunk, a_ref, sems)
    out_ref[...] = column_product(copies, chunk, x_ref, a_ref, ah_ref, al_ref)


def second_kernel(chunk, where_ref, x_ref, part_ref, index_ref, coupling_ref, inverse_ref, term_ref, u_ref, ah_ref, al_ref, a_ref, sems):
    n, half = x_ref.shape
    levels, k = index_ref.shape
    side = where_ref[0]
    copies = load_columns(inverse_ref, (1 - side) * half, half // chunk, chunk, a_ref, sems)
    hot = [one_hot(index_ref, level, half, side * half) for level in range(levels)]
    u = part_ref[...] + column_product(copies, chunk, x_ref, a_ref, ah_ref, al_ref)
    u_ref[...] = u
    uh, um = split(u)
    ul = (u - uh.astype(F32) - um.astype(F32)).astype(BF16)
    parts = jnp.concatenate([uh, um, ul], axis=0)
    for level in range(levels):
        picked = dot(parts, hot[level])
        picked = picked[:n] + picked[n:2 * n] + picked[2 * n:]
        term_ref[:, level * k:(level + 1) * k] = product(picked, split(coupling_ref[level]), NT)


def spread_kernel(where_ref, index_ref, coupling_ref, high_ref, low_ref):
    levels, k = index_ref.shape
    half = high_ref.shape[1]
    for level in range(levels):
        hot = one_hot(index_ref, level, half, where_ref[0] * half)
        ch, cl = split(coupling_ref[level])
        moved = dot(jnp.concatenate([ch, cl], axis=0), hot, NT).astype(BF16)
        high_ref[level * k:(level + 1) * k, :] = moved[:k]
        low_ref[level * k:(level + 1) * k, :] = moved[k:]


def back_kernel(first, count, u_ref, high_ref, low_ref, ah_ref, al_ref, out_ref):
    n = u_ref.shape[0]
    uh, ul = split(u_ref[...])
    low = low_ref[...]
    left = jnp.concatenate([high_ref[...], uh, ul], axis=0)
    m = low.shape[0]
    ah = jnp.concatenate([ah_ref[first + s] for s in range(count)], axis=1)
    al = jnp.concatenate([al_ref[first + s] for s in range(count)], axis=1)
    one = dot(left, ah)
    three = dot(left[:m + n], al)
    out_ref[:m, :] = one[:m] + dot(low, ah) + three[:m]
    out_ref[m:, :] = one[m:m + n] + one[m + n:] + three[m:]


def tree_kernel(where_ref, inverse_ref, parent_ref, to_root_ref, own_ref, root_ref):
    k = inverse_ref.shape[1]
    near, sibling, middle = where_ref[1], where_ref[2], where_ref[3]
    top = inverse_ref.shape[0] - 1
    inv0, inv1, inv2 = inverse_ref[near], inverse_ref[middle], inverse_ref[top]
    g0 = full(parent_ref[near], inv0)
    gs = full(parent_ref[sibling], inverse_ref[sibling])
    g1 = full(parent_ref[middle], inv1)
    to_root_ref[:, :k] = g1
    to_root_ref[:, k:2 * k] = -full(g1, g0)
    to_root_ref[:, 2 * k:] = -full(g1, gs)
    own_ref[0] = g0
    own_ref[1] = gs
    own_ref[2] = full(inv0, inv0, TN)
    own_ref[3] = full(inv1, inv1, TN)
    h2 = full(inv2, inv2, TN)
    k1 = full(h2, g1)
    root_ref[:, :k] = full(k1, g0)
    root_ref[:, k:2 * k] = -k1
    root_ref[:, 2 * k:] = h2


def join_kernel(mine0_ref, mine1_ref, got0_ref, got1_ref, root_ref, base_ref, low_ref, qh_ref, ql_ref):
    k = root_ref.shape[0]
    root = root_ref[...]
    m = root.shape[1]
    columns = mine0_ref.shape[1]
    for s, (mine, got) in enumerate(((mine0_ref, got0_ref), (mine1_ref, got1_ref))):
        cols = slice(s * columns, (s + 1) * columns)
        b = mine[:m, :] + got[:m, :]
        base_ref[:, cols] = mine[m:, :] + got[m:, :]
        low_ref[:, cols] = b[:2 * k]
        qh, ql = split(product(root, split(b)))
        qh_ref[:, cols] = qh
        ql_ref[:, cols] = ql
    rh, rl = split(root)
    qh_ref[:, 2 * columns:] = rh
    ql_ref[:, 2 * columns:] = rl


def middle_kernel(where_ref, own_ref, other_ref, rhs_ref, to_root_ref, source_ref, up_ref):
    k = to_root_ref.shape[0]
    own = own_ref[...]
    both = own + other_ref[...]
    source = jnp.concatenate(
        [
            rhs_ref[where_ref[3]] - both[:, k:2 * k],
            rhs_ref[where_ref[1]] - own[:, :k],
            rhs_ref[where_ref[2]] - other_ref[:, :k],
        ],
        axis=1,
    )
    source_ref[...] = source
    up_ref[...] = both[:, 2 * k:] + product(source, split(to_root_ref[...]), NT)


def lower_kernel(source_ref, own_ref, base_ref, low_ref, pre_ref, solved_ref):
    k = own_ref.shape[1]
    t1, s0, sb = source_ref[:, :k], source_ref[:, k:2 * k], source_ref[:, 2 * k:]
    c0 = product(s0, split(own_ref[2]))
    s1 = t1 - product(s0, split(own_ref[0]), NT) - product(sb, split(own_ref[1]), NT)
    c1 = product(s1, split(own_ref[3]))
    c0 = c0 - product(c1, split(own_ref[0]))
    solved_ref[0] = c0
    solved_ref[1] = c1
    pre_ref[...] = base_ref[...] - product(jnp.concatenate([c0, c1], axis=1), split(low_ref[...]))


def last_kernel(up_ref, other_ref, rhs_ref, pre_ref, solved_ref, qh_ref, ql_ref, out_ref, sep_ref):
    k = up_ref.shape[1]
    width = pre_ref.shape[1]
    s2 = rhs_ref[rhs_ref.shape[0] - 1] - (up_ref[...] + other_ref[...])
    add = product(s2, (qh_ref[...], ql_ref[...]))
    out_ref[...] = pre_ref[...] - add[:, :width]
    sep_ref[0] = solved_ref[0] + add[:, width:width + k]
    sep_ref[1] = solved_ref[1] + add[:, width + k:width + 2 * k]
    sep_ref[2] = add[:, width + 2 * k:]


def swap_core(x):
    return lax.ppermute(x, "sep", [(0, 1), (1, 0)])


def swap_leaf(x, mask):
    return lax.ppermute(x, "leaf", [(i, i ^ mask) for i in range(lax.axis_size("leaf"))])


def ordered(*arrays):
    return lax.optimization_barrier(arrays)


def local(leaf_rhs, leaf_inverse, skeleton_index, leaf_coupling, sep_rhs, sep_inverse, sep_parent):
    side = lax.axis_index("sep")
    leaf = lax.axis_index("leaf")
    plane = leaf // 32
    where = jnp.stack([side, plane, plane ^ 1, 4 + plane // 2]).astype(jnp.int32)
    mine, index, coupling = leaf_rhs[0], skeleton_index[0], leaf_coupling[0]
    inverse = leaf_inverse[0]
    n, half = mine.shape
    levels, k = index.shape
    m = levels * k
    chunk = 256
    slots = [pltpu.VMEM((half // chunk, half, chunk), F32), pltpu.SemaphoreType.DMA((half // chunk,))]
    steps = half // chunk
    parts = [shape(steps, half, chunk, dtype=BF16)] * 2
    theirs = swap_core(mine)
    part, *home = call("first_half", functools.partial(first_kernel, chunk), [shape(n, half)] + parts,
                       [SMEM, VMEM, HBM], slots, limit=48)(where, mine, inverse)
    term, u, *away = call("second_half", functools.partial(second_kernel, chunk), [shape(n, m), shape(n, half)] + parts,
                          [SMEM, VMEM, VMEM, VMEM, VMEM, HBM], slots, limit=48)(where, theirs, part, index, coupling, inverse)
    term, index, coupling = ordered(term, index, coupling)
    got = swap_core(term)
    high, low = call("spread", spread_kernel, [shape(m, half, dtype=BF16)] * 2, [SMEM, VMEM, VMEM])(where, index, coupling)
    term, high, low, got = ordered(term, high, low, got)
    total = term + got

    def back(first, u, split_inverse):
        out, = call("back", functools.partial(back_kernel, first, steps // 2), [shape(m + n, half // 2)],
                    [VMEM] * 5)(u, high, low, *split_inverse)
        return out

    sent = []
    kept = []
    for mask, first, held in ((1, 0, away), (2, steps // 2, away), (6, 0, home), (8, steps // 2, home)):
        total, u = ordered(total, u)
        got = swap_leaf(total, mask)
        out = back(first, u, held)
        total, out, got = ordered(total, out, got)
        if held is away:
            sent.append(swap_core(out))
        else:
            kept.append(out)
        total = total + got
    total, sep_inverse, sep_parent = ordered(total, sep_inverse, sep_parent)
    got = swap_leaf(total, 24)
    to_root, own, root = call("tree", tree_kernel, [shape(k, m), shape(4, k, k), shape(k, m)],
                              [SMEM, VMEM, VMEM])(where, sep_inverse, sep_parent)
    total, to_root, got = ordered(total, to_root, got)
    total = total + got
    total, root = ordered(total, root)
    got = swap_leaf(total, 32)
    base, lower, qh, ql = call("join", join_kernel,
                               [shape(n, half), shape(2 * k, half)] + [shape(k, half + m, dtype=BF16)] * 2,
                               [VMEM] * 5)(kept[0], kept[1], sent[0], sent[1], root)
    total, got, base = ordered(total, got, base)
    source, up = call("middle", middle_kernel, [shape(n, m), shape(n, k)], [SMEM] + [VMEM] * 4)(
        where, total, got, sep_rhs, to_root)
    other = swap_leaf(up, 96)
    pre, solved = call("lower", lower_kernel, [shape(n, half), shape(2, n, k)], [VMEM] * 4)(source, own, base, lower)
    pre, other = ordered(pre, other)
    out, sep = call("last", last_kernel, [shape(n, half), shape(levels, n, k)], [VMEM] * 7)(
        up, other, sep_rhs, pre, solved, qh, ql)
    return (out[None], sep[None])


def solution(mesh):
    placed = (
        P("leaf", None, "sep"),
        P("leaf", "sep", None),
        P("leaf", None, None),
        P("leaf", None, None, None),
        P(),
        P(),
        P(),
    )
    return jax.shard_map(
        local,
        mesh=mesh,
        in_specs=placed,
        out_specs=(P("leaf", None, "sep"), P("leaf", None, None, None)),
        check_vma=False,
    )
```

time: 68.4 us -> 47.8 us (0.70)
  the two profiles are of different devices: /device:TPU:1 before, /device:TPU:30 now
where the time goes in v2:
time: 47.8 us; the launch traced here: 47.7 us
  Pallas kernels  18.6 us (39%)
  starting transfers between devices  14.8 us (31%)
  waiting for transfers between devices  11.8 us (25%)
  local copies, waits for them, and re-layouts  1.54 us (3%)
  between operations  0.81 us (2%)
    ppermute x7, starting transfers between devices, swap_leaf(): lax.ppermute(x, 'leaf', [(i, i ^ mask) for i in range(lax.axis_size('leaf...  13.8 us
    ppermute x7, waiting for transfers between devices, swap_leaf(): lax.ppermute(x, 'leaf', [(i, i ^ mask) for i in range(lax.axis_size('leaf...  11.8 us
    pallas_call x4, Pallas kernels, back(): call('back', functools.partial(back_kernel, first, steps // 2), [shape(m...  5.77 us
    pallas_call x1, Pallas kernels, local(): call('second_half', functools.partial(second_kernel, chunk), [shape(n, m)...  3.83 us
    pallas_call x1, Pallas kernels, local(): call('first_half', functools.partial(first_kernel, chunk), [shape(n, half...  3.23 us
    pallas_call x1, Pallas kernels, local(): call('tree', tree_kernel, [shape(k, m), shape(4, k, k), shape(k, m)], [SM...  1.72 us
    unnamed x11, local copies, waits for them, and re-layouts  1.54 us
    pallas_call x1, Pallas kernels, local(): call('spread', spread_kernel, [shape(m, half, dtype=BF16)] * 2, [SMEM, VM...  1.12 us
  transfers between devices with their start and end apart: 11, of which 7 were waited for; matrix products, arithmetic and copies ran while one was open for 2% of the time, Pallas kernels for 28%

profile of v2, /device:TPU:30, one launch (start us, length us, event | category | flops | bytes accessed | tf_op | source)
XLA Modules:
  0.0 47.7 jit_solution(11088649447335980817)
XLA Ops:
  0.8 0.7 %copy.11 = s32[1,3,128]{2,1,0:T(4,128)S(1)} copy(s32[1,3,128]{2,0,1:T(1,128)} %param.9) | data formatting | bytes 3072
  1.5 0.8 %copy-done.4 = f32[1,16,1024]{2,1,0:T(8,128)S(1)} copy-done((f32[1,16,1024]{2,1,0:T(8,128)S(1)}, f32[1,16,1024]{2,1,0:T(8,128)}, u32[]{:S(2)}) %copy-start.4) | copy-done | bytes 65560
  2.4 3.2 %first_half.1 = (f32[16,1024]{1,0:T(8,128)S(1)}, bf16[4,1024,256]{2,1,0:T(8,128)(2,1)S(1)}, bf16[4,1024,256]{2,1,0:T(8,128)(2,1)S(1)}) custom-call(s32[4]{0:T(128)S(1)} %pad_add_fusion.where_ref, f32[16,1024]{1,0:T(8,128)S(1)} %bitcast.15, f32[1024,2048]{1,0:T(8,128)} %bitcast.18), custom_call_target="tpu_custom_call" | custom-call | tf_op jit(solution)/shard_map/first_half/pallas_call | solution.py:242
  5.6 3.8 %second_half.1 = (f32[16,384]{1,0:T(8,128)S(1)}, f32[16,1024]{1,0:T(8,128)S(1)}, bf16[4,1024,256]{2,1,0:T(8,128)(2,1)S(1)}, bf16[4,1024,256]{2,1,0:T(8,128)(2,1)S(1)}) custom-call(s32[4]{0:T(128)S(1)} %pad_add_fusion.where_ref, f32[16,1024]{1,0:T(8,128)S(1)} %collective-permute-done.x_ref, f32[16,1024]{1,0:T(8,128)S(1)} %get-tuple-element.64.part_ref, ...), custom_call_target="tpu_custom_call" | custom-call | tf_op jit(solution)/shard_map/second_half/pallas_call | solution.py:244
  10.0 1.1 %spread.1 = (bf16[384,1024]{1,0:T(8,128)(2,1)S(1)}, bf16[384,1024]{1,0:T(8,128)(2,1)S(1)}) custom-call(s32[4]{0:T(128)S(1)} %pad_add_fusion.where_ref, s32[3,128]{1,0:T(4,128)S(1)} %bitcast.17, f32[3,128,128]{2,1,0:T(8,128)S(1)} %bitcast.13), custom_call_target="tpu_custom_call" | custom-call | tf_op jit(solution)/shard_map/spread/pallas_call | solution.py:248
  11.2 2.0 %collective-permute-start.2 = (f32[16,384]{1,0:T(8,128)S(1)}, f32[16,384]{1,0:T(8,128)S(1)}, u32[]{:S(2)}, u32[]{:S(2)}) collective-permute-start(f32[16,384]{1,0:T(8,128)S(1)} %add.20), channel_id=1, source_target_pairs={{0,2},{2,0},{4,6},{6,4},{8,10},{10,8},{12,14},{14,12},{16,18},{18,... | collective-permute-start | bytes 73736 | tf_op jit(solution)/shard_map/ppermute | solution.py:220
  13.2 1.4 %back.4 = f32[400,512]{1,0:T(8,128)S(1)} custom-call(f32[16,1024]{1,0:T(8,128)S(1)} %get-tuple-element.93.u_ref, bf16[384,1024]{1,0:T(8,128)(2,1)S(1)} %get-tuple-element.76.high_ref, bf16[384,1024]{1,0:T(8,128)(2,1)S(1)} %get-tuple-element.77.low_ref, bf16[4,1024,256]{2,1,0:T(8,128)(2,1)S(1)} %get-tuple-element.78.ah_ref, ...), custom_call_target="tpu_custom_call" | custom-call | tf_op jit(solution)/shard_map/back/pallas_call | solution.py:253
  15.1 3.3 %collective-permute-start.3 = (f32[16,384]{1,0:T(8,128)S(1)}, f32[16,384]{1,0:T(8,128)S(1)}, u32[]{:S(2)}, u32[]{:S(2)}) collective-permute-start(f32[16,384]{1,0:T(8,128)S(1)} %add.21), channel_id=1, source_target_pairs={{0,4},{2,6},{4,0},{6,2},{8,12},{10,14},{12,8},{14,10},{16,20},{18,... | collective-permute-start | bytes 73736 | tf_op jit(solution)/shard_map/ppermute | solution.py:220
  18.3 1.4 %back.5 = f32[400,512]{1,0:T(8,128)S(1)} custom-call(f32[16,1024]{1,0:T(8,128)S(1)} %get-tuple-element.93.u_ref, bf16[384,1024]{1,0:T(8,128)(2,1)S(1)} %get-tuple-element.76.high_ref, bf16[384,1024]{1,0:T(8,128)(2,1)S(1)} %get-tuple-element.77.low_ref, bf16[4,1024,256]{2,1,0:T(8,128)(2,1)S(1)} %get-tuple-element.78.ah_ref, ...), custom_call_target="tpu_custom_call" | custom-call | tf_op jit(solution)/shard_map/back/pallas_call | solution.py:253
  20.4 5.8 %collective-permute-start.4 = (f32[16,384]{1,0:T(8,128)S(1)}, f32[16,384]{1,0:T(8,128)S(1)}, u32[]{:S(2)}, u32[]{:S(2)}) collective-permute-start(f32[16,384]{1,0:T(8,128)S(1)} %add.22), channel_id=1, source_target_pairs={{0,12},{2,14},{4,8},{6,10},{8,4},{10,6},{12,0},{14,2},{16,28},{18,... | collective-permute-start | bytes 73736 | tf_op jit(solution)/shard_map/ppermute | solution.py:220
  26.2 1.4 %back.6.mine0_ref = f32[400,512]{1,0:T(8,128)S(1)} custom-call(f32[16,1024]{1,0:T(8,128)S(1)} %get-tuple-element.93.u_ref, bf16[384,1024]{1,0:T(8,128)(2,1)S(1)} %get-tuple-element.76.high_ref, bf16[384,1024]{1,0:T(8,128)(2,1)S(1)} %get-tuple-element.77.low_ref, bf16[4,1024,256]{2,1,0:T(8,128)(2,1)S(1)} %get-tuple-element.88.ah_ref, ...), custom_call_target="tpu_custom_call" | custom-call | tf_op jit(solution)/shard_map/back/pallas_call | solution.py:253
  28.1 0.8 %collective-permute-start.5 = (f32[16,384]{1,0:T(8,128)S(1)}, f32[16,384]{1,0:T(8,128)S(1)}, u32[]{:S(2)}, u32[]{:S(2)}) collective-permute-start(f32[16,384]{1,0:T(8,128)S(1)} %add.23), channel_id=1, source_target_pairs={{0,16},{2,18},{4,20},{6,22},{8,24},{10,26},{12,28},{14,30},{16,0},... | collective-permute-start | bytes 73736 | tf_op jit(solution)/shard_map/ppermute | solution.py:220
  28.9 1.4 %back.7.mine1_ref = f32[400,512]{1,0:T(8,128)S(1)} custom-call(f32[16,1024]{1,0:T(8,128)S(1)} %get-tuple-element.93.u_ref, bf16[384,1024]{1,0:T(8,128)(2,1)S(1)} %get-tuple-element.76.high_ref, bf16[384,1024]{1,0:T(8,128)(2,1)S(1)} %get-tuple-element.77.low_ref, bf16[4,1024,256]{2,1,0:T(8,128)(2,1)S(1)} %get-tuple-element.88.ah_ref, ...), custom_call_target="tpu_custom_call" | custom-call | tf_op jit(solution)/shard_map/back/pallas_call | solution.py:253
  30.4 1.6 %collective-permute-done.5 = f32[16,384]{1,0:T(8,128)S(1)} collective-permute-done((f32[16,384]{1,0:T(8,128)S(1)}, f32[16,384]{1,0:T(8,128)S(1)}, u32[]{:S(2)}, u32[]{:S(2)}) %collective-permute-start.5) | collective-permute-done | bytes 24608 | tf_op jit(solution)/shard_map/ppermute | solution.py:220
  32.5 1.7 %tree.1 = (f32[128,384]{1,0:T(8,128)S(1)}, f32[4,128,128]{2,1,0:T(8,128)S(1)}, f32[128,384]{1,0:T(8,128)S(1)}) custom-call(s32[4]{0:T(128)S(1)} %pad_add_fusion.where_ref, f32[7,128,128]{2,1,0:T(8,128)S(1)} %copy-done.1, f32[6,128,128]{2,1,0:T(8,128)S(1)} %copy-done.2), custom_call_target="tpu_custom_call" | custom-call | tf_op jit(solution)/shard_map/tree/pallas_call | solution.py:271
  34.2 3.1 %collective-permute-done.6 = f32[16,384]{1,0:T(8,128)S(1)} collective-permute-done((f32[16,384]{1,0:T(8,128)S(1)}, f32[16,384]{1,0:T(8,128)S(1)}, u32[]{:S(2)}, u32[]{:S(2)}) %collective-permute-start.6) | collective-permute-done | bytes 24608 | tf_op jit(solution)/shard_map/ppermute | solution.py:220
  37.3 0.8 %collective-permute-start.7 = (f32[16,384]{1,0:T(8,128)S(1)}, f32[16,384]{1,0:T(8,128)S(1)}, u32[]{:S(2)}, u32[]{:S(2)}) collective-permute-start(f32[16,384]{1,0:T(8,128)S(1)} %add.25.own_ref), channel_id=1, source_target_pairs={{0,64},{2,66},{4,68},{6,70},{8,72},{10,74},{12,76},{14,78},{16,80}... | collective-permute-start | bytes 73736 | tf_op jit(solution)/shard_map/ppermute | solution.py:220
  38.2 0.7 %join.1 = (f32[16,1024]{1,0:T(8,128)S(1)}, f32[256,1024]{1,0:T(8,128)S(1)}, bf16[128,1408]{1,0:T(8,128)(2,1)S(1)}, bf16[128,1408]{1,0:T(8,128)(2,1)S(1)}) custom-call(f32[400,512]{1,0:T(8,128)S(1)} %back.6.mine0_ref, f32[400,512]{1,0:T(8,128)S(1)} %back.7.mine1_ref, f32[400,512]{1,0:T(8,128)S(1)} %collective-permute-done.8.got0_ref, ...), custom_call_target="tpu_custom_call" | custom-call | tf_op jit(solution)/shard_map/join/pallas_call | solution.py:277
  38.9 2.3 %collective-permute-done.7.other_ref = f32[16,384]{1,0:T(8,128)S(1)} collective-permute-done((f32[16,384]{1,0:T(8,128)S(1)}, f32[16,384]{1,0:T(8,128)S(1)}, u32[]{:S(2)}, u32[]{:S(2)}) %collective-permute-start.7) | collective-permute-done | bytes 24608 | tf_op jit(solution)/shard_map/ppermute | solution.py:220
  41.2 0.7 %middle.1 = (f32[16,384]{1,0:T(8,128)S(1)}, f32[16,128]{1,0:T(8,128)S(1)}) custom-call(s32[4]{0:T(128)S(1)} %pad_add_fusion.where_ref, f32[16,384]{1,0:T(8,128)S(1)} %add.25.own_ref, f32[16,384]{1,0:T(8,128)S(1)} %collective-permute-done.7.other_ref, f32[7,16,128]{2,1,0:T(8,128)S(1)} %copy-done.3, f32[128,384]{1,0:T(8,128)S(1)} %get-tuple-element.112.to_root_ref), custom_call_target="tpu_custom_call" | custom-call | tf_op jit(solution)/shard_map/middle/pallas_call | solution.py:281
  41.9 0.6 %collective-permute-start.10 = (f32[16,128]{1,0:T(8,128)S(1)}, f32[16,128]{1,0:T(8,128)S(1)}, u32[]{:S(2)}, u32[]{:S(2)}) collective-permute-start(f32[16,128]{1,0:T(8,128)S(1)} %get-tuple-element.113.up_ref), channel_id=1, source_target_pairs={{0,192},{2,194},{4,196},{6,198},{8,200},{10,202},{12,204},{14,206}... | collective-permute-start | bytes 24584 | tf_op jit(solution)/shard_map/ppermute | solution.py:220
  42.4 0.7 %lower.1 = (f32[16,1024]{1,0:T(8,128)S(1)}, f32[2,16,128]{2,1,0:T(8,128)S(1)}) custom-call(f32[16,384]{1,0:T(8,128)S(1)} %get-tuple-element.114.source_ref, f32[4,128,128]{2,1,0:T(8,128)S(1)} %get-tuple-element.115.own_ref, f32[16,1024]{1,0:T(8,128)S(1)} %get-tuple-element.116.base_ref, f32[256,1024]{1,0:T(8,128)S(1)} %get-tuple-element.117.low_ref), custom_call_target="tpu_custom_call" | custom-call | tf_op jit(solution)/shard_map/lower/pallas_call | solution.py:284
  43.1 3.7 %collective-permute-done.10.other_ref = f32[16,128]{1,0:T(8,128)S(1)} collective-permute-done((f32[16,128]{1,0:T(8,128)S(1)}, f32[16,128]{1,0:T(8,128)S(1)}, u32[]{:S(2)}, u32[]{:S(2)}) %collective-permute-start.10) | collective-permute-done | bytes 8224 | tf_op jit(solution)/shard_map/ppermute | solution.py:220
  46.8 0.8 %last.1 = (f32[16,1024]{1,0:T(8,128)}, f32[3,16,128]{2,1,0:T(8,128)}) custom-call(f32[16,128]{1,0:T(8,128)S(1)} %get-tuple-element.113.up_ref, f32[16,128]{1,0:T(8,128)S(1)} %collective-permute-done.10.other_ref, f32[7,16,128]{2,1,0:T(8,128)S(1)} %copy-done.3, f32[16,1024]{1,0:T(8,128)S(1)} %get-tuple-element.120.pre_ref, ...), custom_call_target="tpu_custom_call" | custom-call | tf_op jit(solution)/shard_map/last/pallas_call | solution.py:286
  (28 shorter events, 2.7 us)
Async XLA Ops:
  0.6 5.0 %collective-permute-start = (f32[16,1024]{1,0:T(8,128)}, f32[16,1024]{1,0:T(8,128)S(1)}, u32[]{:S(2)}, u32[]{:S(2)}) collective-permute-start(f32[16,1024]{1,0:T(8,128)} %bitcast.14), channel_id=1, source_target_pairs={{0,1},{1,0},{2,3},{3,2},{4,5},{5,4},{6,7},{7,6},{8,9},{9,8},{10,11... | collective-permute-start | bytes 196616 | tf_op jit(solution)/shard_map/ppermute | solution.py:216
  1.5 0.8 %copy-start.4 = (f32[1,16,1024]{2,1,0:T(8,128)S(1)}, f32[1,16,1024]{2,1,0:T(8,128)}, u32[]{:S(2)}) copy-start(f32[1,16,1024]{2,1,0:T(8,128)} %param.7) | copy-start | bytes 196612
  2.4 3.2 %copy-start = (f32[1,3,128,128]{3,2,1,0:T(8,128)S(1)}, f32[1,3,128,128]{3,2,1,0:T(8,128)}, u32[]{:S(2)}) copy-start(f32[1,3,128,128]{3,2,1,0:T(8,128)} %param.10) | copy-start | bytes 589828
  9.5 1.7 %collective-permute-start.1 = (f32[16,384]{1,0:T(8,128)S(1)}, f32[16,384]{1,0:T(8,128)S(1)}, u32[]{:S(2)}, u32[]{:S(2)}) collective-permute-start(f32[16,384]{1,0:T(8,128)S(1)} %get-tuple-element.71), channel_id=1, source_target_pairs={{0,1},{1,0},{2,3},{3,2},{4,5},{5,4},{6,7},{7,6},{8,9},{9,8},{10,11... | collective-permute-start | bytes 73736 | tf_op jit(solution)/shard_map/ppermute | solution.py:216
  11.2 3.9 %collective-permute-start.2 = (f32[16,384]{1,0:T(8,128)S(1)}, f32[16,384]{1,0:T(8,128)S(1)}, u32[]{:S(2)}, u32[]{:S(2)}) collective-permute-start(f32[16,384]{1,0:T(8,128)S(1)} %add.20), channel_id=1, source_target_pairs={{0,2},{2,0},{4,6},{6,4},{8,10},{10,8},{12,14},{14,12},{16,18},{18,... | collective-permute-start | bytes 73736 | tf_op jit(solution)/shard_map/ppermute | solution.py:220
  15.1 5.1 %collective-permute-start.3 = (f32[16,384]{1,0:T(8,128)S(1)}, f32[16,384]{1,0:T(8,128)S(1)}, u32[]{:S(2)}, u32[]{:S(2)}) collective-permute-start(f32[16,384]{1,0:T(8,128)S(1)} %add.21), channel_id=1, source_target_pairs={{0,4},{2,6},{4,0},{6,2},{8,12},{10,14},{12,8},{14,10},{16,20},{18,... | collective-permute-start | bytes 73736 | tf_op jit(solution)/shard_map/ppermute | solution.py:220
  19.8 18.4 %collective-permute-start.8 = (f32[400,512]{1,0:T(8,128)S(1)}, f32[400,512]{1,0:T(8,128)S(1)}, u32[]{:S(2)}, u32[]{:S(2)}) collective-permute-start(f32[400,512]{1,0:T(8,128)S(1)} %back.4), channel_id=1, source_target_pairs={{0,1},{1,0},{2,3},{3,2},{4,5},{5,4},{6,7},{7,6},{8,9},{9,8},{10,11... | collective-permute-start | bytes 2457608 | tf_op jit(solution)/shard_map/ppermute | solution.py:216
  20.2 18.0 %collective-permute-start.9 = (f32[400,512]{1,0:T(8,128)S(1)}, f32[400,512]{1,0:T(8,128)S(1)}, u32[]{:S(2)}, u32[]{:S(2)}) collective-permute-start(f32[400,512]{1,0:T(8,128)S(1)} %back.5), channel_id=1, source_target_pairs={{0,1},{1,0},{2,3},{3,2},{4,5},{5,4},{6,7},{7,6},{8,9},{9,8},{10,11... | collective-permute-start | bytes 2457608 | tf_op jit(solution)/shard_map/ppermute | solution.py:216
  20.4 7.7 %collective-permute-start.4 = (f32[16,384]{1,0:T(8,128)S(1)}, f32[16,384]{1,0:T(8,128)S(1)}, u32[]{:S(2)}, u32[]{:S(2)}) collective-permute-start(f32[16,384]{1,0:T(8,128)S(1)} %add.22), channel_id=1, source_target_pairs={{0,12},{2,14},{4,8},{6,10},{8,4},{10,6},{12,0},{14,2},{16,28},{18,... | collective-permute-start | bytes 73736 | tf_op jit(solution)/shard_map/ppermute | solution.py:220
  28.1 4.4 %copy-start.1 = (f32[7,128,128]{2,1,0:T(8,128)S(1)}, f32[7,128,128]{2,1,0:T(8,128)}, u32[]{:S(2)}) copy-start(f32[7,128,128]{2,1,0:T(8,128)} %inverse_ref) | copy-start | bytes 1376260
  28.1 4.4 %copy-start.2 = (f32[6,128,128]{2,1,0:T(8,128)S(1)}, f32[6,128,128]{2,1,0:T(8,128)}, u32[]{:S(2)}) copy-start(f32[6,128,128]{2,1,0:T(8,128)} %parent_ref) | copy-start | bytes 1179652
  28.1 3.9 %collective-permute-start.5 = (f32[16,384]{1,0:T(8,128)S(1)}, f32[16,384]{1,0:T(8,128)S(1)}, u32[]{:S(2)}, u32[]{:S(2)}) collective-permute-start(f32[16,384]{1,0:T(8,128)S(1)} %add.23), channel_id=1, source_target_pairs={{0,16},{2,18},{4,20},{6,22},{8,24},{10,26},{12,28},{14,30},{16,0},... | collective-permute-start | bytes 73736 | tf_op jit(solution)/shard_map/ppermute | solution.py:220
  32.0 9.1 %copy-start.3 = (f32[7,16,128]{2,1,0:T(8,128)S(1)}, f32[7,16,128]{2,1,0:T(8,128)}, u32[]{:S(2)}) copy-start(f32[7,16,128]{2,1,0:T(8,128)} %rhs_ref.3) | copy-start | bytes 172036
  32.0 5.3 %collective-permute-start.6 = (f32[16,384]{1,0:T(8,128)S(1)}, f32[16,384]{1,0:T(8,128)S(1)}, u32[]{:S(2)}, u32[]{:S(2)}) collective-permute-start(f32[16,384]{1,0:T(8,128)S(1)} %add.24), channel_id=1, source_target_pairs={{0,48},{2,50},{4,52},{6,54},{8,56},{10,58},{12,60},{14,62},{16,32}... | collective-permute-start | bytes 73736 | tf_op jit(solution)/shard_map/ppermute | solution.py:220
  37.3 3.8 %collective-permute-start.7 = (f32[16,384]{1,0:T(8,128)S(1)}, f32[16,384]{1,0:T(8,128)S(1)}, u32[]{:S(2)}, u32[]{:S(2)}) collective-permute-start(f32[16,384]{1,0:T(8,128)S(1)} %add.25.own_ref), channel_id=1, source_target_pairs={{0,64},{2,66},{4,68},{6,70},{8,72},{10,74},{12,76},{14,78},{16,80}... | collective-permute-start | bytes 73736 | tf_op jit(solution)/shard_map/ppermute | solution.py:220
  41.9 4.9 %collective-permute-start.10 = (f32[16,128]{1,0:T(8,128)S(1)}, f32[16,128]{1,0:T(8,128)S(1)}, u32[]{:S(2)}, u32[]{:S(2)}) collective-permute-start(f32[16,128]{1,0:T(8,128)S(1)} %get-tuple-element.113.up_ref), channel_id=1, source_target_pairs={{0,192},{2,194},{4,196},{6,198},{8,200},{10,202},{12,204},{14,206}... | collective-permute-start | bytes 24584 | tf_op jit(solution)/shard_map/ppermute | solution.py:220

commit v3 on v2

v3 whole, which is shorter than its diff:
```python
import functools

import jax
import jax.numpy as jnp
from jax import lax
from jax.experimental import pallas as pl
from jax.experimental.pallas import tpu as pltpu
from jax.sharding import PartitionSpec as P

F32, BF16 = jnp.float32, jnp.bfloat16
HIGH = lax.Precision.HIGHEST
MIB = 1 << 20
VMEM = pl.BlockSpec(memory_space=pltpu.VMEM)
HBM = pl.BlockSpec(memory_space=pltpu.HBM)
NN = (((1,), (0,)), ((), ()))
NT = (((1,), (1,)), ((), ()))
TN = (((0,), (0,)), ((), ()))


def shape(*dims, dtype=F32):
    return jax.ShapeDtypeStruct(dims, dtype)


def dot(a, b, dims=NN):
    return lax.dot_general(a, b, dims, preferred_element_type=F32)


def full(a, b, dims=NN):
    return lax.dot_general(a, b, dims, precision=HIGH, preferred_element_type=F32)


def split(x):
    high = x.astype(BF16)
    return high, (x - high.astype(F32)).astype(BF16)


def product(a, split_b, dims=NN):
    ah, al = split(a)
    bh, bl = split_b
    rows = a.shape[0]
    both = dot(jnp.concatenate([ah, al], axis=0), bh, dims)
    return both[:rows] + both[rows:] + dot(ah, bl, dims)


def call(name, body, outs, ins, scratch=(), limit=24):
    return pl.pallas_call(
        body,
        out_shape=outs,
        in_specs=ins,
        out_specs=[VMEM] * len(outs),
        scratch_shapes=list(scratch),
        compiler_params=pltpu.CompilerParams(vmem_limit_bytes=limit * MIB),
        name=name,
    )


def load_columns(inverse_ref, first, steps, chunk, a_ref, sems):
    copies = []
    for s in range(steps):
        start = pl.multiple_of(first + s * chunk, chunk)
        copy = pltpu.make_async_copy(inverse_ref.at[:, pl.ds(start, chunk)], a_ref.at[s], sems.at[s])
        copy.start()
        copies.append(copy)
    return copies


def load_kernel(chunk, inverse_ref, ah_ref, al_ref, a_ref, sems):
    steps, half = a_ref.shape[:2]
    copies = load_columns(inverse_ref, lax.axis_index("sep") * half, steps, chunk, a_ref, sems)
    for s, copy in enumerate(copies):
        copy.wait()
        ah_ref[s], al_ref[s] = split(a_ref[s])


def paired(x):
    return jnp.concatenate(split(x), axis=0)


def one_hot(index_ref, level, rows, first):
    row = lax.broadcasted_iota(jnp.int32, (rows, index_ref.shape[1]), 0) + first
    return jnp.where(row == index_ref[level:level + 1, :], 1.0, 0.0).astype(BF16)


def leaf_kernel(chunk, mine_ref, theirs_ref, index_ref, coupling_ref, hh_ref, hl_ref, inverse_ref, term_ref, u_ref, ah_ref, al_ref, a_ref, sems):
    n, half = mine_ref.shape
    levels, k = index_ref.shape
    side = lax.axis_index("sep")
    copies = load_columns(inverse_ref, (1 - side) * half, half // chunk, chunk, a_ref, sems)
    total = jnp.zeros((2 * n, half), F32)
    for s in range(half // chunk):
        x = paired(mine_ref[:, s * chunk:(s + 1) * chunk])
        total = total + (dot(x, hh_ref[s], NT) + dot(x, hl_ref[s], NT))
    hot = [one_hot(index_ref, level, half, side * half) for level in range(levels)]
    for s, copy in enumerate(copies):
        x = paired(theirs_ref[:, s * chunk:(s + 1) * chunk])
        copy.wait()
        ah, al = split(a_ref[s])
        ah_ref[s] = ah
        al_ref[s] = al
        total = total + (dot(x, ah, NT) + dot(x, al, NT))
    u = total[:n] + total[n:]
    u_ref[...] = u
    uh, um = split(u)
    ul = (u - uh.astype(F32) - um.astype(F32)).astype(BF16)
    parts = jnp.concatenate([uh, um, ul], axis=0)
    for level in range(levels):
        picked = dot(parts, hot[level])
        picked = picked[:n] + picked[n:2 * n] + picked[2 * n:]
        term_ref[:, level * k:(level + 1) * k] = product(picked, split(coupling_ref[level]), NT)


def spread_kernel(index_ref, coupling_ref, high_ref, low_ref):
    levels, k = index_ref.shape
    half = high_ref.shape[1]
    for level in range(levels):
        hot = one_hot(index_ref, level, half, lax.axis_index("sep") * half)
        ch, cl = split(coupling_ref[level])
        moved = dot(jnp.concatenate([ch, cl], axis=0), hot, NT).astype(BF16)
        high_ref[level * k:(level + 1) * k, :] = moved[:k]
        low_ref[level * k:(level + 1) * k, :] = moved[k:]


def back_kernel(first, count, u_ref, high_ref, low_ref, ah_ref, al_ref, out_ref):
    n = u_ref.shape[0]
    uh, ul = split(u_ref[...])
    low = low_ref[...]
    left = jnp.concatenate([high_ref[...], uh, ul], axis=0)
    m = low.shape[0]
    ah = jnp.concatenate([ah_ref[first + s] for s in range(count)], axis=1)
    al = jnp.concatenate([al_ref[first + s] for s in range(count)], axis=1)
    one = dot(left, ah)
    three = dot(left[:m + n], al)
    out_ref[:m, :] = one[:m] + dot(low, ah) + three[:m]
    out_ref[m:, :] = one[m:m + n] + one[m + n:] + three[m:]


def pair_matrices(inverse_ref, parent_ref, near, sibling, middle):
    g0 = full(parent_ref[near], inverse_ref[near])
    gs = full(parent_ref[sibling], inverse_ref[sibling])
    g1 = full(parent_ref[middle], inverse_ref[middle])
    return g0, gs, g1, jnp.concatenate([g1, -full(g1, g0), -full(g1, gs)], axis=1)


def tree_kernel(inverse_ref, parent_ref, rhs_ref, wayh_ref, wayl_ref, own_ref, root_ref, chosen_ref):
    k = inverse_ref.shape[1]
    plane = lax.axis_index("leaf") >> 5
    near, sibling, middle = plane, plane ^ 1, 4 + (plane >> 1)
    top = inverse_ref.shape[0] - 1
    inv0, inv1, inv2 = inverse_ref[near], inverse_ref[middle], inverse_ref[top]
    g0, gs, g1, way = pair_matrices(inverse_ref, parent_ref, near, sibling, middle)
    wayh_ref[0], wayl_ref[0] = split(way)
    way = pair_matrices(inverse_ref, parent_ref, 3 - near, (3 - near) ^ 1, 9 - middle)[3]
    wayh_ref[1], wayl_ref[1] = split(way)
    own_ref[0] = g0
    own_ref[1] = gs
    own_ref[2] = full(inv0, inv0, TN)
    own_ref[3] = full(inv1, inv1, TN)
    h2 = full(inv2, inv2, TN)
    k1 = full(h2, g1)
    root_ref[:, :k] = full(k1, g0)
    root_ref[:, k:2 * k] = -k1
    root_ref[:, 2 * k:] = h2
    chosen_ref[:, :k] = rhs_ref[middle]
    chosen_ref[:, k:2 * k] = rhs_ref[near]
    chosen_ref[:, 2 * k:3 * k] = rhs_ref[sibling]
    chosen_ref[:, 3 * k:] = rhs_ref[top]


def join_kernel(mine0_ref, mine1_ref, got0_ref, got1_ref, root_ref, base_ref, low_ref, qh_ref, ql_ref):
    k = root_ref.shape[0]
    root = root_ref[...]
    m = root.shape[1]
    columns = mine0_ref.shape[1]
    for s, (mine, got) in enumerate(((mine0_ref, got0_ref), (mine1_ref, got1_ref))):
        cols = slice(s * columns, (s + 1) * columns)
        b = mine[:m, :] + got[:m, :]
        base_ref[:, cols] = mine[m:, :] + got[m:, :]
        low_ref[:, cols] = b[:2 * k]
        qh, ql = split(product(root, split(b)))
        qh_ref[:, cols] = qh
        ql_ref[:, cols] = ql
    rh, rl = split(root)
    qh_ref[:, 2 * columns:] = rh
    ql_ref[:, 2 * columns:] = rl


def source_kernel(own_ref, other_ref, chosen_ref, out_ref):
    k = own_ref.shape[1] // 3
    out_ref[:, :k] = chosen_ref[:, :k] - own_ref[:, k:2 * k] - other_ref[:, k:2 * k]
    out_ref[:, k:2 * k] = chosen_ref[:, k:2 * k] - own_ref[:, :k]
    out_ref[:, 2 * k:3 * k] = chosen_ref[:, 2 * k:3 * k] - other_ref[:, :k]
    out_ref[:, 3 * k:] = own_ref[:, 2 * k:] + other_ref[:, 2 * k:]


def lower_kernel(source_ref, chosen_ref, wayh_ref, wayl_ref, own_ref, base_ref, low_ref, pre_ref, solved_ref, top_ref):
    k = own_ref.shape[1]
    t1, s0, sb = source_ref[:, :k], source_ref[:, k:2 * k], source_ref[:, 2 * k:3 * k]
    c0 = product(s0, split(own_ref[2]))
    s1 = t1 - product(s0, split(own_ref[0]), NT) - product(sb, split(own_ref[1]), NT)
    c1 = product(s1, split(own_ref[3]))
    c0 = c0 - product(c1, split(own_ref[0]))
    solved_ref[0] = c0
    solved_ref[1] = c1
    pre_ref[...] = base_ref[...] - product(jnp.concatenate([c0, c1], axis=1), split(low_ref[...]))
    up = product(source_ref[:, :3 * k], (wayh_ref[0], wayl_ref[0]), NT)
    top_ref[...] = chosen_ref[:, 3 * k:] - source_ref[:, 3 * k:] - up


def last_kernel(other_ref, wayh_ref, wayl_ref, top_ref, pre_ref, solved_ref, qh_ref, ql_ref, out_ref, sep_ref):
    k = top_ref.shape[1]
    width = pre_ref.shape[1]
    up = product(other_ref[:, :3 * k], (wayh_ref[1], wayl_ref[1]), NT)
    s2 = top_ref[...] - other_ref[:, 3 * k:] - up
    add = product(s2, (qh_ref[...], ql_ref[...]))
    out_ref[...] = pre_ref[...] - add[:, :width]
    sep_ref[0] = solved_ref[0] + add[:, width:width + k]
    sep_ref[1] = solved_ref[1] + add[:, width + k:width + 2 * k]
    sep_ref[2] = add[:, width + 2 * k:]


def swap_core(x):
    return lax.ppermute(x, "sep", [(0, 1), (1, 0)])


def swap_leaf(x, mask):
    return lax.ppermute(x, "leaf", [(i, i ^ mask) for i in range(lax.axis_size("leaf"))])


def ordered(*arrays):
    return lax.optimization_barrier(arrays)


def local(leaf_rhs, leaf_inverse, skeleton_index, leaf_coupling, sep_rhs, sep_inverse, sep_parent):
    mine, index, coupling = leaf_rhs[0], skeleton_index[0], leaf_coupling[0]
    inverse = leaf_inverse[0]
    n, half = mine.shape
    levels, k = index.shape
    m = levels * k
    chunk = 256
    steps = half // chunk
    slots = [pltpu.VMEM((steps, half, chunk), F32), pltpu.SemaphoreType.DMA((steps,))]
    parts = [shape(steps, half, chunk, dtype=BF16)] * 2
    theirs = swap_core(mine)
    home = call("load", functools.partial(load_kernel, chunk), parts, [HBM], slots, limit=48)(inverse)
    term, u, *away = call("leaf", functools.partial(leaf_kernel, chunk), [shape(n, m), shape(n, half)] + parts,
                          [VMEM] * 6 + [HBM], slots, limit=43)(mine, theirs, index, coupling, *home, inverse)
    term, index, coupling = ordered(term, index, coupling)
    got = swap_core(term)
    high, low = call("spread", spread_kernel, [shape(m, half, dtype=BF16)] * 2, [VMEM, VMEM])(index, coupling)
    term, high, low, got = ordered(term, high, low, got)
    total = term + got

    def back(first, u, split_inverse):
        out, = call("back", functools.partial(back_kernel, first, steps // 2), [shape(m + n, half // 2)],
                    [VMEM] * 5)(u, high, low, *split_inverse)
        return out

    sent = []
    kept = []
    for mask, first, held in ((1, 0, away), (3, steps // 2, away), (6, 0, home), (8, steps // 2, home)):
        total, u = ordered(total, u)
        got = swap_leaf(total, mask)
        out = back(first, u, held)
        if held is away:
            sent.append(swap_core(out))
        else:
            kept.append(out)
        total, out, got = ordered(total, out, got)
        total = total + got
    total, sep_inverse, sep_parent = ordered(total, sep_inverse, sep_parent)
    got = swap_leaf(total, 24)
    wayh, wayl, own, root, chosen = call(
        "tree", tree_kernel,
        [shape(2, k, m, dtype=BF16)] * 2 + [shape(4, k, k), shape(k, m), shape(n, m + k)],
        [VMEM] * 3)(sep_inverse, sep_parent, sep_rhs)
    total, root, got = ordered(total, root, got)
    total = total + got
    total, root = ordered(total, root)
    got = swap_leaf(total, 32)
    base, lower, qh, ql = call("join", join_kernel,
                               [shape(n, half), shape(2 * k, half)] + [shape(k, half + m, dtype=BF16)] * 2,
                               [VMEM] * 5)(kept[0], kept[1], sent[0], sent[1], root)
    total, got, base = ordered(total, got, base)
    source, = call("source", source_kernel, [shape(n, m + k)], [VMEM] * 3)(total, got, chosen)
    other = swap_leaf(source, 96)
    pre, solved, top = call("lower", lower_kernel, [shape(n, half), shape(2, n, k), shape(n, k)], [VMEM] * 7)(
        source, chosen, wayh, wayl, own, base, lower)
    pre, other = ordered(pre, other)
    out, sep = call("last", last_kernel, [shape(n, half), shape(levels, n, k)], [VMEM] * 8)(
        other, wayh, wayl, top, pre, solved, qh, ql)
    return (out[None], sep[None])


def solution(mesh):
    placed = (
        P("leaf", None, "sep"),
        P("leaf", "sep", None),
        P("leaf", None, None),
        P("leaf", None, None, None),
        P(),
        P(),
        P(),
    )
    return jax.shard_map(
        local,
        mesh=mesh,
        in_specs=placed,
        out_specs=(P("leaf", None, "sep"), P("leaf", None, None, None)),
        check_vma=False,
    )
```

time: 47.8 us -> 47.3 us (0.990)
  the two profiles are of different devices: /device:TPU:30 before, /device:TPU:32 now
where the time goes in v3:
time: 47.3 us; the launch traced here: 47.2 us
  starting transfers between devices  20 us (42%)
  Pallas kernels  17.3 us (37%)
  waiting for transfers between devices  8.4 us (18%)
  between operations  0.76 us (2%)
  local copies, waits for them, and re-layouts  0.7 us (1%)
    ppermute x7, starting transfers between devices, swap_leaf(): lax.ppermute(x, 'leaf', [(i, i ^ mask) for i in range(lax.axis_size('leaf...  19 us
    ppermute x7, waiting for transfers between devices, swap_leaf(): lax.ppermute(x, 'leaf', [(i, i ^ mask) for i in range(lax.axis_size('leaf...  8.13 us
    pallas_call x4, Pallas kernels, back(): call('back', functools.partial(back_kernel, first, steps // 2), [shape(m...  5.8 us
    pallas_call x1, Pallas kernels, local(): call('leaf', functools.partial(leaf_kernel, chunk), [shape(n, m), shape(n...  4.26 us
    pallas_call x1, Pallas kernels, local(): call('load', functools.partial(load_kernel, chunk), parts, [HBM], slots,...  2.41 us
    pallas_call x1, Pallas kernels, local(): call('tree', tree_kernel, [shape(2, k, m, dtype=BF16)] * 2 + [shape(4, k,...  1.62 us
    pallas_call x1, Pallas kernels, local(): call('last', last_kernel, [shape(n, half), shape(levels, n, k)], [VMEM] * 8)  1.09 us
    ppermute x4, starting transfers between devices, swap_core(): return lax.ppermute(x, 'sep', [(0, 1), (1, 0)])  1 us
  transfers between devices with their start and end apart: 11, of which 8 were waited for; matrix products, arithmetic and copies ran while one was open for 1% of the time, Pallas kernels for 25%

profile of v3, /device:TPU:32, one launch (start us, length us, event | category | flops | bytes accessed | tf_op | source)
XLA Modules:
  0.0 47.2 jit_solution(9278612770801467257)
XLA Ops:
  0.7 0.7 %copy.11 = s32[1,3,128]{2,1,0:T(4,128)S(1)} copy(s32[1,3,128]{2,0,1:T(1,128)} %param.9) | data formatting | bytes 3072
  1.4 2.4 %load.1 = (bf16[4,1024,256]{2,1,0:T(8,128)(2,1)S(1)}, bf16[4,1024,256]{2,1,0:T(8,128)(2,1)S(1)}) custom-call(f32[1024,2048]{1,0:T(8,128)} %bitcast.14), custom_call_target="tpu_custom_call" | custom-call | tf_op jit(solution)/shard_map/load/pallas_call | solution.py:244
  3.9 4.3 %leaf.1 = (f32[16,384]{1,0:T(8,128)S(1)}, f32[16,1024]{1,0:T(8,128)S(1)}, bf16[4,1024,256]{2,1,0:T(8,128)(2,1)S(1)}, bf16[4,1024,256]{2,1,0:T(8,128)(2,1)S(1)}) custom-call(f32[16,1024]{1,0:T(8,128)S(1)} %bitcast.11, f32[16,1024]{1,0:T(8,128)S(1)} %collective-permute-done.theirs_ref, s32[3,128]{1,0:T(4,128)S(1)} %bitcast.12, f32[3,128,128]{2,1,0:T(8,128)S(1)} %bitcast.8, ...), custom_call_target="tpu_custom_call" | custom-call | tf_op jit(solution)/shard_map/leaf/pallas_call | solution.py:245
  9.6 1.8 %collective-permute-start.2 = (f32[16,384]{1,0:T(8,128)S(1)}, f32[16,384]{1,0:T(8,128)S(1)}, u32[]{:S(2)}, u32[]{:S(2)}) collective-permute-start(f32[16,384]{1,0:T(8,128)S(1)} %add.18), channel_id=1, source_target_pairs={{0,2},{2,0},{4,6},{6,4},{8,10},{10,8},{12,14},{14,12},{16,18},{18,... | collective-permute-start | bytes 73736 | tf_op jit(solution)/shard_map/ppermute | solution.py:226
  11.4 1.5 %back.4 = f32[400,512]{1,0:T(8,128)S(1)} custom-call(f32[16,1024]{1,0:T(8,128)S(1)} %get-tuple-element.88.u_ref, bf16[384,1024]{1,0:T(8,128)(2,1)S(1)} %get-tuple-element.73.high_ref, bf16[384,1024]{1,0:T(8,128)(2,1)S(1)} %get-tuple-element.74.low_ref, bf16[4,1024,256]{2,1,0:T(8,128)(2,1)S(1)} %get-tuple-element.75.ah_ref, ...), custom_call_target="tpu_custom_call" | custom-call | tf_op jit(solution)/shard_map/back/pallas_call | solution.py:254
  13.4 1.5 %back.5 = f32[400,512]{1,0:T(8,128)S(1)} custom-call(f32[16,1024]{1,0:T(8,128)S(1)} %get-tuple-element.88.u_ref, bf16[384,1024]{1,0:T(8,128)(2,1)S(1)} %get-tuple-element.73.high_ref, bf16[384,1024]{1,0:T(8,128)(2,1)S(1)} %get-tuple-element.74.low_ref, bf16[4,1024,256]{2,1,0:T(8,128)(2,1)S(1)} %get-tuple-element.75.ah_ref, ...), custom_call_target="tpu_custom_call" | custom-call | tf_op jit(solution)/shard_map/back/pallas_call | solution.py:254
  15.1 2.0 %collective-permute-start.3 = (f32[16,384]{1,0:T(8,128)S(1)}, f32[16,384]{1,0:T(8,128)S(1)}, u32[]{:S(2)}, u32[]{:S(2)}) collective-permute-start(f32[16,384]{1,0:T(8,128)S(1)} %add.19), channel_id=1, source_target_pairs={{0,6},{2,4},{4,2},{6,0},{8,14},{10,12},{12,10},{14,8},{16,22},{18,... | collective-permute-start | bytes 73736 | tf_op jit(solution)/shard_map/ppermute | solution.py:226
  17.0 1.8 %collective-permute-done.3 = f32[16,384]{1,0:T(8,128)S(1)} collective-permute-done((f32[16,384]{1,0:T(8,128)S(1)}, f32[16,384]{1,0:T(8,128)S(1)}, u32[]{:S(2)}, u32[]{:S(2)}) %collective-permute-start.3) | collective-permute-done | bytes 24608 | tf_op jit(solution)/shard_map/ppermute | solution.py:226
  18.9 7.2 %collective-permute-start.4 = (f32[16,384]{1,0:T(8,128)S(1)}, f32[16,384]{1,0:T(8,128)S(1)}, u32[]{:S(2)}, u32[]{:S(2)}) collective-permute-start(f32[16,384]{1,0:T(8,128)S(1)} %add.20), channel_id=1, source_target_pairs={{0,12},{2,14},{4,8},{6,10},{8,4},{10,6},{12,0},{14,2},{16,28},{18,... | collective-permute-start | bytes 73736 | tf_op jit(solution)/shard_map/ppermute | solution.py:226
  26.1 1.4 %back.6.mine0_ref = f32[400,512]{1,0:T(8,128)S(1)} custom-call(f32[16,1024]{1,0:T(8,128)S(1)} %get-tuple-element.88.u_ref, bf16[384,1024]{1,0:T(8,128)(2,1)S(1)} %get-tuple-element.73.high_ref, bf16[384,1024]{1,0:T(8,128)(2,1)S(1)} %get-tuple-element.74.low_ref, bf16[4,1024,256]{2,1,0:T(8,128)(2,1)S(1)} %get-tuple-element.60.hh_ref.ah_ref, ...), custom_call_target="tpu_custom_call" | custom-call | tf_op jit(solution)/shard_map/back/pallas_call | solution.py:254
  27.5 0.6 %collective-permute-done.4 = f32[16,384]{1,0:T(8,128)S(1)} collective-permute-done((f32[16,384]{1,0:T(8,128)S(1)}, f32[16,384]{1,0:T(8,128)S(1)}, u32[]{:S(2)}, u32[]{:S(2)}) %collective-permute-start.4) | collective-permute-done | bytes 24608 | tf_op jit(solution)/shard_map/ppermute | solution.py:226
  28.2 1.4 %collective-permute-start.5 = (f32[16,384]{1,0:T(8,128)S(1)}, f32[16,384]{1,0:T(8,128)S(1)}, u32[]{:S(2)}, u32[]{:S(2)}) collective-permute-start(f32[16,384]{1,0:T(8,128)S(1)} %add.21), channel_id=1, source_target_pairs={{0,16},{2,18},{4,20},{6,22},{8,24},{10,26},{12,28},{14,30},{16,0},... | collective-permute-start | bytes 73736 | tf_op jit(solution)/shard_map/ppermute | solution.py:226
  29.6 1.4 %back.7.mine1_ref = f32[400,512]{1,0:T(8,128)S(1)} custom-call(f32[16,1024]{1,0:T(8,128)S(1)} %get-tuple-element.88.u_ref, bf16[384,1024]{1,0:T(8,128)(2,1)S(1)} %get-tuple-element.73.high_ref, bf16[384,1024]{1,0:T(8,128)(2,1)S(1)} %get-tuple-element.74.low_ref, bf16[4,1024,256]{2,1,0:T(8,128)(2,1)S(1)} %get-tuple-element.60.hh_ref.ah_ref, ...), custom_call_target="tpu_custom_call" | custom-call | tf_op jit(solution)/shard_map/back/pallas_call | solution.py:254
  31.1 1.0 %collective-permute-done.5 = f32[16,384]{1,0:T(8,128)S(1)} collective-permute-done((f32[16,384]{1,0:T(8,128)S(1)}, f32[16,384]{1,0:T(8,128)S(1)}, u32[]{:S(2)}, u32[]{:S(2)}) %collective-permute-start.5) | collective-permute-done | bytes 24608 | tf_op jit(solution)/shard_map/ppermute | solution.py:226
  32.1 2.8 %collective-permute-start.6 = (f32[16,384]{1,0:T(8,128)S(1)}, f32[16,384]{1,0:T(8,128)S(1)}, u32[]{:S(2)}, u32[]{:S(2)}) collective-permute-start(f32[16,384]{1,0:T(8,128)S(1)} %add.22), channel_id=1, source_target_pairs={{0,48},{2,50},{4,52},{6,54},{8,56},{10,58},{12,60},{14,62},{16,32}... | collective-permute-start | bytes 73736 | tf_op jit(solution)/shard_map/ppermute | solution.py:226
  34.9 1.6 %tree.1 = (bf16[2,128,384]{2,1,0:T(8,128)(2,1)S(1)}, bf16[2,128,384]{2,1,0:T(8,128)(2,1)S(1)}, f32[4,128,128]{2,1,0:T(8,128)S(1)}, f32[128,384]{1,0:T(8,128)S(1)}, f32[16,512]{1,0:T(8,128)S(1)}) custom-call(f32[7,128,128]{2,1,0:T(8,128)S(1)} %copy-done.1, f32[6,128,128]{2,1,0:T(8,128)S(1)} %copy-done.2, f32[7,16,128]{2,1,0:T(8,128)S(1)} %copy-done.4), custom_call_target="tpu_custom_call" | custom-call | tf_op jit(solution)/shard_map/tree/pallas_call | solution.py:272
  36.5 0.6 %collective-permute-done.6 = f32[16,384]{1,0:T(8,128)S(1)} collective-permute-done((f32[16,384]{1,0:T(8,128)S(1)}, f32[16,384]{1,0:T(8,128)S(1)}, u32[]{:S(2)}, u32[]{:S(2)}) %collective-permute-start.6) | collective-permute-done | bytes 24608 | tf_op jit(solution)/shard_map/ppermute | solution.py:226
  37.2 1.2 %collective-permute-start.7 = (f32[16,384]{1,0:T(8,128)S(1)}, f32[16,384]{1,0:T(8,128)S(1)}, u32[]{:S(2)}, u32[]{:S(2)}) collective-permute-start(f32[16,384]{1,0:T(8,128)S(1)} %add.23.own_ref), channel_id=1, source_target_pairs={{0,64},{2,66},{4,68},{6,70},{8,72},{10,74},{12,76},{14,78},{16,80}... | collective-permute-start | bytes 73736 | tf_op jit(solution)/shard_map/ppermute | solution.py:226
  38.4 0.7 %join.1 = (f32[16,1024]{1,0:T(8,128)S(1)}, f32[256,1024]{1,0:T(8,128)S(1)}, bf16[128,1408]{1,0:T(8,128)(2,1)S(1)}, bf16[128,1408]{1,0:T(8,128)(2,1)S(1)}) custom-call(f32[400,512]{1,0:T(8,128)S(1)} %back.6.mine0_ref, f32[400,512]{1,0:T(8,128)S(1)} %back.7.mine1_ref, f32[400,512]{1,0:T(8,128)S(1)} %collective-permute-done.8.got0_ref, ...), custom_call_target="tpu_custom_call" | custom-call | tf_op jit(solution)/shard_map/join/pallas_call | solution.py:280
  39.1 1.8 %collective-permute-done.7.other_ref = f32[16,384]{1,0:T(8,128)S(1)} collective-permute-done((f32[16,384]{1,0:T(8,128)S(1)}, f32[16,384]{1,0:T(8,128)S(1)}, u32[]{:S(2)}, u32[]{:S(2)}) %collective-permute-start.7) | collective-permute-done | bytes 24608 | tf_op jit(solution)/shard_map/ppermute | solution.py:226
  41.0 2.5 %collective-permute-start.10 = (f32[16,512]{1,0:T(8,128)S(1)}, f32[16,512]{1,0:T(8,128)S(1)}, u32[]{:S(2)}, u32[]{:S(2)}) collective-permute-start(f32[16,512]{1,0:T(8,128)S(1)} %source.1.source_ref), channel_id=1, source_target_pairs={{0,192},{2,194},{4,196},{6,198},{8,200},{10,202},{12,204},{14,206}... | collective-permute-start | bytes 98312 | tf_op jit(solution)/shard_map/ppermute | solution.py:226
  43.5 0.8 %lower.1 = (f32[16,1024]{1,0:T(8,128)S(1)}, f32[2,16,128]{2,1,0:T(8,128)S(1)}, f32[16,128]{1,0:T(8,128)S(1)}) custom-call(f32[16,512]{1,0:T(8,128)S(1)} %source.1.source_ref, f32[16,512]{1,0:T(8,128)S(1)} %get-tuple-element.103.chosen_ref, bf16[2,128,384]{2,1,0:T(8,128)(2,1)S(1)} %get-tuple-element.104.wayh_ref, ...), custom_call_target="tpu_custom_call" | custom-call | tf_op jit(solution)/shard_map/lower/pallas_call | solution.py:286
  44.3 1.8 %collective-permute-done.10.other_ref = f32[16,512]{1,0:T(8,128)S(1)} collective-permute-done((f32[16,512]{1,0:T(8,128)S(1)}, f32[16,512]{1,0:T(8,128)S(1)}, u32[]{:S(2)}, u32[]{:S(2)}) %collective-permute-start.10) | collective-permute-done | bytes 32800 | tf_op jit(solution)/shard_map/ppermute | solution.py:226
  46.1 1.1 %last.1 = (f32[16,1024]{1,0:T(8,128)}, f32[3,16,128]{2,1,0:T(8,128)}) custom-call(f32[16,512]{1,0:T(8,128)S(1)} %collective-permute-done.10.other_ref, bf16[2,128,384]{2,1,0:T(8,128)(2,1)S(1)} %get-tuple-element.104.wayh_ref, bf16[2,128,384]{2,1,0:T(8,128)(2,1)S(1)} %get-tuple-element.105.wayl_ref, f32[16,128]{1,0:T(8,128)S(1)} %get-tuple-element.111.top_ref, ...), custom_call_target="tpu_custom_call" | custom-call | tf_op jit(solution)/shard_map/last/pallas_call | solution.py:289
  (27 shorter events, 2.3 us)
Async XLA Ops:
  0.6 3.2 %collective-permute-start = (f32[16,1024]{1,0:T(8,128)}, f32[16,1024]{1,0:T(8,128)S(1)}, u32[]{:S(2)}, u32[]{:S(2)}) collective-permute-start(f32[16,1024]{1,0:T(8,128)} %bitcast.10), channel_id=1, source_target_pairs={{0,1},{1,0},{2,3},{3,2},{4,5},{5,4},{6,7},{7,6},{8,9},{9,8},{10,11... | collective-permute-start | bytes 196616 | tf_op jit(solution)/shard_map/ppermute | solution.py:222
  1.4 2.4 %copy-start = (f32[1,3,128,128]{3,2,1,0:T(8,128)S(1)}, f32[1,3,128,128]{3,2,1,0:T(8,128)}, u32[]{:S(2)}) copy-start(f32[1,3,128,128]{3,2,1,0:T(8,128)} %param.10) | copy-start | bytes 589828
  1.4 2.4 %copy-start.3 = (f32[1,16,1024]{2,1,0:T(8,128)S(1)}, f32[1,16,1024]{2,1,0:T(8,128)}, u32[]{:S(2)}) copy-start(f32[1,16,1024]{2,1,0:T(8,128)} %param.7) | copy-start | bytes 196612
  8.1 1.4 %collective-permute-start.1 = (f32[16,384]{1,0:T(8,128)S(1)}, f32[16,384]{1,0:T(8,128)S(1)}, u32[]{:S(2)}, u32[]{:S(2)}) collective-permute-start(f32[16,384]{1,0:T(8,128)S(1)} %get-tuple-element.68), channel_id=1, source_target_pairs={{0,1},{1,0},{2,3},{3,2},{4,5},{5,4},{6,7},{7,6},{8,9},{9,8},{10,11... | collective-permute-start | bytes 73736 | tf_op jit(solution)/shard_map/ppermute | solution.py:222
  9.6 3.8 %collective-permute-start.2 = (f32[16,384]{1,0:T(8,128)S(1)}, f32[16,384]{1,0:T(8,128)S(1)}, u32[]{:S(2)}, u32[]{:S(2)}) collective-permute-start(f32[16,384]{1,0:T(8,128)S(1)} %add.18), channel_id=1, source_target_pairs={{0,2},{2,0},{4,6},{6,4},{8,10},{10,8},{12,14},{14,12},{16,18},{18,... | collective-permute-start | bytes 73736 | tf_op jit(solution)/shard_map/ppermute | solution.py:226
  12.9 25.5 %collective-permute-start.8 = (f32[400,512]{1,0:T(8,128)S(1)}, f32[400,512]{1,0:T(8,128)S(1)}, u32[]{:S(2)}, u32[]{:S(2)}) collective-permute-start(f32[400,512]{1,0:T(8,128)S(1)} %back.4), channel_id=1, source_target_pairs={{0,1},{1,0},{2,3},{3,2},{4,5},{5,4},{6,7},{7,6},{8,9},{9,8},{10,11... | collective-permute-start | bytes 2457608 | tf_op jit(solution)/shard_map/ppermute | solution.py:222
  14.9 23.5 %collective-permute-start.9 = (f32[400,512]{1,0:T(8,128)S(1)}, f32[400,512]{1,0:T(8,128)S(1)}, u32[]{:S(2)}, u32[]{:S(2)}) collective-permute-start(f32[400,512]{1,0:T(8,128)S(1)} %back.5), channel_id=1, source_target_pairs={{0,1},{1,0},{2,3},{3,2},{4,5},{5,4},{6,7},{7,6},{8,9},{9,8},{10,11... | collective-permute-start | bytes 2457608 | tf_op jit(solution)/shard_map/ppermute | solution.py:222
  15.1 3.8 %collective-permute-start.3 = (f32[16,384]{1,0:T(8,128)S(1)}, f32[16,384]{1,0:T(8,128)S(1)}, u32[]{:S(2)}, u32[]{:S(2)}) collective-permute-start(f32[16,384]{1,0:T(8,128)S(1)} %add.19), channel_id=1, source_target_pairs={{0,6},{2,4},{4,2},{6,0},{8,14},{10,12},{12,10},{14,8},{16,22},{18,... | collective-permute-start | bytes 73736 | tf_op jit(solution)/shard_map/ppermute | solution.py:226
  18.9 9.3 %collective-permute-start.4 = (f32[16,384]{1,0:T(8,128)S(1)}, f32[16,384]{1,0:T(8,128)S(1)}, u32[]{:S(2)}, u32[]{:S(2)}) collective-permute-start(f32[16,384]{1,0:T(8,128)S(1)} %add.20), channel_id=1, source_target_pairs={{0,12},{2,14},{4,8},{6,10},{8,4},{10,6},{12,0},{14,2},{16,28},{18,... | collective-permute-start | bytes 73736 | tf_op jit(solution)/shard_map/ppermute | solution.py:226
  28.2 6.7 %copy-start.1 = (f32[7,128,128]{2,1,0:T(8,128)S(1)}, f32[7,128,128]{2,1,0:T(8,128)}, u32[]{:S(2)}) copy-start(f32[7,128,128]{2,1,0:T(8,128)} %inverse_ref) | copy-start | bytes 1376260
  28.2 6.7 %copy-start.2 = (f32[6,128,128]{2,1,0:T(8,128)S(1)}, f32[6,128,128]{2,1,0:T(8,128)}, u32[]{:S(2)}) copy-start(f32[6,128,128]{2,1,0:T(8,128)} %parent_ref) | copy-start | bytes 1179652
  28.2 6.7 %copy-start.4 = (f32[7,16,128]{2,1,0:T(8,128)S(1)}, f32[7,16,128]{2,1,0:T(8,128)}, u32[]{:S(2)}) copy-start(f32[7,16,128]{2,1,0:T(8,128)} %rhs_ref.1) | copy-start | bytes 172036
  28.2 3.9 %collective-permute-start.5 = (f32[16,384]{1,0:T(8,128)S(1)}, f32[16,384]{1,0:T(8,128)S(1)}, u32[]{:S(2)}, u32[]{:S(2)}) collective-permute-start(f32[16,384]{1,0:T(8,128)S(1)} %add.21), channel_id=1, source_target_pairs={{0,16},{2,18},{4,20},{6,22},{8,24},{10,26},{12,28},{14,30},{16,0},... | collective-permute-start | bytes 73736 | tf_op jit(solution)/shard_map/ppermute | solution.py:226
  32.1 5.0 %collective-permute-start.6 = (f32[16,384]{1,0:T(8,128)S(1)}, f32[16,384]{1,0:T(8,128)S(1)}, u32[]{:S(2)}, u32[]{:S(2)}) collective-permute-start(f32[16,384]{1,0:T(8,128)S(1)} %add.22), channel_id=1, source_target_pairs={{0,48},{2,50},{4,52},{6,54},{8,56},{10,58},{12,60},{14,62},{16,32}... | collective-permute-start | bytes 73736 | tf_op jit(solution)/shard_map/ppermute | solution.py:226
  37.2 3.8 %collective-permute-start.7 = (f32[16,384]{1,0:T(8,128)S(1)}, f32[16,384]{1,0:T(8,128)S(1)}, u32[]{:S(2)}, u32[]{:S(2)}) collective-permute-start(f32[16,384]{1,0:T(8,128)S(1)} %add.23.own_ref), channel_id=1, source_target_pairs={{0,64},{2,66},{4,68},{6,70},{8,72},{10,74},{12,76},{14,78},{16,80}... | collective-permute-start | bytes 73736 | tf_op jit(solution)/shard_map/ppermute | solution.py:226
  41.0 5.1 %collective-permute-start.10 = (f32[16,512]{1,0:T(8,128)S(1)}, f32[16,512]{1,0:T(8,128)S(1)}, u32[]{:S(2)}, u32[]{:S(2)}) collective-permute-start(f32[16,512]{1,0:T(8,128)S(1)} %source.1.source_ref), channel_id=1, source_target_pairs={{0,192},{2,194},{4,196},{6,198},{8,200},{10,202},{12,204},{14,206}... | collective-permute-start | bytes 98312 | tf_op jit(solution)/shard_map/ppermute | solution.py:226

commit v4 on v3

--- a/solution.py
+++ b/solution.py
@@ -77,13 +77,13 @@
 
 
 def one_hot(index_ref, level, rows, first):
-    row = lax.broadcasted_iota(jnp.int32, (rows, index_ref.shape[1]), 0) + first
-    return jnp.where(row == index_ref[level:level + 1, :], 1.0, 0.0).astype(BF16)
+    row = lax.broadcasted_iota(jnp.int32, (rows, index_ref.shape[2]), 0) + first
+    return jnp.where(row == index_ref[level], 1.0, 0.0).astype(BF16)
 
 
 def leaf_kernel(chunk, mine_ref, theirs_ref, index_ref, coupling_ref, hh_ref, hl_ref, inverse_ref, term_ref, u_ref, ah_ref, al_ref, a_ref, sems):
     n, half = mine_ref.shape
-    levels, k = index_ref.shape
+    levels, _, k = index_ref.shape
     side = lax.axis_index("sep")
     copies = load_columns(inverse_ref, (1 - side) * half, half // chunk, chunk, a_ref, sems)
     total = jnp.zeros((2 * n, half), F32)
@@ -110,7 +110,7 @@
 
 
 def spread_kernel(index_ref, coupling_ref, high_ref, low_ref):
-    levels, k = index_ref.shape
+    levels, _, k = index_ref.shape
     half = high_ref.shape[1]
     for level in range(levels):
         hot = one_hot(index_ref, level, half, lax.axis_index("sep") * half)
@@ -223,7 +223,12 @@
 
 
 def swap_leaf(x, mask):
-    return lax.ppermute(x, "leaf", [(i, i ^ mask) for i in range(lax.axis_size("leaf"))])
+    count = lax.axis_size("leaf")
+    return lax.ppermute(x, ("leaf", "sep"), [(2 * i + 1, 2 * (i ^ mask) + 1) for i in range(count)])
+
+
+def second_core(x):
+    return jnp.where(lax.axis_index("sep") == 1, x, lax.ppermute(x, "sep", [(1, 0)]))
 
 
 def ordered(*arrays):
@@ -231,10 +236,11 @@
 
 
 def local(leaf_rhs, leaf_inverse, skeleton_index, leaf_coupling, sep_rhs, sep_inverse, sep_parent):
-    mine, index, coupling = leaf_rhs[0], skeleton_index[0], leaf_coupling[0]
+    mine, coupling = leaf_rhs[0], leaf_coupling[0]
+    index = jnp.transpose(skeleton_index, (1, 0, 2))
     inverse = leaf_inverse[0]
     n, half = mine.shape
-    levels, k = index.shape
+    levels, _, k = index.shape
     m = levels * k
     chunk = 256
     steps = half // chunk
@@ -255,17 +261,13 @@
                     [VMEM] * 5)(u, high, low, *split_inverse)
         return out
 
-    sent = []
-    kept = []
+    made = []
     for mask, first, held in ((1, 0, away), (3, steps // 2, away), (6, 0, home), (8, steps // 2, home)):
         total, u = ordered(total, u)
         got = swap_leaf(total, mask)
         out = back(first, u, held)
-        if held is away:
-            sent.append(swap_core(out))
-        else:
-            kept.append(out)
         total, out, got = ordered(total, out, got)
+        made.append(swap_core(out) if held is away else out)
         total = total + got
     total, sep_inverse, sep_parent = ordered(total, sep_inverse, sep_parent)
     got = swap_leaf(total, 24)
@@ -279,13 +281,15 @@
     got = swap_leaf(total, 32)
     base, lower, qh, ql = call("join", join_kernel,
                                [shape(n, half), shape(2 * k, half)] + [shape(k, half + m, dtype=BF16)] * 2,
-                               [VMEM] * 5)(kept[0], kept[1], sent[0], sent[1], root)
+                               [VMEM] * 5)(made[2], made[3], made[0], made[1], root)
     total, got, base = ordered(total, got, base)
     source, = call("source", source_kernel, [shape(n, m + k)], [VMEM] * 3)(total, got, chosen)
     other = swap_leaf(source, 96)
+    source = second_core(source)
     pre, solved, top = call("lower", lower_kernel, [shape(n, half), shape(2, n, k), shape(n, k)], [VMEM] * 7)(
         source, chosen, wayh, wayl, own, base, lower)
     pre, other = ordered(pre, other)
+    other = second_core(other)
     out, sep = call("last", last_kernel, [shape(n, half), shape(levels, n, k)], [VMEM] * 8)(
         other, wayh, wayl, top, pre, solved, qh, ql)
     return (out[None], sep[None])

time: 47.3 us -> 56.2 us (1.19)
  the two profiles are of different devices: /device:TPU:32 before, /device:TPU:1 now
where the time goes in v4:
time: 56.2 us; the launch traced here: 55.9 us
  starting transfers between devices  32.4 us (58%)
  Pallas kernels  17.3 us (31%)
  waiting for transfers between devices  5.15 us (9%)
  between operations  0.93 us (2%)
    ppermute x7, starting transfers between devices, swap_leaf(): lax.ppermute(x, ('leaf', 'sep'), [(2 * i + 1, 2 * (i ^ mask) + 1) for i i...  26.1 us
    pallas_call x4, Pallas kernels, back(): call('back', functools.partial(back_kernel, first, steps // 2), [shape(m...  5.82 us
    pallas_call x1, Pallas kernels, local(): call('leaf', functools.partial(leaf_kernel, chunk), [shape(n, m), shape(n...  4.26 us
    ppermute x4, starting transfers between devices, swap_core(): return lax.ppermute(x, 'sep', [(0, 1), (1, 0)])  3.79 us
    ppermute x7, waiting for transfers between devices, swap_leaf(): lax.ppermute(x, ('leaf', 'sep'), [(2 * i + 1, 2 * (i ^ mask) + 1) for i i...  3.75 us
    ppermute x2, starting transfers between devices, second_core(): lax.ppermute(x, 'sep', [(1, 0)])  2.56 us
    pallas_call x1, Pallas kernels, local(): call('load', functools.partial(load_kernel, chunk), parts, [HBM], slots,...  2.41 us
    pallas_call x1, Pallas kernels, local(): call('tree', tree_kernel, [shape(2, k, m, dtype=BF16)] * 2 + [shape(4, k,...  1.63 us
  transfers between devices with their start and end apart: 13, of which 7 were waited for; matrix products, arithmetic and copies ran while one was open for 0% of the time, Pallas kernels for 21%

profile of v4, /device:TPU:1, one launch (start us, length us, event | category | flops | bytes accessed | tf_op | source)
XLA Modules:
  0.0 55.9 jit_solution(11874135252007213701)
XLA Ops:
  0.6 3.3 %collective-permute-start = (f32[16,1024]{1,0:T(8,128)}, f32[16,1024]{1,0:T(8,128)S(1)}, u32[]{:S(2)}, u32[]{:S(2)}) collective-permute-start(f32[16,1024]{1,0:T(8,128)} %bitcast.8), channel_id=1, source_target_pairs={{0,1},{1,0},{2,3},{3,2},{4,5},{5,4},{6,7},{7,6},{8,9},{9,8},{10,11... | collective-permute-start | bytes 196616 | tf_op jit(solution)/shard_map/ppermute | solution.py:222
  4.0 2.4 %load.1 = (bf16[4,1024,256]{2,1,0:T(8,128)(2,1)S(1)}, bf16[4,1024,256]{2,1,0:T(8,128)(2,1)S(1)}) custom-call(f32[1024,2048]{1,0:T(8,128)} %bitcast.12), custom_call_target="tpu_custom_call" | custom-call | tf_op jit(solution)/shard_map/load/pallas_call | solution.py:250
  6.4 4.3 %leaf.1 = (f32[16,384]{1,0:T(8,128)S(1)}, f32[16,1024]{1,0:T(8,128)S(1)}, bf16[4,1024,256]{2,1,0:T(8,128)(2,1)S(1)}, bf16[4,1024,256]{2,1,0:T(8,128)(2,1)S(1)}) custom-call(f32[16,1024]{1,0:T(8,128)S(1)} %bitcast.9, f32[16,1024]{1,0:T(8,128)S(1)} %collective-permute-done.theirs_ref, s32[3,1,128]{2,1,0:T(1,128)S(1)} %bitcast.10, f32[3,128,128]{2,1,0:T(8,128)S(1)} %bitcast.6, ...), custom_call_target="tpu_custom_call" | custom-call | tf_op jit(solution)/shard_map/leaf/pallas_call | solution.py:251
  12.0 1.9 %collective-permute-start.2 = (f32[16,384]{1,0:T(8,128)S(1)}, f32[16,384]{1,0:T(8,128)S(1)}, u32[]{:S(2)}, u32[]{:S(2)}) collective-permute-start(f32[16,384]{1,0:T(8,128)S(1)} %add.18), channel_id=1, source_target_pairs={{1,3},{3,1},{5,7},{7,5},{9,11},{11,9},{13,15},{15,13},{17,19},{19,... | collective-permute-start | bytes 73736 | tf_op jit(solution)/shard_map/ppermute | solution.py:227
  13.9 1.5 %back.4 = f32[400,512]{1,0:T(8,128)S(1)} custom-call(f32[16,1024]{1,0:T(8,128)S(1)} %get-tuple-element.92.u_ref, bf16[384,1024]{1,0:T(8,128)(2,1)S(1)} %get-tuple-element.77.high_ref, bf16[384,1024]{1,0:T(8,128)(2,1)S(1)} %get-tuple-element.78.low_ref, bf16[4,1024,256]{2,1,0:T(8,128)(2,1)S(1)} %get-tuple-element.79.ah_ref, ...), custom_call_target="tpu_custom_call" | custom-call | tf_op jit(solution)/shard_map/back/pallas_call | solution.py:260
  15.4 1.2 %collective-permute-done.2 = f32[16,384]{1,0:T(8,128)S(1)} collective-permute-done((f32[16,384]{1,0:T(8,128)S(1)}, f32[16,384]{1,0:T(8,128)S(1)}, u32[]{:S(2)}, u32[]{:S(2)}) %collective-permute-start.2) | collective-permute-done | bytes 24608 | tf_op jit(solution)/shard_map/ppermute | solution.py:227
  16.5 4.5 %collective-permute-start.3 = (f32[16,384]{1,0:T(8,128)S(1)}, f32[16,384]{1,0:T(8,128)S(1)}, u32[]{:S(2)}, u32[]{:S(2)}) collective-permute-start(f32[16,384]{1,0:T(8,128)S(1)} %add.19), channel_id=1, source_target_pairs={{1,7},{3,5},{5,3},{7,1},{9,15},{11,13},{13,11},{15,9},{17,23},{19,... | collective-permute-start | bytes 73736 | tf_op jit(solution)/shard_map/ppermute | solution.py:227
  21.1 1.5 %back.5 = f32[400,512]{1,0:T(8,128)S(1)} custom-call(f32[16,1024]{1,0:T(8,128)S(1)} %get-tuple-element.92.u_ref, bf16[384,1024]{1,0:T(8,128)(2,1)S(1)} %get-tuple-element.77.high_ref, bf16[384,1024]{1,0:T(8,128)(2,1)S(1)} %get-tuple-element.78.low_ref, bf16[4,1024,256]{2,1,0:T(8,128)(2,1)S(1)} %get-tuple-element.79.ah_ref, ...), custom_call_target="tpu_custom_call" | custom-call | tf_op jit(solution)/shard_map/back/pallas_call | solution.py:260
  23.1 4.3 %collective-permute-start.4 = (f32[16,384]{1,0:T(8,128)S(1)}, f32[16,384]{1,0:T(8,128)S(1)}, u32[]{:S(2)}, u32[]{:S(2)}) collective-permute-start(f32[16,384]{1,0:T(8,128)S(1)} %add.20), channel_id=1, source_target_pairs={{1,13},{3,15},{5,9},{7,11},{9,5},{11,7},{13,1},{15,3},{17,29},{19,... | collective-permute-start | bytes 73736 | tf_op jit(solution)/shard_map/ppermute | solution.py:227
  27.4 1.4 %back.6.mine0_ref = f32[400,512]{1,0:T(8,128)S(1)} custom-call(f32[16,1024]{1,0:T(8,128)S(1)} %get-tuple-element.92.u_ref, bf16[384,1024]{1,0:T(8,128)(2,1)S(1)} %get-tuple-element.77.high_ref, bf16[384,1024]{1,0:T(8,128)(2,1)S(1)} %get-tuple-element.78.low_ref, bf16[4,1024,256]{2,1,0:T(8,128)(2,1)S(1)} %get-tuple-element.64.hh_ref.ah_ref, ...), custom_call_target="tpu_custom_call" | custom-call | tf_op jit(solution)/shard_map/back/pallas_call | solution.py:260
  28.9 0.9 %collective-permute-done.4 = f32[16,384]{1,0:T(8,128)S(1)} collective-permute-done((f32[16,384]{1,0:T(8,128)S(1)}, f32[16,384]{1,0:T(8,128)S(1)}, u32[]{:S(2)}, u32[]{:S(2)}) %collective-permute-start.4) | collective-permute-done | bytes 24608 | tf_op jit(solution)/shard_map/ppermute | solution.py:227
  29.8 3.3 %collective-permute-start.5 = (f32[16,384]{1,0:T(8,128)S(1)}, f32[16,384]{1,0:T(8,128)S(1)}, u32[]{:S(2)}, u32[]{:S(2)}) collective-permute-start(f32[16,384]{1,0:T(8,128)S(1)} %add.21), channel_id=1, source_target_pairs={{1,17},{3,19},{5,21},{7,23},{9,25},{11,27},{13,29},{15,31},{17,1},... | collective-permute-start | bytes 73736 | tf_op jit(solution)/shard_map/ppermute | solution.py:227
  33.2 1.4 %back.7.mine1_ref = f32[400,512]{1,0:T(8,128)S(1)} custom-call(f32[16,1024]{1,0:T(8,128)S(1)} %get-tuple-element.92.u_ref, bf16[384,1024]{1,0:T(8,128)(2,1)S(1)} %get-tuple-element.77.high_ref, bf16[384,1024]{1,0:T(8,128)(2,1)S(1)} %get-tuple-element.78.low_ref, bf16[4,1024,256]{2,1,0:T(8,128)(2,1)S(1)} %get-tuple-element.64.hh_ref.ah_ref, ...), custom_call_target="tpu_custom_call" | custom-call | tf_op jit(solution)/shard_map/back/pallas_call | solution.py:260
  34.7 4.5 %collective-permute-start.6 = (f32[16,384]{1,0:T(8,128)S(1)}, f32[16,384]{1,0:T(8,128)S(1)}, u32[]{:S(2)}, u32[]{:S(2)}) collective-permute-start(f32[16,384]{1,0:T(8,128)S(1)} %add.22), channel_id=1, source_target_pairs={{1,49},{3,51},{5,53},{7,55},{9,57},{11,59},{13,61},{15,63},{17,33}... | collective-permute-start | bytes 73736 | tf_op jit(solution)/shard_map/ppermute | solution.py:227
  39.2 1.6 %tree.1 = (bf16[2,128,384]{2,1,0:T(8,128)(2,1)S(1)}, bf16[2,128,384]{2,1,0:T(8,128)(2,1)S(1)}, f32[4,128,128]{2,1,0:T(8,128)S(1)}, f32[128,384]{1,0:T(8,128)S(1)}, f32[16,512]{1,0:T(8,128)S(1)}) custom-call(f32[7,128,128]{2,1,0:T(8,128)S(1)} %copy-done.1, f32[6,128,128]{2,1,0:T(8,128)S(1)} %copy-done.2, f32[7,16,128]{2,1,0:T(8,128)S(1)} %copy-done.4), custom_call_target="tpu_custom_call" | custom-call | tf_op jit(solution)/shard_map/tree/pallas_call | solution.py:274
  40.9 3.1 %collective-permute-start.7 = (f32[16,384]{1,0:T(8,128)S(1)}, f32[16,384]{1,0:T(8,128)S(1)}, u32[]{:S(2)}, u32[]{:S(2)}) collective-permute-start(f32[16,384]{1,0:T(8,128)S(1)} %add.23.own_ref), channel_id=1, source_target_pairs={{1,65},{3,67},{5,69},{7,71},{9,73},{11,75},{13,77},{15,79},{17,81}... | collective-permute-start | bytes 73736 | tf_op jit(solution)/shard_map/ppermute | solution.py:227
  44.0 0.7 %join.1 = (f32[16,1024]{1,0:T(8,128)S(1)}, f32[256,1024]{1,0:T(8,128)S(1)}, bf16[128,1408]{1,0:T(8,128)(2,1)S(1)}, bf16[128,1408]{1,0:T(8,128)(2,1)S(1)}) custom-call(f32[400,512]{1,0:T(8,128)S(1)} %back.6.mine0_ref, f32[400,512]{1,0:T(8,128)S(1)} %back.7.mine1_ref, f32[400,512]{1,0:T(8,128)S(1)} %collective-permute-done.8.got0_ref, ...), custom_call_target="tpu_custom_call" | custom-call | tf_op jit(solution)/shard_map/join/pallas_call | solution.py:282
  44.7 0.7 %collective-permute-done.7.other_ref = f32[16,384]{1,0:T(8,128)S(1)} collective-permute-done((f32[16,384]{1,0:T(8,128)S(1)}, f32[16,384]{1,0:T(8,128)S(1)}, u32[]{:S(2)}, u32[]{:S(2)}) %collective-permute-start.7) | collective-permute-done | bytes 24608 | tf_op jit(solution)/shard_map/ppermute | solution.py:227
  45.5 1.3 %collective-permute-start.10 = (f32[16,512]{1,0:T(8,128)S(1)}, f32[16,512]{1,0:T(8,128)S(1)}, u32[]{:S(2)}, u32[]{:S(2)}) collective-permute-start(f32[16,512]{1,0:T(8,128)S(1)} %source.1), channel_id=1, source_target_pairs={{1,0},{3,2},{5,4},{7,6},{9,8},{11,10},{13,12},{15,14},{17,16},{19,... | collective-permute-start | bytes 98312 | tf_op jit(solution)/shard_map/ppermute | solution.py:231
  46.8 4.4 %collective-permute-start.11 = (f32[16,512]{1,0:T(8,128)S(1)}, f32[16,512]{1,0:T(8,128)S(1)}, u32[]{:S(2)}, u32[]{:S(2)}) collective-permute-start(f32[16,512]{1,0:T(8,128)S(1)} %source.1), channel_id=1, source_target_pairs={{1,193},{3,195},{5,197},{7,199},{9,201},{11,203},{13,205},{15,207}... | collective-permute-start | bytes 98312 | tf_op jit(solution)/shard_map/ppermute | solution.py:227
  51.2 0.8 %lower.1 = (f32[16,1024]{1,0:T(8,128)S(1)}, f32[2,16,128]{2,1,0:T(8,128)S(1)}, f32[16,128]{1,0:T(8,128)S(1)}) custom-call(f32[16,512]{1,0:T(8,128)S(1)} %broadcast_select_fusion.1.source_ref, f32[16,512]{1,0:T(8,128)S(1)} %get-tuple-element.111.chosen_ref, bf16[2,128,384]{2,1,0:T(8,128)(2,1)S(1)} %get-tuple-element.112.wayh_ref, ...), custom_call_target="tpu_custom_call" | custom-call | tf_op jit(solution)/shard_map/lower/pallas_call | solution.py:289
  52.6 1.3 %collective-permute-start.12 = (f32[16,512]{1,0:T(8,128)S(1)}, f32[16,512]{1,0:T(8,128)S(1)}, u32[]{:S(2)}, u32[]{:S(2)}) collective-permute-start(f32[16,512]{1,0:T(8,128)S(1)} %collective-permute-done.11), channel_id=1, source_target_pairs={{1,0},{3,2},{5,4},{7,6},{9,8},{11,10},{13,12},{15,14},{17,16},{19,... | collective-permute-start | bytes 98312 | tf_op jit(solution)/shard_map/ppermute | solution.py:231
  53.9 0.8 %collective-permute-done.12 = f32[16,512]{1,0:T(8,128)S(1)} collective-permute-done((f32[16,512]{1,0:T(8,128)S(1)}, f32[16,512]{1,0:T(8,128)S(1)}, u32[]{:S(2)}, u32[]{:S(2)}) %collective-permute-start.12) | collective-permute-done | bytes 32800 | tf_op jit(solution)/shard_map/ppermute | solution.py:231
  54.8 1.1 %last.1 = (f32[16,1024]{1,0:T(8,128)}, f32[3,16,128]{2,1,0:T(8,128)}) custom-call(f32[16,512]{1,0:T(8,128)S(1)} %broadcast_select_fusion.other_ref, bf16[2,128,384]{2,1,0:T(8,128)(2,1)S(1)} %get-tuple-element.112.wayh_ref, bf16[2,128,384]{2,1,0:T(8,128)(2,1)S(1)} %get-tuple-element.113.wayl_ref, f32[16,128]{1,0:T(8,128)S(1)} %get-tuple-element.119.top_ref, ...), custom_call_target="tpu_custom_call" | custom-call | tf_op jit(solution)/shard_map/last/pallas_call | solution.py:293
  (34 shorter events, 2.6 us)
Async XLA Ops:
  0.6 5.8 %collective-permute-start = (f32[16,1024]{1,0:T(8,128)}, f32[16,1024]{1,0:T(8,128)S(1)}, u32[]{:S(2)}, u32[]{:S(2)}) collective-permute-start(f32[16,1024]{1,0:T(8,128)} %bitcast.8), channel_id=1, source_target_pairs={{0,1},{1,0},{2,3},{3,2},{4,5},{5,4},{6,7},{7,6},{8,9},{9,8},{10,11... | collective-permute-start | bytes 196616 | tf_op jit(solution)/shard_map/ppermute | solution.py:222
  4.0 2.4 %copy-start = (f32[1,3,128,128]{3,2,1,0:T(8,128)S(1)}, f32[1,3,128,128]{3,2,1,0:T(8,128)}, u32[]{:S(2)}) copy-start(f32[1,3,128,128]{3,2,1,0:T(8,128)} %param.10) | copy-start | bytes 589828
  4.0 2.4 %copy-start.3 = (f32[1,16,1024]{2,1,0:T(8,128)S(1)}, f32[1,16,1024]{2,1,0:T(8,128)}, u32[]{:S(2)}) copy-start(f32[1,16,1024]{2,1,0:T(8,128)} %param.7) | copy-start | bytes 196612
  4.0 2.5 %copy-start.5 = (s32[1,3,128]{2,0,1:T(1,128)S(1)}, s32[1,3,128]{2,0,1:T(1,128)}, u32[]{:S(2)}) copy-start(s32[1,3,128]{2,0,1:T(1,128)} %param.9) | copy-start | bytes 4612
  10.7 1.3 %collective-permute-start.1 = (f32[16,384]{1,0:T(8,128)S(1)}, f32[16,384]{1,0:T(8,128)S(1)}, u32[]{:S(2)}, u32[]{:S(2)}) collective-permute-start(f32[16,384]{1,0:T(8,128)S(1)} %get-tuple-element.72), channel_id=1, source_target_pairs={{0,1},{1,0},{2,3},{3,2},{4,5},{5,4},{6,7},{7,6},{8,9},{9,8},{10,11... | collective-permute-start | bytes 73736 | tf_op jit(solution)/shard_map/ppermute | solution.py:222
  12.0 4.6 %collective-permute-start.2 = (f32[16,384]{1,0:T(8,128)S(1)}, f32[16,384]{1,0:T(8,128)S(1)}, u32[]{:S(2)}, u32[]{:S(2)}) collective-permute-start(f32[16,384]{1,0:T(8,128)S(1)} %add.18), channel_id=1, source_target_pairs={{1,3},{3,1},{5,7},{7,5},{9,11},{11,9},{13,15},{15,13},{17,19},{19,... | collective-permute-start | bytes 73736 | tf_op jit(solution)/shard_map/ppermute | solution.py:227
  16.5 6.4 %collective-permute-start.3 = (f32[16,384]{1,0:T(8,128)S(1)}, f32[16,384]{1,0:T(8,128)S(1)}, u32[]{:S(2)}, u32[]{:S(2)}) collective-permute-start(f32[16,384]{1,0:T(8,128)S(1)} %add.19), channel_id=1, source_target_pairs={{1,7},{3,5},{5,3},{7,1},{9,15},{11,13},{13,11},{15,9},{17,23},{19,... | collective-permute-start | bytes 73736 | tf_op jit(solution)/shard_map/ppermute | solution.py:227
  22.5 21.5 %collective-permute-start.8 = (f32[400,512]{1,0:T(8,128)S(1)}, f32[400,512]{1,0:T(8,128)S(1)}, u32[]{:S(2)}, u32[]{:S(2)}) collective-permute-start(f32[400,512]{1,0:T(8,128)S(1)} %back.4), channel_id=1, source_target_pairs={{0,1},{1,0},{2,3},{3,2},{4,5},{5,4},{6,7},{7,6},{8,9},{9,8},{10,11... | collective-permute-start | bytes 2457608 | tf_op jit(solution)/shard_map/ppermute | solution.py:222
  22.9 21.1 %collective-permute-start.9 = (f32[400,512]{1,0:T(8,128)S(1)}, f32[400,512]{1,0:T(8,128)S(1)}, u32[]{:S(2)}, u32[]{:S(2)}) collective-permute-start(f32[400,512]{1,0:T(8,128)S(1)} %back.5), channel_id=1, source_target_pairs={{0,1},{1,0},{2,3},{3,2},{4,5},{5,4},{6,7},{7,6},{8,9},{9,8},{10,11... | collective-permute-start | bytes 2457608 | tf_op jit(solution)/shard_map/ppermute | solution.py:222
  23.1 6.7 %collective-permute-start.4 = (f32[16,384]{1,0:T(8,128)S(1)}, f32[16,384]{1,0:T(8,128)S(1)}, u32[]{:S(2)}, u32[]{:S(2)}) collective-permute-start(f32[16,384]{1,0:T(8,128)S(1)} %add.20), channel_id=1, source_target_pairs={{1,13},{3,15},{5,9},{7,11},{9,5},{11,7},{13,1},{15,3},{17,29},{19,... | collective-permute-start | bytes 73736 | tf_op jit(solution)/shard_map/ppermute | solution.py:227
  29.8 9.4 %copy-start.1 = (f32[7,128,128]{2,1,0:T(8,128)S(1)}, f32[7,128,128]{2,1,0:T(8,128)}, u32[]{:S(2)}) copy-start(f32[7,128,128]{2,1,0:T(8,128)} %inverse_ref) | copy-start | bytes 1376260
  29.8 9.4 %copy-start.2 = (f32[6,128,128]{2,1,0:T(8,128)S(1)}, f32[6,128,128]{2,1,0:T(8,128)}, u32[]{:S(2)}) copy-start(f32[6,128,128]{2,1,0:T(8,128)} %parent_ref) | copy-start | bytes 1179652
  29.8 9.4 %copy-start.4 = (f32[7,16,128]{2,1,0:T(8,128)S(1)}, f32[7,16,128]{2,1,0:T(8,128)}, u32[]{:S(2)}) copy-start(f32[7,16,128]{2,1,0:T(8,128)} %rhs_ref.1) | copy-start | bytes 172036
  29.8 4.8 %collective-permute-start.5 = (f32[16,384]{1,0:T(8,128)S(1)}, f32[16,384]{1,0:T(8,128)S(1)}, u32[]{:S(2)}, u32[]{:S(2)}) collective-permute-start(f32[16,384]{1,0:T(8,128)S(1)} %add.21), channel_id=1, source_target_pairs={{1,17},{3,19},{5,21},{7,23},{9,25},{11,27},{13,29},{15,31},{17,1},... | collective-permute-start | bytes 73736 | tf_op jit(solution)/shard_map/ppermute | solution.py:227
  34.7 6.2 %collective-permute-start.6 = (f32[16,384]{1,0:T(8,128)S(1)}, f32[16,384]{1,0:T(8,128)S(1)}, u32[]{:S(2)}, u32[]{:S(2)}) collective-permute-start(f32[16,384]{1,0:T(8,128)S(1)} %add.22), channel_id=1, source_target_pairs={{1,49},{3,51},{5,53},{7,55},{9,57},{11,59},{13,61},{15,63},{17,33}... | collective-permute-start | bytes 73736 | tf_op jit(solution)/shard_map/ppermute | solution.py:227
  40.9 4.6 %collective-permute-start.7 = (f32[16,384]{1,0:T(8,128)S(1)}, f32[16,384]{1,0:T(8,128)S(1)}, u32[]{:S(2)}, u32[]{:S(2)}) collective-permute-start(f32[16,384]{1,0:T(8,128)S(1)} %add.23.own_ref), channel_id=1, source_target_pairs={{1,65},{3,67},{5,69},{7,71},{9,73},{11,75},{13,77},{15,79},{17,81}... | collective-permute-start | bytes 73736 | tf_op jit(solution)/shard_map/ppermute | solution.py:227
  45.5 5.7 %collective-permute-start.10 = (f32[16,512]{1,0:T(8,128)S(1)}, f32[16,512]{1,0:T(8,128)S(1)}, u32[]{:S(2)}, u32[]{:S(2)}) collective-permute-start(f32[16,512]{1,0:T(8,128)S(1)} %source.1), channel_id=1, source_target_pairs={{1,0},{3,2},{5,4},{7,6},{9,8},{11,10},{13,12},{15,14},{17,16},{19,... | collective-permute-start | bytes 98312 | tf_op jit(solution)/shard_map/ppermute | solution.py:231
  46.8 5.9 %collective-permute-start.11 = (f32[16,512]{1,0:T(8,128)S(1)}, f32[16,512]{1,0:T(8,128)S(1)}, u32[]{:S(2)}, u32[]{:S(2)}) collective-permute-start(f32[16,512]{1,0:T(8,128)S(1)} %source.1), channel_id=1, source_target_pairs={{1,193},{3,195},{5,197},{7,199},{9,201},{11,203},{13,205},{15,207}... | collective-permute-start | bytes 98312 | tf_op jit(solution)/shard_map/ppermute | solution.py:227
  52.6 2.1 %collective-permute-start.12 = (f32[16,512]{1,0:T(8,128)S(1)}, f32[16,512]{1,0:T(8,128)S(1)}, u32[]{:S(2)}, u32[]{:S(2)}) collective-permute-start(f32[16,512]{1,0:T(8,128)S(1)} %collective-permute-done.11), channel_id=1, source_target_pairs={{1,0},{3,2},{5,4},{7,6},{9,8},{11,10},{13,12},{15,14},{17,16},{19,... | collective-permute-start | bytes 98312 | tf_op jit(solution)/shard_map/ppermute | solution.py:231

commit v5 on v4

--- a/solution.py
+++ b/solution.py
@@ -184,6 +184,11 @@
     ql_ref[:, 2 * columns:] = rl
 
 
+def mix_kernel(total_ref, one_ref, two_ref, out_ref):
+    first = lax.axis_index("sep") == 0
+    out_ref[...] = one_ref[...] + jnp.where(first, total_ref[...], two_ref[...])
+
+
 def source_kernel(own_ref, other_ref, chosen_ref, out_ref):
     k = own_ref.shape[1] // 3
     out_ref[:, :k] = chosen_ref[:, :k] - own_ref[:, k:2 * k] - other_ref[:, k:2 * k]
@@ -222,13 +227,10 @@
     return lax.ppermute(x, "sep", [(0, 1), (1, 0)])
 
 
-def swap_leaf(x, mask):
-    count = lax.axis_size("leaf")
-    return lax.ppermute(x, ("leaf", "sep"), [(2 * i + 1, 2 * (i ^ mask) + 1) for i in range(count)])
-
-
-def second_core(x):
-    return jnp.where(lax.axis_index("sep") == 1, x, lax.ppermute(x, "sep", [(1, 0)]))
+def swap_leaf(x, mask, first_mask=None):
+    masks = (mask if first_mask is None else first_mask, mask)
+    count = 2 * lax.axis_size("leaf")
+    return lax.ppermute(x, ("leaf", "sep"), [(i, i ^ 2 * masks[i % 2]) for i in range(count)])
 
 
 def ordered(*arrays):
@@ -261,35 +263,49 @@
                     [VMEM] * 5)(u, high, low, *split_inverse)
         return out
 
-    made = []
-    for mask, first, held in ((1, 0, away), (3, steps // 2, away), (6, 0, home), (8, steps // 2, home)):
-        total, u = ordered(total, u)
-        got = swap_leaf(total, mask)
-        out = back(first, u, held)
-        total, out, got = ordered(total, out, got)
-        made.append(swap_core(out) if held is away else out)
-        total = total + got
-    total, sep_inverse, sep_parent = ordered(total, sep_inverse, sep_parent)
-    got = swap_leaf(total, 24)
-    wayh, wayl, own, root, chosen = call(
-        "tree", tree_kernel,
-        [shape(2, k, m, dtype=BF16)] * 2 + [shape(4, k, k), shape(k, m), shape(n, m + k)],
-        [VMEM] * 3)(sep_inverse, sep_parent, sep_rhs)
-    total, root, got = ordered(total, root, got)
+    def quad_sum(total, far, near, last, work):
+        one = swap_leaf(total, far, near)
+        two = swap_leaf(total, last, near)
+        done = work()
+        total, done, one, two = ordered(total, done, one, two)
+        total, = call("mix", mix_kernel, [shape(n, m)], [VMEM] * 3)(total, one, two)
+        return total, done
+
+    total, u = ordered(total, u)
+    got = swap_leaf(total, 1)
+    away0 = back(0, u, away)
+    total, away0, got = ordered(total, away0, got)
     total = total + got
-    total, root = ordered(total, root)
+    got0 = swap_core(away0)
+
+    total, u, sep_inverse, sep_parent = ordered(total, u, sep_inverse, sep_parent)
+    def work():
+        away1 = back(steps // 2, u, away)
+        return (away1,) + tuple(call(
+            "tree", tree_kernel,
+            [shape(2, k, m, dtype=BF16)] * 2 + [shape(4, k, k), shape(k, m), shape(n, m + k)],
+            [VMEM] * 3)(sep_inverse, sep_parent, sep_rhs))
+    total, (away1, wayh, wayl, own, root, chosen) = quad_sum(total, 6, 2, 5, work)
+    total = total + swap_core(total)
+
+    total, u, away1 = ordered(total, u, away1)
+    got1 = swap_core(away1)
+    total, home0 = quad_sum(total, 16, 8, 24, lambda: back(0, u, home))
+    total = total + swap_core(total)
+
+    total, u = ordered(total, u)
     got = swap_leaf(total, 32)
+    home1 = back(steps // 2, u, home)
+    total, home1, got = ordered(total, home1, got)
+    source, = call("source", source_kernel, [shape(n, m + k)], [VMEM] * 3)(total, got, chosen)
+    source, home0, home1, got0, got1, root = ordered(source, home0, home1, got0, got1, root)
+    other = swap_leaf(source, 96)
     base, lower, qh, ql = call("join", join_kernel,
                                [shape(n, half), shape(2 * k, half)] + [shape(k, half + m, dtype=BF16)] * 2,
-                               [VMEM] * 5)(made[2], made[3], made[0], made[1], root)
-    total, got, base = ordered(total, got, base)
-    source, = call("source", source_kernel, [shape(n, m + k)], [VMEM] * 3)(total, got, chosen)
-    other = swap_leaf(source, 96)
-    source = second_core(source)
+                               [VMEM] * 5)(home0, home1, got0, got1, root)
     pre, solved, top = call("lower", lower_kernel, [shape(n, half), shape(2, n, k), shape(n, k)], [VMEM] * 7)(
         source, chosen, wayh, wayl, own, base, lower)
     pre, other = ordered(pre, other)
-    other = second_core(other)
     out, sep = call("last", last_kernel, [shape(n, half), shape(levels, n, k)], [VMEM] * 8)(
         other, wayh, wayl, top, pre, solved, qh, ql)
     return (out[None], sep[None])

time: 56.2 us -> 42.9 us (0.76)
  the two profiles are of different devices: /device:TPU:1 before, /device:TPU:6 now
where the time goes in v5:
time: 42.9 us; the launch traced here: 42.8 us
  Pallas kernels  17.4 us (41%)
  starting transfers between devices  14.1 us (33%)
  waiting for transfers between devices  10.4 us (24%)
  between operations  0.84 us (2%)
    ppermute x7, starting transfers between devices, swap_leaf(): lax.ppermute(x, ('leaf', 'sep'), [(i, i ^ 2 * masks[i % 2]) for i in rang...  8.8 us
    ppermute x7, waiting for transfers between devices, swap_leaf(): lax.ppermute(x, ('leaf', 'sep'), [(i, i ^ 2 * masks[i % 2]) for i in rang...  8.57 us
    pallas_call x4, Pallas kernels, back(): call('back', functools.partial(back_kernel, first, steps // 2), [shape(m...  5.81 us
    ppermute x6, starting transfers between devices, swap_core(): return lax.ppermute(x, 'sep', [(0, 1), (1, 0)])  5.34 us
    pallas_call x1, Pallas kernels, local(): call('leaf', functools.partial(leaf_kernel, chunk), [shape(n, m), shape(n...  4.27 us
    pallas_call x1, Pallas kernels, local(): call('load', functools.partial(load_kernel, chunk), parts, [HBM], slots,...  2.43 us
    ppermute x6, waiting for transfers between devices, swap_core(): return lax.ppermute(x, 'sep', [(0, 1), (1, 0)])  1.87 us
    pallas_call x1, Pallas kernels, work(): call('tree', tree_kernel, [shape(2, k, m, dtype=BF16)] * 2 + [shape(4, k,...  1.62 us
  transfers between devices with their start and end apart: 13, of which 9 were waited for; matrix products, arithmetic and copies ran while one was open for 0% of the time, Pallas kernels for 28%

profile of v5, /device:TPU:6, one launch (start us, length us, event | category | flops | bytes accessed | tf_op | source)
XLA Modules:
  0.0 42.8 jit_solution(2074102666293081954)
XLA Ops:
  0.8 2.4 %load.1 = (bf16[4,1024,256]{2,1,0:T(8,128)(2,1)S(1)}, bf16[4,1024,256]{2,1,0:T(8,128)(2,1)S(1)}) custom-call(f32[1024,2048]{1,0:T(8,128)} %bitcast.12), custom_call_target="tpu_custom_call" | custom-call | tf_op jit(solution)/shard_map/load/pallas_call | solution.py:252
  3.2 4.3 %leaf.1 = (f32[16,384]{1,0:T(8,128)S(1)}, f32[16,1024]{1,0:T(8,128)S(1)}, bf16[4,1024,256]{2,1,0:T(8,128)(2,1)S(1)}, bf16[4,1024,256]{2,1,0:T(8,128)(2,1)S(1)}) custom-call(f32[16,1024]{1,0:T(8,128)S(1)} %bitcast.9, f32[16,1024]{1,0:T(8,128)S(1)} %collective-permute-done.theirs_ref, s32[3,1,128]{2,1,0:T(1,128)S(1)} %bitcast.10, f32[3,128,128]{2,1,0:T(8,128)S(1)} %bitcast.6, ...), custom_call_target="tpu_custom_call" | custom-call | tf_op jit(solution)/shard_map/leaf/pallas_call | solution.py:253
  8.1 0.6 %spread.1 = (bf16[384,1024]{1,0:T(8,128)(2,1)S(1)}, bf16[384,1024]{1,0:T(8,128)(2,1)S(1)}) custom-call(s32[3,1,128]{2,1,0:T(1,128)S(1)} %bitcast.11, f32[3,128,128]{2,1,0:T(8,128)S(1)} %bitcast.7), custom_call_target="tpu_custom_call" | custom-call | tf_op jit(solution)/shard_map/spread/pallas_call | solution.py:257
  8.9 1.9 %collective-permute-start.2 = (f32[16,384]{1,0:T(8,128)S(1)}, f32[16,384]{1,0:T(8,128)S(1)}, u32[]{:S(2)}, u32[]{:S(2)}) collective-permute-start(f32[16,384]{1,0:T(8,128)S(1)} %add.12), channel_id=1, source_target_pairs={{0,2},{1,3},{2,0},{3,1},{4,6},{5,7},{6,4},{7,5},{8,10},{9,11},{10,... | collective-permute-start | bytes 73736 | tf_op jit(solution)/shard_map/ppermute | solution.py:233
  10.8 1.5 %back.4 = f32[400,512]{1,0:T(8,128)S(1)} custom-call(f32[16,1024]{1,0:T(8,128)S(1)} %get-tuple-element.107.u_ref, bf16[384,1024]{1,0:T(8,128)(2,1)S(1)} %get-tuple-element.82.high_ref, bf16[384,1024]{1,0:T(8,128)(2,1)S(1)} %get-tuple-element.83.low_ref, bf16[4,1024,256]{2,1,0:T(8,128)(2,1)S(1)} %get-tuple-element.84.ah_ref, ...), custom_call_target="tpu_custom_call" | custom-call | tf_op jit(solution)/shard_map/back/pallas_call | solution.py:262
  12.8 3.4 %collective-permute-start.4 = (f32[16,384]{1,0:T(8,128)S(1)}, f32[16,384]{1,0:T(8,128)S(1)}, u32[]{:S(2)}, u32[]{:S(2)}) collective-permute-start(f32[16,384]{1,0:T(8,128)S(1)} %add.13.total_ref), channel_id=1, source_target_pairs={{0,4},{1,11},{2,6},{3,9},{4,0},{5,15},{6,2},{7,13},{8,12},{9,3},{1... | collective-permute-start | bytes 73736 | tf_op jit(solution)/shard_map/ppermute | solution.py:233
  16.2 1.5 %back.5 = f32[400,512]{1,0:T(8,128)S(1)} custom-call(f32[16,1024]{1,0:T(8,128)S(1)} %get-tuple-element.107.u_ref, bf16[384,1024]{1,0:T(8,128)(2,1)S(1)} %get-tuple-element.82.high_ref, bf16[384,1024]{1,0:T(8,128)(2,1)S(1)} %get-tuple-element.83.low_ref, bf16[4,1024,256]{2,1,0:T(8,128)(2,1)S(1)} %get-tuple-element.84.ah_ref, ...), custom_call_target="tpu_custom_call" | custom-call | tf_op jit(solution)/shard_map/back/pallas_call | solution.py:262
  17.7 1.6 %tree.1 = (bf16[2,128,384]{2,1,0:T(8,128)(2,1)S(1)}, bf16[2,128,384]{2,1,0:T(8,128)(2,1)S(1)}, f32[4,128,128]{2,1,0:T(8,128)S(1)}, f32[128,384]{1,0:T(8,128)S(1)}, f32[16,512]{1,0:T(8,128)S(1)}) custom-call(f32[7,128,128]{2,1,0:T(8,128)S(1)} %copy-done.1, f32[6,128,128]{2,1,0:T(8,128)S(1)} %copy-done.2, f32[7,16,128]{2,1,0:T(8,128)S(1)} %copy-done.4), custom_call_target="tpu_custom_call" | custom-call | tf_op jit(solution)/shard_map/tree/pallas_call | solution.py:284
  19.4 1.6 %collective-permute-done.3.one_ref = f32[16,384]{1,0:T(8,128)S(1)} collective-permute-done((f32[16,384]{1,0:T(8,128)S(1)}, f32[16,384]{1,0:T(8,128)S(1)}, u32[]{:S(2)}, u32[]{:S(2)}) %collective-permute-start.3) | collective-permute-done | bytes 24608 | tf_op jit(solution)/shard_map/ppermute | solution.py:233
  20.9 2.5 %collective-permute-start.5 = (f32[16,384]{1,0:T(8,128)S(1)}, f32[16,384]{1,0:T(8,128)S(1)}, u32[]{:S(2)}, u32[]{:S(2)}) collective-permute-start(f32[16,384]{1,0:T(8,128)S(1)} %mix.2), channel_id=1, source_target_pairs={{0,1},{1,0},{2,3},{3,2},{4,5},{5,4},{6,7},{7,6},{8,9},{9,8},{10,11... | collective-permute-start | bytes 73736 | tf_op jit(solution)/shard_map/ppermute | solution.py:227
  23.5 0.7 %collective-permute-done.5 = f32[16,384]{1,0:T(8,128)S(1)} collective-permute-done((f32[16,384]{1,0:T(8,128)S(1)}, f32[16,384]{1,0:T(8,128)S(1)}, u32[]{:S(2)}, u32[]{:S(2)}) %collective-permute-start.5) | collective-permute-done | bytes 24608 | tf_op jit(solution)/shard_map/ppermute | solution.py:227
  24.6 1.6 %collective-permute-start.7 = (f32[16,384]{1,0:T(8,128)S(1)}, f32[16,384]{1,0:T(8,128)S(1)}, u32[]{:S(2)}, u32[]{:S(2)}) collective-permute-start(f32[16,384]{1,0:T(8,128)S(1)} %add.14.total_ref), channel_id=1, source_target_pairs={{0,16},{1,49},{2,18},{3,51},{4,20},{5,53},{6,22},{7,55},{8,24},{9,... | collective-permute-start | bytes 73736 | tf_op jit(solution)/shard_map/ppermute | solution.py:233
  26.6 1.4 %back.6.mine0_ref = f32[400,512]{1,0:T(8,128)S(1)} custom-call(f32[16,1024]{1,0:T(8,128)S(1)} %get-tuple-element.107.u_ref, bf16[384,1024]{1,0:T(8,128)(2,1)S(1)} %get-tuple-element.82.high_ref, bf16[384,1024]{1,0:T(8,128)(2,1)S(1)} %get-tuple-element.83.low_ref, bf16[4,1024,256]{2,1,0:T(8,128)(2,1)S(1)} %get-tuple-element.69.hh_ref.ah_ref, ...), custom_call_target="tpu_custom_call" | custom-call | tf_op jit(solution)/shard_map/back/pallas_call | solution.py:262
  28.4 1.6 %collective-permute-done.6.one_ref = f32[16,384]{1,0:T(8,128)S(1)} collective-permute-done((f32[16,384]{1,0:T(8,128)S(1)}, f32[16,384]{1,0:T(8,128)S(1)}, u32[]{:S(2)}, u32[]{:S(2)}) %collective-permute-start.6) | collective-permute-done | bytes 24608 | tf_op jit(solution)/shard_map/ppermute | solution.py:233
  30.0 1.8 %collective-permute-start.8 = (f32[16,384]{1,0:T(8,128)S(1)}, f32[16,384]{1,0:T(8,128)S(1)}, u32[]{:S(2)}, u32[]{:S(2)}) collective-permute-start(f32[16,384]{1,0:T(8,128)S(1)} %mix.3), channel_id=1, source_target_pairs={{0,1},{1,0},{2,3},{3,2},{4,5},{5,4},{6,7},{7,6},{8,9},{9,8},{10,11... | collective-permute-start | bytes 73736 | tf_op jit(solution)/shard_map/ppermute | solution.py:227
  31.8 0.8 %collective-permute-done.8 = f32[16,384]{1,0:T(8,128)S(1)} collective-permute-done((f32[16,384]{1,0:T(8,128)S(1)}, f32[16,384]{1,0:T(8,128)S(1)}, u32[]{:S(2)}, u32[]{:S(2)}) %collective-permute-start.8) | collective-permute-done | bytes 24608 | tf_op jit(solution)/shard_map/ppermute | solution.py:227
  32.7 0.8 %collective-permute-start.9 = (f32[16,384]{1,0:T(8,128)S(1)}, f32[16,384]{1,0:T(8,128)S(1)}, u32[]{:S(2)}, u32[]{:S(2)}) collective-permute-start(f32[16,384]{1,0:T(8,128)S(1)} %add.15.own_ref), channel_id=1, source_target_pairs={{0,64},{1,65},{2,66},{3,67},{4,68},{5,69},{6,70},{7,71},{8,72},{9,... | collective-permute-start | bytes 73736 | tf_op jit(solution)/shard_map/ppermute | solution.py:233
  33.5 1.4 %back.7.mine1_ref = f32[400,512]{1,0:T(8,128)S(1)} custom-call(f32[16,1024]{1,0:T(8,128)S(1)} %get-tuple-element.107.u_ref, bf16[384,1024]{1,0:T(8,128)(2,1)S(1)} %get-tuple-element.82.high_ref, bf16[384,1024]{1,0:T(8,128)(2,1)S(1)} %get-tuple-element.83.low_ref, bf16[4,1024,256]{2,1,0:T(8,128)(2,1)S(1)} %get-tuple-element.69.hh_ref.ah_ref, ...), custom_call_target="tpu_custom_call" | custom-call | tf_op jit(solution)/shard_map/back/pallas_call | solution.py:262
  34.9 1.5 %collective-permute-done.9.other_ref = f32[16,384]{1,0:T(8,128)S(1)} collective-permute-done((f32[16,384]{1,0:T(8,128)S(1)}, f32[16,384]{1,0:T(8,128)S(1)}, u32[]{:S(2)}, u32[]{:S(2)}) %collective-permute-start.9) | collective-permute-done | bytes 24608 | tf_op jit(solution)/shard_map/ppermute | solution.py:233
  36.5 0.6 %collective-permute-start.12 = (f32[16,512]{1,0:T(8,128)S(1)}, f32[16,512]{1,0:T(8,128)S(1)}, u32[]{:S(2)}, u32[]{:S(2)}) collective-permute-start(f32[16,512]{1,0:T(8,128)S(1)} %source.1.source_ref), channel_id=1, source_target_pairs={{0,192},{1,193},{2,194},{3,195},{4,196},{5,197},{6,198},{7,199},{8... | collective-permute-start | bytes 98312 | tf_op jit(solution)/shard_map/ppermute | solution.py:233
  37.1 0.7 %join.1 = (f32[16,1024]{1,0:T(8,128)S(1)}, f32[256,1024]{1,0:T(8,128)S(1)}, bf16[128,1408]{1,0:T(8,128)(2,1)S(1)}, bf16[128,1408]{1,0:T(8,128)(2,1)S(1)}) custom-call(f32[400,512]{1,0:T(8,128)S(1)} %back.6.mine0_ref, f32[400,512]{1,0:T(8,128)S(1)} %back.7.mine1_ref, f32[400,512]{1,0:T(8,128)S(1)} %collective-permute-done.10.got0_ref, ...), custom_call_target="tpu_custom_call" | custom-call | tf_op jit(solution)/shard_map/join/pallas_call | solution.py:303
  37.8 0.8 %lower.1 = (f32[16,1024]{1,0:T(8,128)S(1)}, f32[2,16,128]{2,1,0:T(8,128)S(1)}, f32[16,128]{1,0:T(8,128)S(1)}) custom-call(f32[16,512]{1,0:T(8,128)S(1)} %source.1.source_ref, f32[16,512]{1,0:T(8,128)S(1)} %get-tuple-element.110.chosen_ref, bf16[2,128,384]{2,1,0:T(8,128)(2,1)S(1)} %get-tuple-element.117.wayh_ref, ...), custom_call_target="tpu_custom_call" | custom-call | tf_op jit(solution)/shard_map/lower/pallas_call | solution.py:306
  38.6 3.1 %collective-permute-done.12.other_ref = f32[16,512]{1,0:T(8,128)S(1)} collective-permute-done((f32[16,512]{1,0:T(8,128)S(1)}, f32[16,512]{1,0:T(8,128)S(1)}, u32[]{:S(2)}, u32[]{:S(2)}) %collective-permute-start.12) | collective-permute-done | bytes 32800 | tf_op jit(solution)/shard_map/ppermute | solution.py:233
  41.7 1.1 %last.1 = (f32[16,1024]{1,0:T(8,128)}, f32[3,16,128]{2,1,0:T(8,128)}) custom-call(f32[16,512]{1,0:T(8,128)S(1)} %collective-permute-done.12.other_ref, bf16[2,128,384]{2,1,0:T(8,128)(2,1)S(1)} %get-tuple-element.117.wayh_ref, bf16[2,128,384]{2,1,0:T(8,128)(2,1)S(1)} %get-tuple-element.118.wayl_ref, f32[16,128]{1,0:T(8,128)S(1)} %get-tuple-element.129.top_ref, ...), custom_call_target="tpu_custom_call" | custom-call | tf_op jit(solution)/shard_map/last/pallas_call | solution.py:309
  (32 shorter events, 2.8 us)
Async XLA Ops:
  0.6 2.6 %collective-permute-start = (f32[16,1024]{1,0:T(8,128)}, f32[16,1024]{1,0:T(8,128)S(1)}, u32[]{:S(2)}, u32[]{:S(2)}) collective-permute-start(f32[16,1024]{1,0:T(8,128)} %bitcast.8), channel_id=1, source_target_pairs={{0,1},{1,0},{2,3},{3,2},{4,5},{5,4},{6,7},{7,6},{8,9},{9,8},{10,11... | collective-permute-start | bytes 196616 | tf_op jit(solution)/shard_map/ppermute | solution.py:227
  0.7 2.5 %copy-start = (f32[1,3,128,128]{3,2,1,0:T(8,128)S(1)}, f32[1,3,128,128]{3,2,1,0:T(8,128)}, u32[]{:S(2)}) copy-start(f32[1,3,128,128]{3,2,1,0:T(8,128)} %param.10) | copy-start | bytes 589828
  0.7 2.5 %copy-start.3 = (f32[1,16,1024]{2,1,0:T(8,128)S(1)}, f32[1,16,1024]{2,1,0:T(8,128)}, u32[]{:S(2)}) copy-start(f32[1,16,1024]{2,1,0:T(8,128)} %param.7) | copy-start | bytes 196612
  0.7 2.5 %copy-start.5 = (s32[1,3,128]{2,0,1:T(1,128)S(1)}, s32[1,3,128]{2,0,1:T(1,128)}, u32[]{:S(2)}) copy-start(s32[1,3,128]{2,0,1:T(1,128)} %param.9) | copy-start | bytes 4612
  7.5 1.4 %collective-permute-start.1 = (f32[16,384]{1,0:T(8,128)S(1)}, f32[16,384]{1,0:T(8,128)S(1)}, u32[]{:S(2)}, u32[]{:S(2)}) collective-permute-start(f32[16,384]{1,0:T(8,128)S(1)} %get-tuple-element.77), channel_id=1, source_target_pairs={{0,1},{1,0},{2,3},{3,2},{4,5},{5,4},{6,7},{7,6},{8,9},{9,8},{10,11... | collective-permute-start | bytes 73736 | tf_op jit(solution)/shard_map/ppermute | solution.py:227
  8.9 3.8 %collective-permute-start.2 = (f32[16,384]{1,0:T(8,128)S(1)}, f32[16,384]{1,0:T(8,128)S(1)}, u32[]{:S(2)}, u32[]{:S(2)}) collective-permute-start(f32[16,384]{1,0:T(8,128)S(1)} %add.12), channel_id=1, source_target_pairs={{0,2},{1,3},{2,0},{3,1},{4,6},{5,7},{6,4},{7,5},{8,10},{9,11},{10,... | collective-permute-start | bytes 73736 | tf_op jit(solution)/shard_map/ppermute | solution.py:233
  12.7 4.9 %copy-start.1 = (f32[7,128,128]{2,1,0:T(8,128)S(1)}, f32[7,128,128]{2,1,0:T(8,128)}, u32[]{:S(2)}) copy-start(f32[7,128,128]{2,1,0:T(8,128)} %inverse_ref) | copy-start | bytes 1376260
  12.7 5.0 %copy-start.2 = (f32[6,128,128]{2,1,0:T(8,128)S(1)}, f32[6,128,128]{2,1,0:T(8,128)}, u32[]{:S(2)}) copy-start(f32[6,128,128]{2,1,0:T(8,128)} %parent_ref) | copy-start | bytes 1179652
  12.7 5.0 %copy-start.4 = (f32[7,16,128]{2,1,0:T(8,128)S(1)}, f32[7,16,128]{2,1,0:T(8,128)}, u32[]{:S(2)}) copy-start(f32[7,16,128]{2,1,0:T(8,128)} %rhs_ref.1) | copy-start | bytes 172036
  12.8 6.6 %collective-permute-start.4 = (f32[16,384]{1,0:T(8,128)S(1)}, f32[16,384]{1,0:T(8,128)S(1)}, u32[]{:S(2)}, u32[]{:S(2)}) collective-permute-start(f32[16,384]{1,0:T(8,128)S(1)} %add.13.total_ref), channel_id=1, source_target_pairs={{0,4},{1,11},{2,6},{3,9},{4,0},{5,15},{6,2},{7,13},{8,12},{9,3},{1... | collective-permute-start | bytes 73736 | tf_op jit(solution)/shard_map/ppermute | solution.py:233
  16.1 4.8 %collective-permute-start.3 = (f32[16,384]{1,0:T(8,128)S(1)}, f32[16,384]{1,0:T(8,128)S(1)}, u32[]{:S(2)}, u32[]{:S(2)}) collective-permute-start(f32[16,384]{1,0:T(8,128)S(1)} %add.13.total_ref), channel_id=1, source_target_pairs={{0,4},{1,13},{2,6},{3,15},{4,0},{5,9},{6,2},{7,11},{8,12},{9,5},{1... | collective-permute-start | bytes 73736 | tf_op jit(solution)/shard_map/ppermute | solution.py:233
  20.9 3.3 %collective-permute-start.5 = (f32[16,384]{1,0:T(8,128)S(1)}, f32[16,384]{1,0:T(8,128)S(1)}, u32[]{:S(2)}, u32[]{:S(2)}) collective-permute-start(f32[16,384]{1,0:T(8,128)S(1)} %mix.2), channel_id=1, source_target_pairs={{0,1},{1,0},{2,3},{3,2},{4,5},{5,4},{6,7},{7,6},{8,9},{9,8},{10,11... | collective-permute-start | bytes 73736 | tf_op jit(solution)/shard_map/ppermute | solution.py:227
  23.4 13.1 %collective-permute-start.10 = (f32[400,512]{1,0:T(8,128)S(1)}, f32[400,512]{1,0:T(8,128)S(1)}, u32[]{:S(2)}, u32[]{:S(2)}) collective-permute-start(f32[400,512]{1,0:T(8,128)S(1)} %back.4), channel_id=1, source_target_pairs={{0,1},{1,0},{2,3},{3,2},{4,5},{5,4},{6,7},{7,6},{8,9},{9,8},{10,11... | collective-permute-start | bytes 2457608 | tf_op jit(solution)/shard_map/ppermute | solution.py:227
  24.3 12.2 %collective-permute-start.11 = (f32[400,512]{1,0:T(8,128)S(1)}, f32[400,512]{1,0:T(8,128)S(1)}, u32[]{:S(2)}, u32[]{:S(2)}) collective-permute-start(f32[400,512]{1,0:T(8,128)S(1)} %back.5), channel_id=1, source_target_pairs={{0,1},{1,0},{2,3},{3,2},{4,5},{5,4},{6,7},{7,6},{8,9},{9,8},{10,11... | collective-permute-start | bytes 2457608 | tf_op jit(solution)/shard_map/ppermute | solution.py:227
  24.6 3.8 %collective-permute-start.7 = (f32[16,384]{1,0:T(8,128)S(1)}, f32[16,384]{1,0:T(8,128)S(1)}, u32[]{:S(2)}, u32[]{:S(2)}) collective-permute-start(f32[16,384]{1,0:T(8,128)S(1)} %add.14.total_ref), channel_id=1, source_target_pairs={{0,16},{1,49},{2,18},{3,51},{4,20},{5,53},{6,22},{7,55},{8,24},{9,... | collective-permute-start | bytes 73736 | tf_op jit(solution)/shard_map/ppermute | solution.py:233
  26.2 3.8 %collective-permute-start.6 = (f32[16,384]{1,0:T(8,128)S(1)}, f32[16,384]{1,0:T(8,128)S(1)}, u32[]{:S(2)}, u32[]{:S(2)}) collective-permute-start(f32[16,384]{1,0:T(8,128)S(1)} %add.14.total_ref), channel_id=1, source_target_pairs={{0,16},{1,33},{2,18},{3,35},{4,20},{5,37},{6,22},{7,39},{8,24},{9,... | collective-permute-start | bytes 73736 | tf_op jit(solution)/shard_map/ppermute | solution.py:233
  30.0 2.6 %collective-permute-start.8 = (f32[16,384]{1,0:T(8,128)S(1)}, f32[16,384]{1,0:T(8,128)S(1)}, u32[]{:S(2)}, u32[]{:S(2)}) collective-permute-start(f32[16,384]{1,0:T(8,128)S(1)} %mix.3), channel_id=1, source_target_pairs={{0,1},{1,0},{2,3},{3,2},{4,5},{5,4},{6,7},{7,6},{8,9},{9,8},{10,11... | collective-permute-start | bytes 73736 | tf_op jit(solution)/shard_map/ppermute | solution.py:227
  32.7 3.8 %collective-permute-start.9 = (f32[16,384]{1,0:T(8,128)S(1)}, f32[16,384]{1,0:T(8,128)S(1)}, u32[]{:S(2)}, u32[]{:S(2)}) collective-permute-start(f32[16,384]{1,0:T(8,128)S(1)} %add.15.own_ref), channel_id=1, source_target_pairs={{0,64},{1,65},{2,66},{3,67},{4,68},{5,69},{6,70},{7,71},{8,72},{9,... | collective-permute-start | bytes 73736 | tf_op jit(solution)/shard_map/ppermute | solution.py:233
  36.5 5.2 %collective-permute-start.12 = (f32[16,512]{1,0:T(8,128)S(1)}, f32[16,512]{1,0:T(8,128)S(1)}, u32[]{:S(2)}, u32[]{:S(2)}) collective-permute-start(f32[16,512]{1,0:T(8,128)S(1)} %source.1.source_ref), channel_id=1, source_target_pairs={{0,192},{1,193},{2,194},{3,195},{4,196},{5,197},{6,198},{7,199},{8... | collective-permute-start | bytes 98312 | tf_op jit(solution)/shard_map/ppermute | solution.py:233

commit v6 on v4

v6 whole, which is shorter than its diff:
```python
import functools

import jax
import jax.numpy as jnp
from jax import lax
from jax.experimental import pallas as pl
from jax.experimental.pallas import tpu as pltpu
from jax.sharding import PartitionSpec as P

F32, BF16 = jnp.float32, jnp.bfloat16
MIB = 1 << 20
VMEM = pl.BlockSpec(memory_space=pltpu.VMEM)
HBM = pl.BlockSpec(memory_space=pltpu.HBM)
NN = (((1,), (0,)), ((), ()))
NT = (((1,), (1,)), ((), ()))
TN = (((0,), (0,)), ((), ()))


def shape(*dims, dtype=F32):
    return jax.ShapeDtypeStruct(dims, dtype)


def dot(a, b, dims=NN):
    return lax.dot_general(a, b, dims, preferred_element_type=F32)


def split(x):
    high = x.astype(BF16)
    return high, (x - high.astype(F32)).astype(BF16)


def product(a, split_b, dims=NN):
    ah, al = split(a)
    bh, bl = split_b
    rows = a.shape[0]
    both = dot(jnp.concatenate([ah, al], axis=0), bh, dims)
    return both[:rows] + both[rows:] + dot(ah, bl, dims)


def call(name, body, outs, ins, scratch=(), limit=24):
    return pl.pallas_call(
        body,
        out_shape=outs,
        in_specs=ins,
        out_specs=[VMEM] * len(outs),
        scratch_shapes=list(scratch),
        compiler_params=pltpu.CompilerParams(vmem_limit_bytes=limit * MIB),
        name=name,
    )


def load_columns(inverse_ref, firsts, chunk, a_ref, sems):
    copies = []
    for s, first in enumerate(firsts):
        start = pl.multiple_of(first, chunk)
        copy = pltpu.make_async_copy(inverse_ref.at[:, pl.ds(start, chunk)], a_ref.at[s], sems.at[s])
        copy.start()
        copies.append(copy)
    return copies


def load_kernel(chunk, inverse_ref, ah_ref, al_ref, a_ref, sems):
    steps, half = ah_ref.shape[:2]
    firsts = [lax.axis_index("sep") * half + s * chunk for s in range(steps)]
    for s, copy in enumerate(load_columns(inverse_ref, firsts, chunk, a_ref, sems)):
        copy.wait()
        ah_ref[s], al_ref[s] = split(a_ref[s])


def paired(x):
    return jnp.concatenate(split(x), axis=0)


def one_hot(index_ref, level, rows, first):
    row = lax.broadcasted_iota(jnp.int32, (rows, index_ref.shape[2]), 0) + first
    return jnp.where(row == index_ref[level], 1.0, 0.0).astype(BF16)


def leaf_kernel(chunk, mine_ref, theirs_ref, index_ref, coupling_ref, hh_ref, hl_ref, inverse_ref, term_ref, u_ref, ah_ref, al_ref, a_ref, sems):
    n, half = mine_ref.shape
    levels, _, k = index_ref.shape
    side = lax.axis_index("sep")
    firsts = [(1 - side) * half + s * chunk for s in range(half // chunk)]
    copies = load_columns(inverse_ref, firsts, chunk, a_ref, sems)
    total = jnp.zeros((2 * n, half), F32)
    for s in range(half // chunk):
        x = paired(mine_ref[:, s * chunk:(s + 1) * chunk])
        total = total + (dot(x, hh_ref[s], NT) + dot(x, hl_ref[s], NT))
    hot = [one_hot(index_ref, level, half, side * half) for level in range(levels)]
    for s, copy in enumerate(copies):
        x = paired(theirs_ref[:, s * chunk:(s + 1) * chunk])
        copy.wait()
        ah, al = split(a_ref[s])
        ah_ref[s] = ah
        al_ref[s] = al
        total = total + (dot(x, ah, NT) + dot(x, al, NT))
    u = total[:n] + total[n:]
    u_ref[...] = u
    uh, um = split(u)
    ul = (u - uh.astype(F32) - um.astype(F32)).astype(BF16)
    parts = jnp.concatenate([uh, um, ul], axis=0)
    picked = dot(parts, jnp.concatenate(hot, axis=1))
    picked = picked[:n] + picked[n:2 * n] + picked[2 * n:]
    for level in range(levels):
        cols = slice(level * k, (level + 1) * k)
        term_ref[:, cols] = product(picked[:, cols], split(coupling_ref[level]), NT)


def spread_kernel(index_ref, coupling_ref, high_ref, low_ref):
    levels, _, k = index_ref.shape
    half = high_ref.shape[1]
    for level in range(levels):
        hot = one_hot(index_ref, level, half, lax.axis_index("sep") * half)
        ch, cl = split(coupling_ref[level])
        moved = dot(jnp.concatenate([ch, cl], axis=0), hot, NT).astype(BF16)
        high_ref[level * k:(level + 1) * k, :] = moved[:k]
        low_ref[level * k:(level + 1) * k, :] = moved[k:]


def back_kernel(first, last, u_ref, high_ref, low_ref, ah_ref, al_ref, out_ref):
    n = u_ref.shape[0]
    uh, ul = split(u_ref[...])
    low = low_ref[...]
    left = jnp.concatenate([high_ref[...], uh, ul], axis=0)
    m = low.shape[0]
    chunk = ah_ref.shape[2]
    for s in range(first, last, 2):
        taken = range(s, min(s + 2, last))
        cols = slice((s - first) * chunk, (taken[-1] + 1 - first) * chunk)
        ah = jnp.concatenate([ah_ref[i] for i in taken], axis=1)
        al = jnp.concatenate([al_ref[i] for i in taken], axis=1)
        one = dot(left, ah)
        three = dot(left[:m + n], al)
        out_ref[:m, cols] = one[:m] + dot(low, ah) + three[:m]
        out_ref[m:, cols] = one[m:m + n] + one[m + n:] + three[m:]


def square(x):
    high, low = split(x)
    return dot(high, high, TN) + dot(low, high, TN) + dot(high, low, TN)


def pair_matrices(inverse_ref, parent_ref, near, sibling, middle):
    g0 = product(parent_ref[near], split(inverse_ref[near]))
    gs = product(parent_ref[sibling], split(inverse_ref[sibling]))
    g1 = product(parent_ref[middle], split(inverse_ref[middle]))
    return g0, gs, g1, jnp.concatenate([g1, -product(g1, split(g0)), -product(g1, split(gs))], axis=1)


def tree_kernel(inverse_ref, parent_ref, rhs_ref, wayh_ref, wayl_ref, own_ref, chosen_ref):
    k = inverse_ref.shape[1]
    plane = lax.axis_index("leaf") >> 5
    near, sibling, middle = plane, plane ^ 1, 4 + (plane >> 1)
    g0, gs, g1, way = pair_matrices(inverse_ref, parent_ref, near, sibling, middle)
    wayh_ref[...], wayl_ref[...] = split(way)
    own_ref[0] = g0
    own_ref[1] = gs
    own_ref[2] = square(inverse_ref[near])
    own_ref[3] = square(inverse_ref[middle])
    own_ref[4] = g1
    chosen_ref[:, :k] = rhs_ref[middle]
    chosen_ref[:, k:2 * k] = rhs_ref[near]
    chosen_ref[:, 2 * k:3 * k] = rhs_ref[sibling]
    chosen_ref[:, 3 * k:] = rhs_ref[inverse_ref.shape[0] - 1]


def root_kernel(inverse_ref, parent_ref, own_ref, wayh_ref, wayl_ref, root_ref):
    k = inverse_ref.shape[1]
    plane = 3 - (lax.axis_index("leaf") >> 5)
    way = pair_matrices(inverse_ref, parent_ref, plane, plane ^ 1, 4 + (plane >> 1))[3]
    wayh_ref[...], wayl_ref[...] = split(way)
    h2 = square(inverse_ref[inverse_ref.shape[0] - 1])
    k1 = product(h2, split(own_ref[4]))
    root_ref[:, :k] = product(k1, split(own_ref[0]))
    root_ref[:, k:2 * k] = -k1
    root_ref[:, 2 * k:] = h2


def columns_of(refs, chunk):
    return [ref.at[:, s:s + chunk] for ref in refs for s in range(0, ref.shape[1], chunk)]


def join_kernel(chunk, mine_ref, got_ref, root_ref, base_ref, low_ref, qh_ref, ql_ref):
    k = root_ref.shape[0]
    root = root_ref[...]
    m = root.shape[1]
    width = base_ref.shape[1]
    pairs = zip(columns_of((mine_ref,), chunk), columns_of((got_ref,), chunk))
    for s, (mine_ref, got_ref) in enumerate(pairs):
        cols = slice(s * chunk, (s + 1) * chunk)
        b = mine_ref[:m, :] + got_ref[:m, :]
        base_ref[:, cols] = mine_ref[m:, :] + got_ref[m:, :]
        low_ref[:, cols] = b[:2 * k]
        qh_ref[:, cols], ql_ref[:, cols] = split(product(root, split(b)))
    qh_ref[:, width:], ql_ref[:, width:] = split(root)


def octet_kernel(total_ref, four_ref, one_ref, two_ref, three_ref, out_ref):
    own = total_ref[...] + four_ref[...]
    first = lax.axis_index("sep") == 0
    out_ref[...] = one_ref[...] + two_ref[...] + three_ref[...] + jnp.where(first, own, 0.0)


def pair_kernel(total_ref, near_ref, five_ref, six_ref, two_ref, out_ref):
    m = total_ref.shape[1]
    first = lax.axis_index("sep") == 0
    heard = five_ref[...] + six_ref[...] + two_ref[...]
    out_ref[:, :m] = jnp.where(first, total_ref[...] + heard, 0.0)
    out_ref[:, m:] = jnp.where(first, near_ref[...], heard)


def source_kernel(part_ref, got_ref, chosen_ref, out_ref):
    k = part_ref.shape[1] // 6
    own = part_ref[:, :3 * k] + got_ref[:, :3 * k]
    other = part_ref[:, 3 * k:] + got_ref[:, 3 * k:]
    out_ref[:, :k] = chosen_ref[:, :k] - own[:, k:2 * k] - other[:, k:2 * k]
    out_ref[:, k:2 * k] = chosen_ref[:, k:2 * k] - own[:, :k]
    out_ref[:, 2 * k:3 * k] = chosen_ref[:, 2 * k:3 * k] - other[:, :k]
    out_ref[:, 3 * k:] = own[:, 2 * k:] + other[:, 2 * k:]


def lower_kernel(source_ref, chosen_ref, wayh_ref, wayl_ref, own_ref, base_ref, low_ref, pre_ref, solved_ref, top_ref):
    k = own_ref.shape[1]
    t1, s0, sb = source_ref[:, :k], source_ref[:, k:2 * k], source_ref[:, 2 * k:3 * k]
    c0 = product(s0, split(own_ref[2]))
    s1 = t1 - product(s0, split(own_ref[0]), NT) - product(sb, split(own_ref[1]), NT)
    c1 = product(s1, split(own_ref[3]))
    c0 = c0 - product(c1, split(own_ref[0]))
    solved_ref[0] = c0
    solved_ref[1] = c1
    pre_ref[...] = base_ref[...] - product(jnp.concatenate([c0, c1], axis=1), split(low_ref[...]))
    up = product(source_ref[:, :3 * k], (wayh_ref[...], wayl_ref[...]), NT)
    top_ref[...] = chosen_ref[:, 3 * k:] - source_ref[:, 3 * k:] - up


def last_kernel(other_ref, wayh_ref, wayl_ref, top_ref, pre_ref, solved_ref, qh_ref, ql_ref, out_ref, sep_ref):
    k = top_ref.shape[1]
    width = pre_ref.shape[1]
    up = product(other_ref[:, :3 * k], (wayh_ref[...], wayl_ref[...]), NT)
    s2 = top_ref[...] - other_ref[:, 3 * k:] - up
    add = product(s2, (qh_ref[...], ql_ref[...]))
    out_ref[...] = pre_ref[...] - add[:, :width]
    sep_ref[0] = solved_ref[0] + add[:, width:width + k]
    sep_ref[1] = solved_ref[1] + add[:, width + k:width + 2 * k]
    sep_ref[2] = add[:, width + 2 * k:]


def swap_core(x):
    return lax.ppermute(x, "sep", [(0, 1), (1, 0)])


def swap_leaf(x, mask, first_mask=None):
    masks = (mask if first_mask is None else first_mask, mask)
    count = 2 * lax.axis_size("leaf")
    return lax.ppermute(x, ("leaf", "sep"), [(i, i ^ 2 * masks[i % 2]) for i in range(count)])


def ordered(*arrays):
    return lax.optimization_barrier(arrays)


def local(leaf_rhs, leaf_inverse, skeleton_index, leaf_coupling, sep_rhs, sep_inverse, sep_parent):
    mine, coupling = leaf_rhs[0], leaf_coupling[0]
    index = jnp.transpose(skeleton_index, (1, 0, 2))
    inverse = leaf_inverse[0]
    n, half = mine.shape
    levels, _, k = index.shape
    m = levels * k
    chunk = 256
    steps = half // chunk
    slots = [pltpu.VMEM((steps, half, chunk), F32), pltpu.SemaphoreType.DMA((steps,))]
    parts = [shape(steps, half, chunk, dtype=BF16)] * 2
    theirs = swap_core(mine)
    home = call("load", functools.partial(load_kernel, chunk), parts, [HBM], slots, limit=48)(inverse)
    term, u, *away = call("leaf", functools.partial(leaf_kernel, chunk), [shape(n, m), shape(n, half)] + parts,
                          [VMEM] * 6 + [HBM], slots, limit=43)(mine, theirs, index, coupling, *home, inverse)
    term, index, coupling = ordered(term, index, coupling)
    got = swap_core(term)
    high, low = call("spread", spread_kernel, [shape(m, half, dtype=BF16)] * 2, [VMEM, VMEM])(index, coupling)
    term, high, low, got = ordered(term, high, low, got)
    total = term + got

    def back(u, split_inverse, first, last):
        out, = call("back", functools.partial(back_kernel, first, last), [shape(m + n, (last - first) * chunk)],
                    [VMEM] * 5)(u, high, low, *split_inverse)
        return out

    total, u = ordered(total, u)
    heard = [swap_leaf(total, *masks) for masks in ((1, 1), (24, 8), (16, 25), (17, 9))]
    sent0 = back(u, away, 0, steps)
    total, sent0, *heard = ordered(total, sent0, *heard)
    total, = call("octet", octet_kernel, [shape(n, m)], [VMEM] * 5)(total, *heard)
    total, sep_inverse, sep_parent, sep_rhs = ordered(total, sep_inverse, sep_parent, sep_rhs)
    got = swap_core(total)
    wayh, wayl, own, chosen = call(
        "tree", tree_kernel, [shape(k, m, dtype=BF16)] * 2 + [shape(5, k, k), shape(n, m + k)],
        [VMEM] * 3)(sep_inverse, sep_parent, sep_rhs)
    total, got, own = ordered(total, got, own)
    total = total + got

    total, u, sent0 = ordered(total, u, sent0)
    received0 = swap_core(sent0)
    heard = [swap_leaf(total, *masks) for masks in ((1, 32), (34, 2), (38, 6), (37, 5))]
    kept0 = back(u, home, 0, steps)
    total, kept0, *heard = ordered(total, kept0, *heard)
    part, = call("pair", pair_kernel, [shape(n, 2 * m)], [VMEM] * 5)(total, *heard)
    part, own, sep_inverse, sep_parent = ordered(part, own, sep_inverse, sep_parent)
    got = swap_core(part)
    otherh, otherl, root = call(
        "root", root_kernel, [shape(k, m, dtype=BF16)] * 2 + [shape(k, m)], [VMEM] * 3)(sep_inverse, sep_parent, own)
    part, got, root = ordered(part, got, root)
    source, = call("source", source_kernel, [shape(n, m + k)], [VMEM] * 3)(part, got, chosen)

    source, u, root = ordered(source, u, root)
    other = swap_leaf(source, 96)
    base, lower, qh, ql = call("join", functools.partial(join_kernel, chunk),
                               [shape(n, half), shape(2 * k, half)] + [shape(k, half + m, dtype=BF16)] * 2,
                               [VMEM] * 3)(kept0, received0, root)
    pre, solved, top = call("lower", lower_kernel, [shape(n, half), shape(2, n, k), shape(n, k)], [VMEM] * 7)(
        source, chosen, wayh, wayl, own, base, lower)
    pre, other = ordered(pre, other)
    out, sep = call("last", last_kernel, [shape(n, half), shape(levels, n, k)], [VMEM] * 8)(
        other, otherh, otherl, top, pre, solved, qh, ql)
    return (out[None], sep[None])


def solution(mesh):
    placed = (
        P("leaf", None, "sep"),
        P("leaf", "sep", None),
        P("leaf", None, None),
        P("leaf", None, None, None),
        P(),
        P(),
        P(),
    )
    return jax.shard_map(
        local,
        mesh=mesh,
        in_specs=placed,
        out_specs=(P("leaf", None, "sep"), P("leaf", None, None, None)),
        check_vma=False,
    )
```

time: 56.2 us -> 41 us (0.73)
  starting transfers between devices: 32.4 us -> 20.8 us
  waiting for transfers between devices: 5.15 us -> 2.94 us
  Pallas kernels: 17.3 us -> 16.4 us
    ppermute x9, starting transfers between devices: 28.6 us -> 16.4 us  [swap_leaf(): lax.ppermute(x, ('leaf', 'sep'), [(i, i ^ 2 * masks[i % 2]) for i in rang...]
    ppermute x9, waiting for transfers between devices: 4.59 us -> 1.59 us  [swap_leaf(): lax.ppermute(x, ('leaf', 'sep'), [(i, i ^ 2 * masks[i % 2]) for i in rang...]
    ppermute x4 -> x5, waiting for transfers between devices: 0.56 us -> 1.35 us  [swap_core(): return lax.ppermute(x, 'sep', [(0, 1), (1, 0)])]
    pallas_call x6 -> x7, Pallas kernels: 8.12 us -> 7.43 us  [the longest x2 5.47 us: back(): call('back', functools.partial(back_kernel, first, last), [shape(m + n, (...]
    ppermute x4 -> x5, starting transfers between devices: 3.79 us -> 4.34 us  [swap_core(): return lax.ppermute(x, 'sep', [(0, 1), (1, 0)])]
  transfers between devices with their start and end apart: 13 -> 14, of which waited for: 7 -> 5; matrix products, arithmetic and copies ran while one was open for 0% -> 0% of each run, Pallas kernels for 21% -> 27%
where the time goes in v6:
time: 41 us; the launch traced here: 40.9 us
  starting transfers between devices  20.8 us (51%)
  Pallas kernels  16.4 us (40%)
  waiting for transfers between devices  2.94 us (7%)
  between operations  0.81 us (2%)
    ppermute x9, starting transfers between devices, swap_leaf(): lax.ppermute(x, ('leaf', 'sep'), [(i, i ^ 2 * masks[i % 2]) for i in rang...  16.4 us
    pallas_call x2, Pallas kernels, back(): call('back', functools.partial(back_kernel, first, last), [shape(m + n, (...  5.47 us
    ppermute x5, starting transfers between devices, swap_core(): return lax.ppermute(x, 'sep', [(0, 1), (1, 0)])  4.34 us
    pallas_call x1, Pallas kernels, local(): call('leaf', functools.partial(leaf_kernel, chunk), [shape(n, m), shape(n...  4.06 us
    pallas_call x1, Pallas kernels, local(): call('load', functools.partial(load_kernel, chunk), parts, [HBM], slots,...  2.41 us
    ppermute x9, waiting for transfers between devices, swap_leaf(): lax.ppermute(x, ('leaf', 'sep'), [(i, i ^ 2 * masks[i % 2]) for i in rang...  1.59 us
    ppermute x5, waiting for transfers between devices, swap_core(): return lax.ppermute(x, 'sep', [(0, 1), (1, 0)])  1.35 us
    pallas_call x1, Pallas kernels, local(): call('last', last_kernel, [shape(n, half), shape(levels, n, k)], [VMEM] * 8)  1.09 us
  transfers between devices with their start and end apart: 14, of which 5 were waited for; matrix products, arithmetic and copies ran while one was open for 0% of the time, Pallas kernels for 27%

profile of v6, /device:TPU:1, one launch (start us, length us, event | category | flops | bytes accessed | tf_op | source)
XLA Modules:
  0.0 40.9 jit_solution(5504162730891355110)
XLA Ops:
  0.6 3.3 %collective-permute-start = (f32[16,1024]{1,0:T(8,128)}, f32[16,1024]{1,0:T(8,128)S(1)}, u32[]{:S(2)}, u32[]{:S(2)}) collective-permute-start(f32[16,1024]{1,0:T(8,128)} %bitcast.8), channel_id=1, source_target_pairs={{0,1},{1,0},{2,3},{3,2},{4,5},{5,4},{6,7},{7,6},{8,9},{9,8},{10,11... | collective-permute-start | bytes 196616 | tf_op jit(solution)/shard_map/ppermute | solution.py:249
  4.0 2.4 %load.1 = (bf16[4,1024,256]{2,1,0:T(8,128)(2,1)S(1)}, bf16[4,1024,256]{2,1,0:T(8,128)(2,1)S(1)}) custom-call(f32[1024,2048]{1,0:T(8,128)} %bitcast.12), custom_call_target="tpu_custom_call" | custom-call | tf_op jit(solution)/shard_map/load/pallas_call | solution.py:274
  6.4 4.1 %leaf.1 = (f32[16,384]{1,0:T(8,128)S(1)}, f32[16,1024]{1,0:T(8,128)S(1)}, bf16[4,1024,256]{2,1,0:T(8,128)(2,1)S(1)}, bf16[4,1024,256]{2,1,0:T(8,128)(2,1)S(1)}) custom-call(f32[16,1024]{1,0:T(8,128)S(1)} %bitcast.9, f32[16,1024]{1,0:T(8,128)S(1)} %collective-permute-done.theirs_ref, s32[3,1,128]{2,1,0:T(1,128)S(1)} %bitcast.10, f32[3,128,128]{2,1,0:T(8,128)S(1)} %bitcast.6, ...), custom_call_target="tpu_custom_call" | custom-call | tf_op jit(solution)/shard_map/leaf/pallas_call | solution.py:275
  10.6 0.6 %spread.1 = (bf16[384,1024]{1,0:T(8,128)(2,1)S(1)}, bf16[384,1024]{1,0:T(8,128)(2,1)S(1)}) custom-call(s32[3,1,128]{2,1,0:T(1,128)S(1)} %bitcast.11, f32[3,128,128]{2,1,0:T(8,128)S(1)} %bitcast.7), custom_call_target="tpu_custom_call" | custom-call | tf_op jit(solution)/shard_map/spread/pallas_call | solution.py:279
  11.2 0.6 %collective-permute-done.1 = f32[16,384]{1,0:T(8,128)S(1)} collective-permute-done((f32[16,384]{1,0:T(8,128)S(1)}, f32[16,384]{1,0:T(8,128)S(1)}, u32[]{:S(2)}, u32[]{:S(2)}) %collective-permute-start.1) | collective-permute-done | bytes 24608 | tf_op jit(solution)/shard_map/ppermute | solution.py:249
  11.8 2.5 %collective-permute-start.5 = (f32[16,384]{1,0:T(8,128)S(1)}, f32[16,384]{1,0:T(8,128)S(1)}, u32[]{:S(2)}, u32[]{:S(2)}) collective-permute-start(f32[16,384]{1,0:T(8,128)S(1)} %add.6.total_ref), channel_id=1, source_target_pairs={{0,18},{1,35},{2,16},{3,33},{4,22},{5,39},{6,20},{7,37},{8,26},{9,... | collective-permute-start | bytes 73736 | tf_op jit(solution)/shard_map/ppermute | solution.py:255
  14.4 2.7 %collective-permute-start.3 = (f32[16,384]{1,0:T(8,128)S(1)}, f32[16,384]{1,0:T(8,128)S(1)}, u32[]{:S(2)}, u32[]{:S(2)}) collective-permute-start(f32[16,384]{1,0:T(8,128)S(1)} %add.6.total_ref), channel_id=1, source_target_pairs={{0,16},{1,49},{2,18},{3,51},{4,20},{5,53},{6,22},{7,55},{8,24},{9,... | collective-permute-start | bytes 73736 | tf_op jit(solution)/shard_map/ppermute | solution.py:255
  17.1 2.7 %back.2 = f32[400,1024]{1,0:T(8,128)S(1)} custom-call(f32[16,1024]{1,0:T(8,128)S(1)} %get-tuple-element.99.u_ref, bf16[384,1024]{1,0:T(8,128)(2,1)S(1)} %get-tuple-element.81.high_ref, bf16[384,1024]{1,0:T(8,128)(2,1)S(1)} %get-tuple-element.82.low_ref, bf16[4,1024,256]{2,1,0:T(8,128)(2,1)S(1)} %get-tuple-element.83.ah_ref, ...), custom_call_target="tpu_custom_call" | custom-call | tf_op jit(solution)/shard_map/back/pallas_call | solution.py:284
  19.9 0.4 %collective-permute-start.6 = (f32[16,384]{1,0:T(8,128)S(1)}, f32[16,384]{1,0:T(8,128)S(1)}, u32[]{:S(2)}, u32[]{:S(2)}) collective-permute-start(f32[16,384]{1,0:T(8,128)S(1)} %octet.1), channel_id=1, source_target_pairs={{0,1},{1,0},{2,3},{3,2},{4,5},{5,4},{6,7},{7,6},{8,9},{9,8},{10,11... | collective-permute-start | bytes 73736 | tf_op jit(solution)/shard_map/ppermute | solution.py:249
  20.4 0.5 %tree.1 = (bf16[128,384]{1,0:T(8,128)(2,1)S(1)}, bf16[128,384]{1,0:T(8,128)(2,1)S(1)}, f32[5,128,128]{2,1,0:T(8,128)S(1)}, f32[16,512]{1,0:T(8,128)S(1)}) custom-call(f32[7,128,128]{2,1,0:T(8,128)S(1)} %copy-done, f32[6,128,128]{2,1,0:T(8,128)S(1)} %copy-done.1, f32[7,16,128]{2,1,0:T(8,128)S(1)} %copy-done.4), custom_call_target="tpu_custom_call" | custom-call | tf_op jit(solution)/shard_map/tree/pallas_call | solution.py:295
  20.8 0.4 collective-permute-done.6
  21.2 0.3 collective-permute-start.12
  21.6 7.0 %collective-permute-start.10 = (f32[16,384]{1,0:T(8,128)S(1)}, f32[16,384]{1,0:T(8,128)S(1)}, u32[]{:S(2)}, u32[]{:S(2)}) collective-permute-start(f32[16,384]{1,0:T(8,128)S(1)} %add.7.total_ref), channel_id=1, source_target_pairs={{0,10},{1,75},{2,8},{3,73},{4,14},{5,79},{6,12},{7,77},{8,2},{9,67... | collective-permute-start | bytes 73736 | tf_op jit(solution)/shard_map/ppermute | solution.py:255
  28.8 0.9 %collective-permute-start.8 = (f32[16,384]{1,0:T(8,128)S(1)}, f32[16,384]{1,0:T(8,128)S(1)}, u32[]{:S(2)}, u32[]{:S(2)}) collective-permute-start(f32[16,384]{1,0:T(8,128)S(1)} %add.7.total_ref), channel_id=1, source_target_pairs={{0,4},{1,69},{2,6},{3,71},{4,0},{5,65},{6,2},{7,67},{8,12},{9,77},... | collective-permute-start | bytes 73736 | tf_op jit(solution)/shard_map/ppermute | solution.py:255
  29.8 0.7 %collective-permute-start.7 = (f32[16,384]{1,0:T(8,128)S(1)}, f32[16,384]{1,0:T(8,128)S(1)}, u32[]{:S(2)}, u32[]{:S(2)}) collective-permute-start(f32[16,384]{1,0:T(8,128)S(1)} %add.7.total_ref), channel_id=1, source_target_pairs={{0,64},{1,3},{2,66},{3,1},{4,68},{5,7},{6,70},{7,5},{8,72},{9,11},... | collective-permute-start | bytes 73736 | tf_op jit(solution)/shard_map/ppermute | solution.py:255
  30.5 2.7 %back.3.mine_ref = f32[400,1024]{1,0:T(8,128)S(1)} custom-call(f32[16,1024]{1,0:T(8,128)S(1)} %get-tuple-element.99.u_ref, bf16[384,1024]{1,0:T(8,128)(2,1)S(1)} %get-tuple-element.81.high_ref, bf16[384,1024]{1,0:T(8,128)(2,1)S(1)} %get-tuple-element.82.low_ref, bf16[4,1024,256]{2,1,0:T(8,128)(2,1)S(1)} %get-tuple-element.68.hh_ref.ah_ref, ...), custom_call_target="tpu_custom_call" | custom-call | tf_op jit(solution)/shard_map/back/pallas_call | solution.py:284
  33.2 1.2 %collective-permute-done.9.six_ref = f32[16,384]{1,0:T(8,128)S(1)} collective-permute-done((f32[16,384]{1,0:T(8,128)S(1)}, f32[16,384]{1,0:T(8,128)S(1)}, u32[]{:S(2)}, u32[]{:S(2)}) %collective-permute-start.9) | collective-permute-done | bytes 24608 | tf_op jit(solution)/shard_map/ppermute | solution.py:255
  34.6 0.8 %root.1 = (bf16[128,384]{1,0:T(8,128)(2,1)S(1)}, bf16[128,384]{1,0:T(8,128)(2,1)S(1)}, f32[128,384]{1,0:T(8,128)S(1)}) custom-call(f32[7,128,128]{2,1,0:T(8,128)S(1)} %copy-done, f32[6,128,128]{2,1,0:T(8,128)S(1)} %copy-done.1, f32[5,128,128]{2,1,0:T(8,128)S(1)} %get-tuple-element.109.own_ref), custom_call_target="tpu_custom_call" | custom-call | tf_op jit(solution)/shard_map/root/pallas_call | solution.py:309
  35.4 0.4 %collective-permute-done.11.got_ref = f32[16,768]{1,0:T(8,128)S(1)} collective-permute-done((f32[16,768]{1,0:T(8,128)S(1)}, f32[16,768]{1,0:T(8,128)S(1)}, u32[]{:S(2)}, u32[]{:S(2)}) %collective-permute-start.11) | collective-permute-done | bytes 49184 | tf_op jit(solution)/shard_map/ppermute | solution.py:249
  35.8 2.2 %collective-permute-start.13 = (f32[16,512]{1,0:T(8,128)S(1)}, f32[16,512]{1,0:T(8,128)S(1)}, u32[]{:S(2)}, u32[]{:S(2)}) collective-permute-start(f32[16,512]{1,0:T(8,128)S(1)} %source.1.source_ref), channel_id=1, source_target_pairs={{0,192},{1,193},{2,194},{3,195},{4,196},{5,197},{6,198},{7,199},{8... | collective-permute-start | bytes 98312 | tf_op jit(solution)/shard_map/ppermute | solution.py:255
  38.0 0.7 %join.1 = (f32[16,1024]{1,0:T(8,128)S(1)}, f32[256,1024]{1,0:T(8,128)S(1)}, bf16[128,1408]{1,0:T(8,128)(2,1)S(1)}, bf16[128,1408]{1,0:T(8,128)(2,1)S(1)}) custom-call(f32[400,1024]{1,0:T(8,128)S(1)} %back.3.mine_ref, f32[400,1024]{1,0:T(8,128)S(1)} %collective-permute-done.12.got_ref, f32[128,384]{1,0:T(8,128)S(1)} %get-tuple-element.120.root_ref), custom_call_target="tpu_custom_call" | custom-call | tf_op jit(solution)/shard_map/join/pallas_call | solution.py:316
  38.6 0.8 %lower.1 = (f32[16,1024]{1,0:T(8,128)S(1)}, f32[2,16,128]{2,1,0:T(8,128)S(1)}, f32[16,128]{1,0:T(8,128)S(1)}) custom-call(f32[16,512]{1,0:T(8,128)S(1)} %source.1.source_ref, f32[16,512]{1,0:T(8,128)S(1)} %get-tuple-element.113.chosen_ref, bf16[128,384]{1,0:T(8,128)(2,1)S(1)} %get-tuple-element.116.wayh_ref, ...), custom_call_target="tpu_custom_call" | custom-call | tf_op jit(solution)/shard_map/lower/pallas_call | solution.py:319
  39.5 0.4 collective-permute-done.13.other_ref
  39.9 1.1 %last.1 = (f32[16,1024]{1,0:T(8,128)}, f32[3,16,128]{2,1,0:T(8,128)}) custom-call(f32[16,512]{1,0:T(8,128)S(1)} %collective-permute-done.13.other_ref, bf16[128,384]{1,0:T(8,128)(2,1)S(1)} %get-tuple-element.125.wayh_ref, bf16[128,384]{1,0:T(8,128)(2,1)S(1)} %get-tuple-element.126.wayl_ref, f32[16,128]{1,0:T(8,128)S(1)} %get-tuple-element.127.top_ref, ...), custom_call_target="tpu_custom_call" | custom-call | tf_op jit(solution)/shard_map/last/pallas_call | solution.py:322
  (31 shorter events, 0.6 us)
Async XLA Ops:
  0.6 5.8 %collective-permute-start = (f32[16,1024]{1,0:T(8,128)}, f32[16,1024]{1,0:T(8,128)S(1)}, u32[]{:S(2)}, u32[]{:S(2)}) collective-permute-start(f32[16,1024]{1,0:T(8,128)} %bitcast.8), channel_id=1, source_target_pairs={{0,1},{1,0},{2,3},{3,2},{4,5},{5,4},{6,7},{7,6},{8,9},{9,8},{10,11... | collective-permute-start | bytes 196616 | tf_op jit(solution)/shard_map/ppermute | solution.py:249
  4.0 2.4 %copy-start.2 = (f32[1,3,128,128]{3,2,1,0:T(8,128)S(1)}, f32[1,3,128,128]{3,2,1,0:T(8,128)}, u32[]{:S(2)}) copy-start(f32[1,3,128,128]{3,2,1,0:T(8,128)} %param.10) | copy-start | bytes 589828
  4.0 2.4 %copy-start.3 = (f32[1,16,1024]{2,1,0:T(8,128)S(1)}, f32[1,16,1024]{2,1,0:T(8,128)}, u32[]{:S(2)}) copy-start(f32[1,16,1024]{2,1,0:T(8,128)} %param.7) | copy-start | bytes 196612
  4.0 2.5 %copy-start.5 = (s32[1,3,128]{2,0,1:T(1,128)S(1)}, s32[1,3,128]{2,0,1:T(1,128)}, u32[]{:S(2)}) copy-start(s32[1,3,128]{2,0,1:T(1,128)} %param.9) | copy-start | bytes 4612
  10.5 1.3 %collective-permute-start.1 = (f32[16,384]{1,0:T(8,128)S(1)}, f32[16,384]{1,0:T(8,128)S(1)}, u32[]{:S(2)}, u32[]{:S(2)}) collective-permute-start(f32[16,384]{1,0:T(8,128)S(1)} %get-tuple-element.76), channel_id=1, source_target_pairs={{0,1},{1,0},{2,3},{3,2},{4,5},{5,4},{6,7},{7,6},{8,9},{9,8},{10,11... | collective-permute-start | bytes 73736 | tf_op jit(solution)/shard_map/ppermute | solution.py:249
  11.8 8.1 %collective-permute-start.5 = (f32[16,384]{1,0:T(8,128)S(1)}, f32[16,384]{1,0:T(8,128)S(1)}, u32[]{:S(2)}, u32[]{:S(2)}) collective-permute-start(f32[16,384]{1,0:T(8,128)S(1)} %add.6.total_ref), channel_id=1, source_target_pairs={{0,18},{1,35},{2,16},{3,33},{4,22},{5,39},{6,20},{7,37},{8,26},{9,... | collective-permute-start | bytes 73736 | tf_op jit(solution)/shard_map/ppermute | solution.py:255
  14.3 5.6 %collective-permute-start.4 = (f32[16,384]{1,0:T(8,128)S(1)}, f32[16,384]{1,0:T(8,128)S(1)}, u32[]{:S(2)}, u32[]{:S(2)}) collective-permute-start(f32[16,384]{1,0:T(8,128)S(1)} %add.6.total_ref), channel_id=1, source_target_pairs={{0,50},{1,33},{2,48},{3,35},{4,54},{5,37},{6,52},{7,39},{8,58},{9,... | collective-permute-start | bytes 73736 | tf_op jit(solution)/shard_map/ppermute | solution.py:255
  14.4 5.5 %collective-permute-start.3 = (f32[16,384]{1,0:T(8,128)S(1)}, f32[16,384]{1,0:T(8,128)S(1)}, u32[]{:S(2)}, u32[]{:S(2)}) collective-permute-start(f32[16,384]{1,0:T(8,128)S(1)} %add.6.total_ref), channel_id=1, source_target_pairs={{0,16},{1,49},{2,18},{3,51},{4,20},{5,53},{6,22},{7,55},{8,24},{9,... | collective-permute-start | bytes 73736 | tf_op jit(solution)/shard_map/ppermute | solution.py:255
  17.1 2.8 %collective-permute-start.2 = (f32[16,384]{1,0:T(8,128)S(1)}, f32[16,384]{1,0:T(8,128)S(1)}, u32[]{:S(2)}, u32[]{:S(2)}) collective-permute-start(f32[16,384]{1,0:T(8,128)S(1)} %add.6.total_ref), channel_id=1, source_target_pairs={{0,2},{1,3},{2,0},{3,1},{4,6},{5,7},{6,4},{7,5},{8,10},{9,11},{10,... | collective-permute-start | bytes 73736 | tf_op jit(solution)/shard_map/ppermute | solution.py:255
  17.1 3.3 %copy-start = (f32[7,128,128]{2,1,0:T(8,128)S(1)}, f32[7,128,128]{2,1,0:T(8,128)}, u32[]{:S(2)}) copy-start(f32[7,128,128]{2,1,0:T(8,128)} %inverse_ref.1) | copy-start | bytes 1376260
  17.1 3.3 %copy-start.1 = (f32[6,128,128]{2,1,0:T(8,128)S(1)}, f32[6,128,128]{2,1,0:T(8,128)}, u32[]{:S(2)}) copy-start(f32[6,128,128]{2,1,0:T(8,128)} %parent_ref.1) | copy-start | bytes 1179652
  17.1 3.3 %copy-start.4 = (f32[7,16,128]{2,1,0:T(8,128)S(1)}, f32[7,16,128]{2,1,0:T(8,128)}, u32[]{:S(2)}) copy-start(f32[7,16,128]{2,1,0:T(8,128)} %rhs_ref) | copy-start | bytes 172036
  19.9 1.3 %collective-permute-start.6 = (f32[16,384]{1,0:T(8,128)S(1)}, f32[16,384]{1,0:T(8,128)S(1)}, u32[]{:S(2)}, u32[]{:S(2)}) collective-permute-start(f32[16,384]{1,0:T(8,128)S(1)} %octet.1), channel_id=1, source_target_pairs={{0,1},{1,0},{2,3},{3,2},{4,5},{5,4},{6,7},{7,6},{8,9},{9,8},{10,11... | collective-permute-start | bytes 73736 | tf_op jit(solution)/shard_map/ppermute | solution.py:249
  21.2 16.7 %collective-permute-start.12 = (f32[400,1024]{1,0:T(8,128)S(1)}, f32[400,1024]{1,0:T(8,128)S(1)}, u32[]{:S(2)}, u32[]{:S(2)}) collective-permute-start(f32[400,1024]{1,0:T(8,128)S(1)} %back.2), channel_id=1, source_target_pairs={{0,1},{1,0},{2,3},{3,2},{4,5},{5,4},{6,7},{7,6},{8,9},{9,8},{10,11... | collective-permute-start | bytes 4915208 | tf_op jit(solution)/shard_map/ppermute | solution.py:249
  21.6 11.7 %collective-permute-start.10 = (f32[16,384]{1,0:T(8,128)S(1)}, f32[16,384]{1,0:T(8,128)S(1)}, u32[]{:S(2)}, u32[]{:S(2)}) collective-permute-start(f32[16,384]{1,0:T(8,128)S(1)} %add.7.total_ref), channel_id=1, source_target_pairs={{0,10},{1,75},{2,8},{3,73},{4,14},{5,79},{6,12},{7,77},{8,2},{9,67... | collective-permute-start | bytes 73736 | tf_op jit(solution)/shard_map/ppermute | solution.py:255
  28.6 5.8 %collective-permute-start.9 = (f32[16,384]{1,0:T(8,128)S(1)}, f32[16,384]{1,0:T(8,128)S(1)}, u32[]{:S(2)}, u32[]{:S(2)}) collective-permute-start(f32[16,384]{1,0:T(8,128)S(1)} %add.7.total_ref), channel_id=1, source_target_pairs={{0,12},{1,77},{2,14},{3,79},{4,8},{5,73},{6,10},{7,75},{8,4},{9,69... | collective-permute-start | bytes 73736 | tf_op jit(solution)/shard_map/ppermute | solution.py:255
  28.8 5.6 %collective-permute-start.8 = (f32[16,384]{1,0:T(8,128)S(1)}, f32[16,384]{1,0:T(8,128)S(1)}, u32[]{:S(2)}, u32[]{:S(2)}) collective-permute-start(f32[16,384]{1,0:T(8,128)S(1)} %add.7.total_ref), channel_id=1, source_target_pairs={{0,4},{1,69},{2,6},{3,71},{4,0},{5,65},{6,2},{7,67},{8,12},{9,77},... | collective-permute-start | bytes 73736 | tf_op jit(solution)/shard_map/ppermute | solution.py:255
  29.8 4.7 %collective-permute-start.7 = (f32[16,384]{1,0:T(8,128)S(1)}, f32[16,384]{1,0:T(8,128)S(1)}, u32[]{:S(2)}, u32[]{:S(2)}) collective-permute-start(f32[16,384]{1,0:T(8,128)S(1)} %add.7.total_ref), channel_id=1, source_target_pairs={{0,64},{1,3},{2,66},{3,1},{4,68},{5,7},{6,70},{7,5},{8,72},{9,11},... | collective-permute-start | bytes 73736 | tf_op jit(solution)/shard_map/ppermute | solution.py:255
  34.5 1.3 %collective-permute-start.11 = (f32[16,768]{1,0:T(8,128)S(1)}, f32[16,768]{1,0:T(8,128)S(1)}, u32[]{:S(2)}, u32[]{:S(2)}) collective-permute-start(f32[16,768]{1,0:T(8,128)S(1)} %pair.1.part_ref), channel_id=1, source_target_pairs={{0,1},{1,0},{2,3},{3,2},{4,5},{5,4},{6,7},{7,6},{8,9},{9,8},{10,11... | collective-permute-start | bytes 147464 | tf_op jit(solution)/shard_map/ppermute | solution.py:249
  35.8 4.1 %collective-permute-start.13 = (f32[16,512]{1,0:T(8,128)S(1)}, f32[16,512]{1,0:T(8,128)S(1)}, u32[]{:S(2)}, u32[]{:S(2)}) collective-permute-start(f32[16,512]{1,0:T(8,128)S(1)} %source.1.source_ref), channel_id=1, source_target_pairs={{0,192},{1,193},{2,194},{3,195},{4,196},{5,197},{6,198},{7,199},{8... | collective-permute-start | bytes 98312 | tf_op jit(solution)/shard_map/ppermute | solution.py:255

commit v7 on v6

--- a/solution.py
+++ b/solution.py
@@ -76,23 +76,29 @@
     return jnp.where(row == index_ref[level], 1.0, 0.0).astype(BF16)
 
 
-def leaf_kernel(chunk, mine_ref, theirs_ref, index_ref, coupling_ref, hh_ref, hl_ref, inverse_ref, term_ref, u_ref, ah_ref, al_ref, a_ref, sems):
+def leaf_kernel(chunk, mine_ref, theirs_ref, index_ref, coupling_ref, eh_ref, el_ref, inverse_ref, term_ref, u_ref, rh_ref, rl_ref, ah_ref, al_ref, a_ref, sems):
     n, half = mine_ref.shape
     levels, _, k = index_ref.shape
     side = lax.axis_index("sep")
-    firsts = [(1 - side) * half + s * chunk for s in range(half // chunk)]
+    early, rest = eh_ref.shape[0], rh_ref.shape[0]
+    firsts = [side * half + (early + s) * chunk for s in range(rest)]
+    firsts += [(1 - side) * half + s * chunk for s in range(half // chunk)]
     copies = load_columns(inverse_ref, firsts, chunk, a_ref, sems)
     total = jnp.zeros((2 * n, half), F32)
-    for s in range(half // chunk):
+    for s in range(early):
         x = paired(mine_ref[:, s * chunk:(s + 1) * chunk])
-        total = total + (dot(x, hh_ref[s], NT) + dot(x, hl_ref[s], NT))
+        total = total + (dot(x, eh_ref[s], NT) + dot(x, el_ref[s], NT))
     hot = [one_hot(index_ref, level, half, side * half) for level in range(levels)]
     for s, copy in enumerate(copies):
-        x = paired(theirs_ref[:, s * chunk:(s + 1) * chunk])
+        mine = s < rest
+        x_ref, high_ref, low_ref = (mine_ref, rh_ref, rl_ref) if mine else (theirs_ref, ah_ref, al_ref)
+        to = s if mine else s - rest
+        at = early + s if mine else to
+        x = paired(x_ref[:, at * chunk:(at + 1) * chunk])
         copy.wait()
         ah, al = split(a_ref[s])
-        ah_ref[s] = ah
-        al_ref[s] = al
+        high_ref[to] = ah
+        low_ref[to] = al
         total = total + (dot(x, ah, NT) + dot(x, al, NT))
     u = total[:n] + total[n:]
     u_ref[...] = u
@@ -117,18 +123,21 @@
         low_ref[level * k:(level + 1) * k, :] = moved[k:]
 
 
-def back_kernel(first, last, u_ref, high_ref, low_ref, ah_ref, al_ref, out_ref):
+def back_kernel(u_ref, high_ref, low_ref, *refs):
+    *refs, out_ref = refs
     n = u_ref.shape[0]
     uh, ul = split(u_ref[...])
     low = low_ref[...]
     left = jnp.concatenate([high_ref[...], uh, ul], axis=0)
     m = low.shape[0]
-    chunk = ah_ref.shape[2]
-    for s in range(first, last, 2):
-        taken = range(s, min(s + 2, last))
-        cols = slice((s - first) * chunk, (taken[-1] + 1 - first) * chunk)
-        ah = jnp.concatenate([ah_ref[i] for i in taken], axis=1)
-        al = jnp.concatenate([al_ref[i] for i in taken], axis=1)
+    chunk = refs[0].shape[2]
+    highs, lows = [
+        [ref.at[s] for ref in some for s in range(ref.shape[0])] for some in (refs[::2], refs[1::2])
+    ]
+    for s in range(0, len(highs), 2):
+        cols = slice(s * chunk, (s + 2) * chunk)
+        ah = jnp.concatenate([ref[...] for ref in highs[s:s + 2]], axis=1)
+        al = jnp.concatenate([ref[...] for ref in lows[s:s + 2]], axis=1)
         one = dot(left, ah)
         three = dot(left[:m + n], al)
         out_ref[:m, cols] = one[:m] + dot(low, ah) + three[:m]
@@ -268,26 +277,30 @@
     m = levels * k
     chunk = 256
     steps = half // chunk
-    slots = [pltpu.VMEM((steps, half, chunk), F32), pltpu.SemaphoreType.DMA((steps,))]
-    parts = [shape(steps, half, chunk, dtype=BF16)] * 2
+    early = 1
+    slots = lambda count: [pltpu.VMEM((count, half, chunk), F32), pltpu.SemaphoreType.DMA((count,))]
+    parts = lambda count: [shape(count, half, chunk, dtype=BF16)] * 2
     theirs = swap_core(mine)
-    home = call("load", functools.partial(load_kernel, chunk), parts, [HBM], slots, limit=48)(inverse)
-    term, u, *away = call("leaf", functools.partial(leaf_kernel, chunk), [shape(n, m), shape(n, half)] + parts,
-                          [VMEM] * 6 + [HBM], slots, limit=43)(mine, theirs, index, coupling, *home, inverse)
+    first = call("load", functools.partial(load_kernel, chunk), parts(early), [HBM], slots(early), limit=51)(inverse)
+    term, u, *rest = call(
+        "leaf", functools.partial(leaf_kernel, chunk),
+        [shape(n, m), shape(n, half)] + parts(steps - early) + parts(steps),
+        [VMEM] * 6 + [HBM], slots(2 * steps - early), limit=44)(mine, theirs, index, coupling, *first, inverse)
+    home, away = (*first, *rest[:2]), rest[2:]
     term, index, coupling = ordered(term, index, coupling)
     got = swap_core(term)
     high, low = call("spread", spread_kernel, [shape(m, half, dtype=BF16)] * 2, [VMEM, VMEM])(index, coupling)
     term, high, low, got = ordered(term, high, low, got)
     total = term + got
 
-    def back(u, split_inverse, first, last):
-        out, = call("back", functools.partial(back_kernel, first, last), [shape(m + n, (last - first) * chunk)],
-                    [VMEM] * 5)(u, high, low, *split_inverse)
+    def back(u, split_inverse):
+        out, = call("back", back_kernel, [shape(m + n, half)], [VMEM] * (3 + len(split_inverse)))(
+            u, high, low, *split_inverse)
         return out
 
     total, u = ordered(total, u)
     heard = [swap_leaf(total, *masks) for masks in ((1, 1), (24, 8), (16, 25), (17, 9))]
-    sent0 = back(u, away, 0, steps)
+    sent0 = back(u, away)
     total, sent0, *heard = ordered(total, sent0, *heard)
     total, = call("octet", octet_kernel, [shape(n, m)], [VMEM] * 5)(total, *heard)
     total, sep_inverse, sep_parent, sep_rhs = ordered(total, sep_inverse, sep_parent, sep_rhs)
@@ -301,7 +314,7 @@
     total, u, sent0 = ordered(total, u, sent0)
     received0 = swap_core(sent0)
     heard = [swap_leaf(total, *masks) for masks in ((1, 32), (34, 2), (38, 6), (37, 5))]
-    kept0 = back(u, home, 0, steps)
+    kept0 = back(u, home)
     total, kept0, *heard = ordered(total, kept0, *heard)
     part, = call("pair", pair_kernel, [shape(n, 2 * m)], [VMEM] * 5)(total, *heard)
     part, own, sep_inverse, sep_parent = ordered(part, own, sep_inverse, sep_parent)

time: 41 us -> 40.1 us (0.978)
  Pallas kernels: 16.4 us -> 15.5 us
    pallas_call x3, Pallas kernels: 7.88 us -> 6.89 us  [the longest x2 5.48 us: back(): call('back', back_kernel, [shape(m + n, half)], [VMEM] * (3 + len(split_i...]
  transfers between devices with their start and end apart: 14 -> 14, of which waited for: 5 -> 5; matrix products, arithmetic and copies ran while one was open for 0% -> 0% of each run, Pallas kernels for 27% -> 26%
where the time goes in v7:
time: 40.1 us; the launch traced here: 40 us
  starting transfers between devices  20.8 us (52%)
  Pallas kernels  15.5 us (39%)
  waiting for transfers between devices  2.94 us (7%)
  between operations  0.81 us (2%)
    ppermute x9, starting transfers between devices, swap_leaf(): lax.ppermute(x, ('leaf', 'sep'), [(i, i ^ 2 * masks[i % 2]) for i in rang...  16.4 us
    pallas_call x2, Pallas kernels, back(): call('back', back_kernel, [shape(m + n, half)], [VMEM] * (3 + len(split_i...  5.48 us
    ppermute x5, starting transfers between devices, swap_core(): return lax.ppermute(x, 'sep', [(0, 1), (1, 0)])  4.34 us
    pallas_call x1, Pallas kernels, local(): call('leaf', functools.partial(leaf_kernel, chunk), [shape(n, m), shape(n...  4.14 us
    ppermute x9, waiting for transfers between devices, swap_leaf(): lax.ppermute(x, ('leaf', 'sep'), [(i, i ^ 2 * masks[i % 2]) for i in rang...  1.58 us
    pallas_call x1, Pallas kernels, local(): call('load', functools.partial(load_kernel, chunk), parts(early), [HBM],...  1.41 us
    ppermute x5, waiting for transfers between devices, swap_core(): return lax.ppermute(x, 'sep', [(0, 1), (1, 0)])  1.36 us
    pallas_call x1, Pallas kernels, local(): call('last', last_kernel, [shape(n, half), shape(levels, n, k)], [VMEM] * 8)  1.09 us
  transfers between devices with their start and end apart: 14, of which 5 were waited for; matrix products, arithmetic and copies ran while one was open for 0% of the time, Pallas kernels for 26%

profile of v7, /device:TPU:1, one launch (start us, length us, event | category | flops | bytes accessed | tf_op | source)
XLA Modules:
  0.0 40.0 jit_solution(9958157756378289640)
XLA Ops:
  0.6 3.3 %collective-permute-start = (f32[16,1024]{1,0:T(8,128)}, f32[16,1024]{1,0:T(8,128)S(1)}, u32[]{:S(2)}, u32[]{:S(2)}) collective-permute-start(f32[16,1024]{1,0:T(8,128)} %bitcast.8), channel_id=1, source_target_pairs={{0,1},{1,0},{2,3},{3,2},{4,5},{5,4},{6,7},{7,6},{8,9},{9,8},{10,11... | collective-permute-start | bytes 196616 | tf_op jit(solution)/shard_map/ppermute | solution.py:258
  4.0 1.4 %load.1 = (bf16[1,1024,256]{2,1,0:T(8,128)(2,1)S(1)}, bf16[1,1024,256]{2,1,0:T(8,128)(2,1)S(1)}) custom-call(f32[1024,2048]{1,0:T(8,128)} %bitcast.12), custom_call_target="tpu_custom_call" | custom-call | tf_op jit(solution)/shard_map/load/pallas_call | solution.py:284
  5.4 4.1 %leaf.1 = (f32[16,384]{1,0:T(8,128)S(1)}, f32[16,1024]{1,0:T(8,128)S(1)}, bf16[3,1024,256]{2,1,0:T(8,128)(2,1)S(1)}, bf16[3,1024,256]{2,1,0:T(8,128)(2,1)S(1)}, ...) custom-call(f32[16,1024]{1,0:T(8,128)S(1)} %bitcast.9, ...), custom_call_target="tpu_custom_call" | custom-call | tf_op jit(solution)/shard_map/leaf/pallas_call | solution.py:285
  9.7 0.6 %spread.1 = (bf16[384,1024]{1,0:T(8,128)(2,1)S(1)}, bf16[384,1024]{1,0:T(8,128)(2,1)S(1)}) custom-call(s32[3,1,128]{2,1,0:T(1,128)S(1)} %bitcast.11, f32[3,128,128]{2,1,0:T(8,128)S(1)} %bitcast.7), custom_call_target="tpu_custom_call" | custom-call | tf_op jit(solution)/shard_map/spread/pallas_call | solution.py:292
  10.3 0.6 %collective-permute-done.1 = f32[16,384]{1,0:T(8,128)S(1)} collective-permute-done((f32[16,384]{1,0:T(8,128)S(1)}, f32[16,384]{1,0:T(8,128)S(1)}, u32[]{:S(2)}, u32[]{:S(2)}) %collective-permute-start.1) | collective-permute-done | bytes 24608 | tf_op jit(solution)/shard_map/ppermute | solution.py:258
  10.9 2.5 %collective-permute-start.5 = (f32[16,384]{1,0:T(8,128)S(1)}, f32[16,384]{1,0:T(8,128)S(1)}, u32[]{:S(2)}, u32[]{:S(2)}) collective-permute-start(f32[16,384]{1,0:T(8,128)S(1)} %add.6.total_ref), channel_id=1, source_target_pairs={{0,18},{1,35},{2,16},{3,33},{4,22},{5,39},{6,20},{7,37},{8,26},{9,... | collective-permute-start | bytes 73736 | tf_op jit(solution)/shard_map/ppermute | solution.py:264
  13.4 2.7 %collective-permute-start.3 = (f32[16,384]{1,0:T(8,128)S(1)}, f32[16,384]{1,0:T(8,128)S(1)}, u32[]{:S(2)}, u32[]{:S(2)}) collective-permute-start(f32[16,384]{1,0:T(8,128)S(1)} %add.6.total_ref), channel_id=1, source_target_pairs={{0,16},{1,49},{2,18},{3,51},{4,20},{5,53},{6,22},{7,55},{8,24},{9,... | collective-permute-start | bytes 73736 | tf_op jit(solution)/shard_map/ppermute | solution.py:264
  16.2 2.7 %back.2 = f32[400,1024]{1,0:T(8,128)S(1)} custom-call(f32[16,1024]{1,0:T(8,128)S(1)} %get-tuple-element.101.u_ref, bf16[384,1024]{1,0:T(8,128)(2,1)S(1)} %get-tuple-element.83.high_ref, bf16[384,1024]{1,0:T(8,128)(2,1)S(1)} %get-tuple-element.84.low_ref, bf16[4,1024,256]{2,1,0:T(8,128)(2,1)S(1)} %get-tuple-element.85.refs_0_, ...), custom_call_target="tpu_custom_call" | custom-call | tf_op jit(solution)/shard_map/back/pallas_call | solution.py:297
  19.0 0.4 %collective-permute-start.6 = (f32[16,384]{1,0:T(8,128)S(1)}, f32[16,384]{1,0:T(8,128)S(1)}, u32[]{:S(2)}, u32[]{:S(2)}) collective-permute-start(f32[16,384]{1,0:T(8,128)S(1)} %octet.1), channel_id=1, source_target_pairs={{0,1},{1,0},{2,3},{3,2},{4,5},{5,4},{6,7},{7,6},{8,9},{9,8},{10,11... | collective-permute-start | bytes 73736 | tf_op jit(solution)/shard_map/ppermute | solution.py:258
  19.5 0.5 %tree.1 = (bf16[128,384]{1,0:T(8,128)(2,1)S(1)}, bf16[128,384]{1,0:T(8,128)(2,1)S(1)}, f32[5,128,128]{2,1,0:T(8,128)S(1)}, f32[16,512]{1,0:T(8,128)S(1)}) custom-call(f32[7,128,128]{2,1,0:T(8,128)S(1)} %copy-done, f32[6,128,128]{2,1,0:T(8,128)S(1)} %copy-done.1, f32[7,16,128]{2,1,0:T(8,128)S(1)} %copy-done.4), custom_call_target="tpu_custom_call" | custom-call | tf_op jit(solution)/shard_map/tree/pallas_call | solution.py:308
  19.9 0.4 collective-permute-done.6
  20.3 0.3 collective-permute-start.12
  20.6 7.0 %collective-permute-start.10 = (f32[16,384]{1,0:T(8,128)S(1)}, f32[16,384]{1,0:T(8,128)S(1)}, u32[]{:S(2)}, u32[]{:S(2)}) collective-permute-start(f32[16,384]{1,0:T(8,128)S(1)} %add.7.total_ref), channel_id=1, source_target_pairs={{0,10},{1,75},{2,8},{3,73},{4,14},{5,79},{6,12},{7,77},{8,2},{9,67... | collective-permute-start | bytes 73736 | tf_op jit(solution)/shard_map/ppermute | solution.py:264
  27.9 0.9 %collective-permute-start.8 = (f32[16,384]{1,0:T(8,128)S(1)}, f32[16,384]{1,0:T(8,128)S(1)}, u32[]{:S(2)}, u32[]{:S(2)}) collective-permute-start(f32[16,384]{1,0:T(8,128)S(1)} %add.7.total_ref), channel_id=1, source_target_pairs={{0,4},{1,69},{2,6},{3,71},{4,0},{5,65},{6,2},{7,67},{8,12},{9,77},... | collective-permute-start | bytes 73736 | tf_op jit(solution)/shard_map/ppermute | solution.py:264
  28.8 0.7 %collective-permute-start.7 = (f32[16,384]{1,0:T(8,128)S(1)}, f32[16,384]{1,0:T(8,128)S(1)}, u32[]{:S(2)}, u32[]{:S(2)}) collective-permute-start(f32[16,384]{1,0:T(8,128)S(1)} %add.7.total_ref), channel_id=1, source_target_pairs={{0,64},{1,3},{2,66},{3,1},{4,68},{5,7},{6,70},{7,5},{8,72},{9,11},... | collective-permute-start | bytes 73736 | tf_op jit(solution)/shard_map/ppermute | solution.py:264
  29.6 2.7 %back.3.mine_ref = f32[400,1024]{1,0:T(8,128)S(1)} custom-call(f32[16,1024]{1,0:T(8,128)S(1)} %get-tuple-element.101.u_ref, bf16[384,1024]{1,0:T(8,128)(2,1)S(1)} %get-tuple-element.83.high_ref, bf16[384,1024]{1,0:T(8,128)(2,1)S(1)} %get-tuple-element.84.low_ref, bf16[1,1024,256]{2,1,0:T(8,128)(2,1)S(1)} %get-tuple-element.70.eh_ref.refs_0_, ...), custom_call_target="tpu_custom_call" | custom-call | tf_op jit(solution)/shard_map/back/pallas_call | solution.py:297
  32.3 1.2 %collective-permute-done.9.six_ref = f32[16,384]{1,0:T(8,128)S(1)} collective-permute-done((f32[16,384]{1,0:T(8,128)S(1)}, f32[16,384]{1,0:T(8,128)S(1)}, u32[]{:S(2)}, u32[]{:S(2)}) %collective-permute-start.9) | collective-permute-done | bytes 24608 | tf_op jit(solution)/shard_map/ppermute | solution.py:264
  33.6 0.8 %root.1 = (bf16[128,384]{1,0:T(8,128)(2,1)S(1)}, bf16[128,384]{1,0:T(8,128)(2,1)S(1)}, f32[128,384]{1,0:T(8,128)S(1)}) custom-call(f32[7,128,128]{2,1,0:T(8,128)S(1)} %copy-done, f32[6,128,128]{2,1,0:T(8,128)S(1)} %copy-done.1, f32[5,128,128]{2,1,0:T(8,128)S(1)} %get-tuple-element.113.own_ref), custom_call_target="tpu_custom_call" | custom-call | tf_op jit(solution)/shard_map/root/pallas_call | solution.py:322
  34.4 0.4 %collective-permute-done.11.got_ref = f32[16,768]{1,0:T(8,128)S(1)} collective-permute-done((f32[16,768]{1,0:T(8,128)S(1)}, f32[16,768]{1,0:T(8,128)S(1)}, u32[]{:S(2)}, u32[]{:S(2)}) %collective-permute-start.11) | collective-permute-done | bytes 49184 | tf_op jit(solution)/shard_map/ppermute | solution.py:258
  34.9 2.2 %collective-permute-start.13 = (f32[16,512]{1,0:T(8,128)S(1)}, f32[16,512]{1,0:T(8,128)S(1)}, u32[]{:S(2)}, u32[]{:S(2)}) collective-permute-start(f32[16,512]{1,0:T(8,128)S(1)} %source.1.source_ref), channel_id=1, source_target_pairs={{0,192},{1,193},{2,194},{3,195},{4,196},{5,197},{6,198},{7,199},{8... | collective-permute-start | bytes 98312 | tf_op jit(solution)/shard_map/ppermute | solution.py:264
  37.0 0.7 %join.1 = (f32[16,1024]{1,0:T(8,128)S(1)}, f32[256,1024]{1,0:T(8,128)S(1)}, bf16[128,1408]{1,0:T(8,128)(2,1)S(1)}, bf16[128,1408]{1,0:T(8,128)(2,1)S(1)}) custom-call(f32[400,1024]{1,0:T(8,128)S(1)} %back.3.mine_ref, f32[400,1024]{1,0:T(8,128)S(1)} %collective-permute-done.12.got_ref, f32[128,384]{1,0:T(8,128)S(1)} %get-tuple-element.124.root_ref), custom_call_target="tpu_custom_call" | custom-call | tf_op jit(solution)/shard_map/join/pallas_call | solution.py:329
  37.7 0.8 %lower.1 = (f32[16,1024]{1,0:T(8,128)S(1)}, f32[2,16,128]{2,1,0:T(8,128)S(1)}, f32[16,128]{1,0:T(8,128)S(1)}) custom-call(f32[16,512]{1,0:T(8,128)S(1)} %source.1.source_ref, f32[16,512]{1,0:T(8,128)S(1)} %get-tuple-element.117.chosen_ref, bf16[128,384]{1,0:T(8,128)(2,1)S(1)} %get-tuple-element.120.wayh_ref, ...), custom_call_target="tpu_custom_call" | custom-call | tf_op jit(solution)/shard_map/lower/pallas_call | solution.py:332
  38.5 0.4 collective-permute-done.13.other_ref
  38.9 1.1 %last.1 = (f32[16,1024]{1,0:T(8,128)}, f32[3,16,128]{2,1,0:T(8,128)}) custom-call(f32[16,512]{1,0:T(8,128)S(1)} %collective-permute-done.13.other_ref, bf16[128,384]{1,0:T(8,128)(2,1)S(1)} %get-tuple-element.129.wayh_ref, bf16[128,384]{1,0:T(8,128)(2,1)S(1)} %get-tuple-element.130.wayl_ref, f32[16,128]{1,0:T(8,128)S(1)} %get-tuple-element.131.top_ref, ...), custom_call_target="tpu_custom_call" | custom-call | tf_op jit(solution)/shard_map/last/pallas_call | solution.py:335
  (31 shorter events, 0.6 us)
Async XLA Ops:
  0.6 4.8 %collective-permute-start = (f32[16,1024]{1,0:T(8,128)}, f32[16,1024]{1,0:T(8,128)S(1)}, u32[]{:S(2)}, u32[]{:S(2)}) collective-permute-start(f32[16,1024]{1,0:T(8,128)} %bitcast.8), channel_id=1, source_target_pairs={{0,1},{1,0},{2,3},{3,2},{4,5},{5,4},{6,7},{7,6},{8,9},{9,8},{10,11... | collective-permute-start | bytes 196616 | tf_op jit(solution)/shard_map/ppermute | solution.py:258
  4.0 1.4 %copy-start.2 = (f32[1,3,128,128]{3,2,1,0:T(8,128)S(1)}, f32[1,3,128,128]{3,2,1,0:T(8,128)}, u32[]{:S(2)}) copy-start(f32[1,3,128,128]{3,2,1,0:T(8,128)} %param.10) | copy-start | bytes 589828
  4.0 1.4 %copy-start.3 = (f32[1,16,1024]{2,1,0:T(8,128)S(1)}, f32[1,16,1024]{2,1,0:T(8,128)}, u32[]{:S(2)}) copy-start(f32[1,16,1024]{2,1,0:T(8,128)} %param.7) | copy-start | bytes 196612
  4.0 1.5 %copy-start.5 = (s32[1,3,128]{2,0,1:T(1,128)S(1)}, s32[1,3,128]{2,0,1:T(1,128)}, u32[]{:S(2)}) copy-start(s32[1,3,128]{2,0,1:T(1,128)} %param.9) | copy-start | bytes 4612
  9.6 1.3 %collective-permute-start.1 = (f32[16,384]{1,0:T(8,128)S(1)}, f32[16,384]{1,0:T(8,128)S(1)}, u32[]{:S(2)}, u32[]{:S(2)}) collective-permute-start(f32[16,384]{1,0:T(8,128)S(1)} %get-tuple-element.78), channel_id=1, source_target_pairs={{0,1},{1,0},{2,3},{3,2},{4,5},{5,4},{6,7},{7,6},{8,9},{9,8},{10,11... | collective-permute-start | bytes 73736 | tf_op jit(solution)/shard_map/ppermute | solution.py:258
  10.9 8.1 %collective-permute-start.5 = (f32[16,384]{1,0:T(8,128)S(1)}, f32[16,384]{1,0:T(8,128)S(1)}, u32[]{:S(2)}, u32[]{:S(2)}) collective-permute-start(f32[16,384]{1,0:T(8,128)S(1)} %add.6.total_ref), channel_id=1, source_target_pairs={{0,18},{1,35},{2,16},{3,33},{4,22},{5,39},{6,20},{7,37},{8,26},{9,... | collective-permute-start | bytes 73736 | tf_op jit(solution)/shard_map/ppermute | solution.py:264
  13.4 5.6 %collective-permute-start.4 = (f32[16,384]{1,0:T(8,128)S(1)}, f32[16,384]{1,0:T(8,128)S(1)}, u32[]{:S(2)}, u32[]{:S(2)}) collective-permute-start(f32[16,384]{1,0:T(8,128)S(1)} %add.6.total_ref), channel_id=1, source_target_pairs={{0,50},{1,33},{2,48},{3,35},{4,54},{5,37},{6,52},{7,39},{8,58},{9,... | collective-permute-start | bytes 73736 | tf_op jit(solution)/shard_map/ppermute | solution.py:264
  13.4 5.5 %collective-permute-start.3 = (f32[16,384]{1,0:T(8,128)S(1)}, f32[16,384]{1,0:T(8,128)S(1)}, u32[]{:S(2)}, u32[]{:S(2)}) collective-permute-start(f32[16,384]{1,0:T(8,128)S(1)} %add.6.total_ref), channel_id=1, source_target_pairs={{0,16},{1,49},{2,18},{3,51},{4,20},{5,53},{6,22},{7,55},{8,24},{9,... | collective-permute-start | bytes 73736 | tf_op jit(solution)/shard_map/ppermute | solution.py:264
  16.2 2.8 %collective-permute-start.2 = (f32[16,384]{1,0:T(8,128)S(1)}, f32[16,384]{1,0:T(8,128)S(1)}, u32[]{:S(2)}, u32[]{:S(2)}) collective-permute-start(f32[16,384]{1,0:T(8,128)S(1)} %add.6.total_ref), channel_id=1, source_target_pairs={{0,2},{1,3},{2,0},{3,1},{4,6},{5,7},{6,4},{7,5},{8,10},{9,11},{10,... | collective-permute-start | bytes 73736 | tf_op jit(solution)/shard_map/ppermute | solution.py:264
  16.2 3.3 %copy-start = (f32[7,128,128]{2,1,0:T(8,128)S(1)}, f32[7,128,128]{2,1,0:T(8,128)}, u32[]{:S(2)}) copy-start(f32[7,128,128]{2,1,0:T(8,128)} %inverse_ref.1) | copy-start | bytes 1376260
  16.2 3.3 %copy-start.1 = (f32[6,128,128]{2,1,0:T(8,128)S(1)}, f32[6,128,128]{2,1,0:T(8,128)}, u32[]{:S(2)}) copy-start(f32[6,128,128]{2,1,0:T(8,128)} %parent_ref.1) | copy-start | bytes 1179652
  16.2 3.3 %copy-start.4 = (f32[7,16,128]{2,1,0:T(8,128)S(1)}, f32[7,16,128]{2,1,0:T(8,128)}, u32[]{:S(2)}) copy-start(f32[7,16,128]{2,1,0:T(8,128)} %rhs_ref) | copy-start | bytes 172036
  19.0 1.3 %collective-permute-start.6 = (f32[16,384]{1,0:T(8,128)S(1)}, f32[16,384]{1,0:T(8,128)S(1)}, u32[]{:S(2)}, u32[]{:S(2)}) collective-permute-start(f32[16,384]{1,0:T(8,128)S(1)} %octet.1), channel_id=1, source_target_pairs={{0,1},{1,0},{2,3},{3,2},{4,5},{5,4},{6,7},{7,6},{8,9},{9,8},{10,11... | collective-permute-start | bytes 73736 | tf_op jit(solution)/shard_map/ppermute | solution.py:258
  20.3 16.7 %collective-permute-start.12 = (f32[400,1024]{1,0:T(8,128)S(1)}, f32[400,1024]{1,0:T(8,128)S(1)}, u32[]{:S(2)}, u32[]{:S(2)}) collective-permute-start(f32[400,1024]{1,0:T(8,128)S(1)} %back.2), channel_id=1, source_target_pairs={{0,1},{1,0},{2,3},{3,2},{4,5},{5,4},{6,7},{7,6},{8,9},{9,8},{10,11... | collective-permute-start | bytes 4915208 | tf_op jit(solution)/shard_map/ppermute | solution.py:258
  20.6 11.7 %collective-permute-start.10 = (f32[16,384]{1,0:T(8,128)S(1)}, f32[16,384]{1,0:T(8,128)S(1)}, u32[]{:S(2)}, u32[]{:S(2)}) collective-permute-start(f32[16,384]{1,0:T(8,128)S(1)} %add.7.total_ref), channel_id=1, source_target_pairs={{0,10},{1,75},{2,8},{3,73},{4,14},{5,79},{6,12},{7,77},{8,2},{9,67... | collective-permute-start | bytes 73736 | tf_op jit(solution)/shard_map/ppermute | solution.py:264
  27.7 5.8 %collective-permute-start.9 = (f32[16,384]{1,0:T(8,128)S(1)}, f32[16,384]{1,0:T(8,128)S(1)}, u32[]{:S(2)}, u32[]{:S(2)}) collective-permute-start(f32[16,384]{1,0:T(8,128)S(1)} %add.7.total_ref), channel_id=1, source_target_pairs={{0,12},{1,77},{2,14},{3,79},{4,8},{5,73},{6,10},{7,75},{8,4},{9,69... | collective-permute-start | bytes 73736 | tf_op jit(solution)/shard_map/ppermute | solution.py:264
  27.9 5.6 %collective-permute-start.8 = (f32[16,384]{1,0:T(8,128)S(1)}, f32[16,384]{1,0:T(8,128)S(1)}, u32[]{:S(2)}, u32[]{:S(2)}) collective-permute-start(f32[16,384]{1,0:T(8,128)S(1)} %add.7.total_ref), channel_id=1, source_target_pairs={{0,4},{1,69},{2,6},{3,71},{4,0},{5,65},{6,2},{7,67},{8,12},{9,77},... | collective-permute-start | bytes 73736 | tf_op jit(solution)/shard_map/ppermute | solution.py:264
  28.8 4.7 %collective-permute-start.7 = (f32[16,384]{1,0:T(8,128)S(1)}, f32[16,384]{1,0:T(8,128)S(1)}, u32[]{:S(2)}, u32[]{:S(2)}) collective-permute-start(f32[16,384]{1,0:T(8,128)S(1)} %add.7.total_ref), channel_id=1, source_target_pairs={{0,64},{1,3},{2,66},{3,1},{4,68},{5,7},{6,70},{7,5},{8,72},{9,11},... | collective-permute-start | bytes 73736 | tf_op jit(solution)/shard_map/ppermute | solution.py:264
  33.5 1.3 %collective-permute-start.11 = (f32[16,768]{1,0:T(8,128)S(1)}, f32[16,768]{1,0:T(8,128)S(1)}, u32[]{:S(2)}, u32[]{:S(2)}) collective-permute-start(f32[16,768]{1,0:T(8,128)S(1)} %pair.1.part_ref), channel_id=1, source_target_pairs={{0,1},{1,0},{2,3},{3,2},{4,5},{5,4},{6,7},{7,6},{8,9},{9,8},{10,11... | collective-permute-start | bytes 147464 | tf_op jit(solution)/shard_map/ppermute | solution.py:258
  34.9 4.1 %collective-permute-start.13 = (f32[16,512]{1,0:T(8,128)S(1)}, f32[16,512]{1,0:T(8,128)S(1)}, u32[]{:S(2)}, u32[]{:S(2)}) collective-permute-start(f32[16,512]{1,0:T(8,128)S(1)} %source.1.source_ref), channel_id=1, source_target_pairs={{0,192},{1,193},{2,194},{3,195},{4,196},{5,197},{6,198},{7,199},{8... | collective-permute-start | bytes 98312 | tf_op jit(solution)/shard_map/ppermute | solution.py:264

commit v8 on v7

--- a/solution.py
+++ b/solution.py
@@ -210,18 +210,16 @@
     out_ref[...] = one_ref[...] + two_ref[...] + three_ref[...] + jnp.where(first, own, 0.0)
 
 
-def pair_kernel(total_ref, near_ref, five_ref, six_ref, two_ref, out_ref):
-    m = total_ref.shape[1]
+def pair_kernel(total_ref, near_ref, two_ref, six_ref, five_ref, out_ref):
+    own = jnp.where(lax.axis_index("sep") == 0, total_ref[...], near_ref[...])
+    out_ref[...] = own + two_ref[...] + six_ref[...] + five_ref[...]
+
+
+def source_kernel(part_ref, got_ref, chosen_ref, out_ref):
+    k = part_ref.shape[1] // 3
     first = lax.axis_index("sep") == 0
-    heard = five_ref[...] + six_ref[...] + two_ref[...]
-    out_ref[:, :m] = jnp.where(first, total_ref[...] + heard, 0.0)
-    out_ref[:, m:] = jnp.where(first, near_ref[...], heard)
-
-
-def source_kernel(part_ref, got_ref, chosen_ref, out_ref):
-    k = part_ref.shape[1] // 6
-    own = part_ref[:, :3 * k] + got_ref[:, :3 * k]
-    other = part_ref[:, 3 * k:] + got_ref[:, 3 * k:]
+    part, got = part_ref[...], got_ref[...]
+    own, other = jnp.where(first, part, got), jnp.where(first, got, part)
     out_ref[:, :k] = chosen_ref[:, :k] - own[:, k:2 * k] - other[:, k:2 * k]
     out_ref[:, k:2 * k] = chosen_ref[:, k:2 * k] - own[:, :k]
     out_ref[:, 2 * k:3 * k] = chosen_ref[:, 2 * k:3 * k] - other[:, :k]
@@ -313,10 +311,10 @@
 
     total, u, sent0 = ordered(total, u, sent0)
     received0 = swap_core(sent0)
-    heard = [swap_leaf(total, *masks) for masks in ((1, 32), (34, 2), (38, 6), (37, 5))]
+    heard = [swap_leaf(total, *masks) for masks in ((32, 1), (34, 2), (39, 7), (37, 5))]
     kept0 = back(u, home)
     total, kept0, *heard = ordered(total, kept0, *heard)
-    part, = call("pair", pair_kernel, [shape(n, 2 * m)], [VMEM] * 5)(total, *heard)
+    part, = call("pair", pair_kernel, [shape(n, m)], [VMEM] * 5)(total, *heard)
     part, own, sep_inverse, sep_parent = ordered(part, own, sep_inverse, sep_parent)
     got = swap_core(part)
     otherh, otherl, root = call(

time: 40.1 us -> 39.8 us (level)
  waiting for transfers between devices: 2.94 us -> 1.88 us
    ppermute x9, waiting for transfers between devices: 1.58 us -> 0.55 us  [swap_leaf(): lax.ppermute(x, ('leaf', 'sep'), [(i, i ^ 2 * masks[i % 2]) for i in rang...]
  transfers between devices with their start and end apart: 14 -> 14, of which waited for: 5 -> 4; matrix products, arithmetic and copies ran while one was open for 0% -> 0% of each run, Pallas kernels for 26% -> 26%
where the time goes in v8:
time: 39.8 us; the launch traced here: 39.3 us
  starting transfers between devices  21.1 us (53%)
  Pallas kernels  15.5 us (39%)
  waiting for transfers between devices  1.88 us (5%)
  between operations  0.83 us (2%)
    ppermute x9, starting transfers between devices, swap_leaf(): lax.ppermute(x, ('leaf', 'sep'), [(i, i ^ 2 * masks[i % 2]) for i in rang...  16.8 us
    pallas_call x2, Pallas kernels, back(): call('back', back_kernel, [shape(m + n, half)], [VMEM] * (3 + len(split_i...  5.48 us
    ppermute x5, starting transfers between devices, swap_core(): return lax.ppermute(x, 'sep', [(0, 1), (1, 0)])  4.34 us
    pallas_call x1, Pallas kernels, local(): call('leaf', functools.partial(leaf_kernel, chunk), [shape(n, m), shape(n...  4.14 us
    pallas_call x1, Pallas kernels, local(): call('load', functools.partial(load_kernel, chunk), parts(early), [HBM],...  1.41 us
    ppermute x5, waiting for transfers between devices, swap_core(): return lax.ppermute(x, 'sep', [(0, 1), (1, 0)])  1.33 us
    pallas_call x1, Pallas kernels, local(): call('last', last_kernel, [shape(n, half), shape(levels, n, k)], [VMEM] * 8)  1.09 us
    pallas_call x1, Pallas kernels, local(): call('lower', lower_kernel, [shape(n, half), shape(2, n, k), shape(n, k)]...  0.82 us
  transfers between devices with their start and end apart: 14, of which 4 were waited for; matrix products, arithmetic and copies ran while one was open for 0% of the time, Pallas kernels for 26%

profile of v8, /device:TPU:1, one launch (start us, length us, event | category | flops | bytes accessed | tf_op | source)
XLA Modules:
  0.0 39.3 jit_solution(7118024033657395178)
XLA Ops:
  0.6 3.3 %collective-permute-start = (f32[16,1024]{1,0:T(8,128)}, f32[16,1024]{1,0:T(8,128)S(1)}, u32[]{:S(2)}, u32[]{:S(2)}) collective-permute-start(f32[16,1024]{1,0:T(8,128)} %bitcast.8), channel_id=1, source_target_pairs={{0,1},{1,0},{2,3},{3,2},{4,5},{5,4},{6,7},{7,6},{8,9},{9,8},{10,11... | collective-permute-start | bytes 196616 | tf_op jit(solution)/shard_map/ppermute | solution.py:256
  4.0 1.4 %load.1 = (bf16[1,1024,256]{2,1,0:T(8,128)(2,1)S(1)}, bf16[1,1024,256]{2,1,0:T(8,128)(2,1)S(1)}) custom-call(f32[1024,2048]{1,0:T(8,128)} %bitcast.12), custom_call_target="tpu_custom_call" | custom-call | tf_op jit(solution)/shard_map/load/pallas_call | solution.py:282
  5.4 4.1 %leaf.1 = (f32[16,384]{1,0:T(8,128)S(1)}, f32[16,1024]{1,0:T(8,128)S(1)}, bf16[3,1024,256]{2,1,0:T(8,128)(2,1)S(1)}, bf16[3,1024,256]{2,1,0:T(8,128)(2,1)S(1)}, ...) custom-call(f32[16,1024]{1,0:T(8,128)S(1)} %bitcast.9, ...), custom_call_target="tpu_custom_call" | custom-call | tf_op jit(solution)/shard_map/leaf/pallas_call | solution.py:283
  9.6 0.1 collective-permute-start.1
  9.7 0.6 %spread.1 = (bf16[384,1024]{1,0:T(8,128)(2,1)S(1)}, bf16[384,1024]{1,0:T(8,128)(2,1)S(1)}) custom-call(s32[3,1,128]{2,1,0:T(1,128)S(1)} %bitcast.11, f32[3,128,128]{2,1,0:T(8,128)S(1)} %bitcast.7), custom_call_target="tpu_custom_call" | custom-call | tf_op jit(solution)/shard_map/spread/pallas_call | solution.py:290
  10.3 0.6 %collective-permute-done.1 = f32[16,384]{1,0:T(8,128)S(1)} collective-permute-done((f32[16,384]{1,0:T(8,128)S(1)}, f32[16,384]{1,0:T(8,128)S(1)}, u32[]{:S(2)}, u32[]{:S(2)}) %collective-permute-start.1) | collective-permute-done | bytes 24608 | tf_op jit(solution)/shard_map/ppermute | solution.py:256
  10.9 2.5 %collective-permute-start.5 = (f32[16,384]{1,0:T(8,128)S(1)}, f32[16,384]{1,0:T(8,128)S(1)}, u32[]{:S(2)}, u32[]{:S(2)}) collective-permute-start(f32[16,384]{1,0:T(8,128)S(1)} %add.6.total_ref), channel_id=1, source_target_pairs={{0,18},{1,35},{2,16},{3,33},{4,22},{5,39},{6,20},{7,37},{8,26},{9,... | collective-permute-start | bytes 73736 | tf_op jit(solution)/shard_map/ppermute | solution.py:262
  13.4 2.7 %collective-permute-start.3 = (f32[16,384]{1,0:T(8,128)S(1)}, f32[16,384]{1,0:T(8,128)S(1)}, u32[]{:S(2)}, u32[]{:S(2)}) collective-permute-start(f32[16,384]{1,0:T(8,128)S(1)} %add.6.total_ref), channel_id=1, source_target_pairs={{0,16},{1,49},{2,18},{3,51},{4,20},{5,53},{6,22},{7,55},{8,24},{9,... | collective-permute-start | bytes 73736 | tf_op jit(solution)/shard_map/ppermute | solution.py:262
  16.2 2.7 %back.2 = f32[400,1024]{1,0:T(8,128)S(1)} custom-call(f32[16,1024]{1,0:T(8,128)S(1)} %get-tuple-element.101.u_ref, bf16[384,1024]{1,0:T(8,128)(2,1)S(1)} %get-tuple-element.83.high_ref, bf16[384,1024]{1,0:T(8,128)(2,1)S(1)} %get-tuple-element.84.low_ref, bf16[4,1024,256]{2,1,0:T(8,128)(2,1)S(1)} %get-tuple-element.85.refs_0_, ...), custom_call_target="tpu_custom_call" | custom-call | tf_op jit(solution)/shard_map/back/pallas_call | solution.py:295
  19.0 0.4 %collective-permute-start.6 = (f32[16,384]{1,0:T(8,128)S(1)}, f32[16,384]{1,0:T(8,128)S(1)}, u32[]{:S(2)}, u32[]{:S(2)}) collective-permute-start(f32[16,384]{1,0:T(8,128)S(1)} %octet.1), channel_id=1, source_target_pairs={{0,1},{1,0},{2,3},{3,2},{4,5},{5,4},{6,7},{7,6},{8,9},{9,8},{10,11... | collective-permute-start | bytes 73736 | tf_op jit(solution)/shard_map/ppermute | solution.py:256
  19.5 0.5 %tree.1 = (bf16[128,384]{1,0:T(8,128)(2,1)S(1)}, bf16[128,384]{1,0:T(8,128)(2,1)S(1)}, f32[5,128,128]{2,1,0:T(8,128)S(1)}, f32[16,512]{1,0:T(8,128)S(1)}) custom-call(f32[7,128,128]{2,1,0:T(8,128)S(1)} %copy-done, f32[6,128,128]{2,1,0:T(8,128)S(1)} %copy-done.1, f32[7,16,128]{2,1,0:T(8,128)S(1)} %copy-done.4), custom_call_target="tpu_custom_call" | custom-call | tf_op jit(solution)/shard_map/tree/pallas_call | solution.py:306
  19.9 0.4 collective-permute-done.6
  20.3 0.3 collective-permute-start.12
  20.6 7.0 %collective-permute-start.10 = (f32[16,384]{1,0:T(8,128)S(1)}, f32[16,384]{1,0:T(8,128)S(1)}, u32[]{:S(2)}, u32[]{:S(2)}) collective-permute-start(f32[16,384]{1,0:T(8,128)S(1)} %add.7.total_ref), channel_id=1, source_target_pairs={{0,10},{1,75},{2,8},{3,73},{4,14},{5,79},{6,12},{7,77},{8,2},{9,67... | collective-permute-start | bytes 73736 | tf_op jit(solution)/shard_map/ppermute | solution.py:262
  27.7 1.2 %collective-permute-start.8 = (f32[16,384]{1,0:T(8,128)S(1)}, f32[16,384]{1,0:T(8,128)S(1)}, u32[]{:S(2)}, u32[]{:S(2)}) collective-permute-start(f32[16,384]{1,0:T(8,128)S(1)} %add.7.total_ref), channel_id=1, source_target_pairs={{0,4},{1,69},{2,6},{3,71},{4,0},{5,65},{6,2},{7,67},{8,12},{9,77},... | collective-permute-start | bytes 73736 | tf_op jit(solution)/shard_map/ppermute | solution.py:262
  28.9 1.2 %collective-permute-start.7 = (f32[16,384]{1,0:T(8,128)S(1)}, f32[16,384]{1,0:T(8,128)S(1)}, u32[]{:S(2)}, u32[]{:S(2)}) collective-permute-start(f32[16,384]{1,0:T(8,128)S(1)} %add.7.total_ref), channel_id=1, source_target_pairs={{0,2},{1,65},{2,0},{3,67},{4,6},{5,69},{6,4},{7,71},{8,10},{9,73},... | collective-permute-start | bytes 73736 | tf_op jit(solution)/shard_map/ppermute | solution.py:262
  30.1 2.7 %back.3.mine_ref = f32[400,1024]{1,0:T(8,128)S(1)} custom-call(f32[16,1024]{1,0:T(8,128)S(1)} %get-tuple-element.101.u_ref, bf16[384,1024]{1,0:T(8,128)(2,1)S(1)} %get-tuple-element.83.high_ref, bf16[384,1024]{1,0:T(8,128)(2,1)S(1)} %get-tuple-element.84.low_ref, bf16[1,1024,256]{2,1,0:T(8,128)(2,1)S(1)} %get-tuple-element.70.eh_ref.refs_0_, ...), custom_call_target="tpu_custom_call" | custom-call | tf_op jit(solution)/shard_map/back/pallas_call | solution.py:295
  33.0 0.8 %root.1 = (bf16[128,384]{1,0:T(8,128)(2,1)S(1)}, bf16[128,384]{1,0:T(8,128)(2,1)S(1)}, f32[128,384]{1,0:T(8,128)S(1)}) custom-call(f32[7,128,128]{2,1,0:T(8,128)S(1)} %copy-done, f32[6,128,128]{2,1,0:T(8,128)S(1)} %copy-done.1, f32[5,128,128]{2,1,0:T(8,128)S(1)} %get-tuple-element.113.own_ref), custom_call_target="tpu_custom_call" | custom-call | tf_op jit(solution)/shard_map/root/pallas_call | solution.py:320
  33.8 0.4 %collective-permute-done.11.got_ref = f32[16,384]{1,0:T(8,128)S(1)} collective-permute-done((f32[16,384]{1,0:T(8,128)S(1)}, f32[16,384]{1,0:T(8,128)S(1)}, u32[]{:S(2)}, u32[]{:S(2)}) %collective-permute-start.11) | collective-permute-done | bytes 24608 | tf_op jit(solution)/shard_map/ppermute | solution.py:256
  34.2 2.0 %collective-permute-start.13 = (f32[16,512]{1,0:T(8,128)S(1)}, f32[16,512]{1,0:T(8,128)S(1)}, u32[]{:S(2)}, u32[]{:S(2)}) collective-permute-start(f32[16,512]{1,0:T(8,128)S(1)} %source.1.source_ref), channel_id=1, source_target_pairs={{0,192},{1,193},{2,194},{3,195},{4,196},{5,197},{6,198},{7,199},{8... | collective-permute-start | bytes 98312 | tf_op jit(solution)/shard_map/ppermute | solution.py:262
  36.2 0.7 %join.1 = (f32[16,1024]{1,0:T(8,128)S(1)}, f32[256,1024]{1,0:T(8,128)S(1)}, bf16[128,1408]{1,0:T(8,128)(2,1)S(1)}, bf16[128,1408]{1,0:T(8,128)(2,1)S(1)}) custom-call(f32[400,1024]{1,0:T(8,128)S(1)} %back.3.mine_ref, f32[400,1024]{1,0:T(8,128)S(1)} %collective-permute-done.12.got_ref, f32[128,384]{1,0:T(8,128)S(1)} %get-tuple-element.124.root_ref), custom_call_target="tpu_custom_call" | custom-call | tf_op jit(solution)/shard_map/join/pallas_call | solution.py:327
  36.9 0.8 %lower.1 = (f32[16,1024]{1,0:T(8,128)S(1)}, f32[2,16,128]{2,1,0:T(8,128)S(1)}, f32[16,128]{1,0:T(8,128)S(1)}) custom-call(f32[16,512]{1,0:T(8,128)S(1)} %source.1.source_ref, f32[16,512]{1,0:T(8,128)S(1)} %get-tuple-element.117.chosen_ref, bf16[128,384]{1,0:T(8,128)(2,1)S(1)} %get-tuple-element.120.wayh_ref, ...), custom_call_target="tpu_custom_call" | custom-call | tf_op jit(solution)/shard_map/lower/pallas_call | solution.py:330
  37.7 0.5 %collective-permute-done.13.other_ref = f32[16,512]{1,0:T(8,128)S(1)} collective-permute-done((f32[16,512]{1,0:T(8,128)S(1)}, f32[16,512]{1,0:T(8,128)S(1)}, u32[]{:S(2)}, u32[]{:S(2)}) %collective-permute-start.13) | collective-permute-done | bytes 32800 | tf_op jit(solution)/shard_map/ppermute | solution.py:262
  38.2 1.1 %last.1 = (f32[16,1024]{1,0:T(8,128)}, f32[3,16,128]{2,1,0:T(8,128)}) custom-call(f32[16,512]{1,0:T(8,128)S(1)} %collective-permute-done.13.other_ref, bf16[128,384]{1,0:T(8,128)(2,1)S(1)} %get-tuple-element.129.wayh_ref, bf16[128,384]{1,0:T(8,128)(2,1)S(1)} %get-tuple-element.130.wayl_ref, f32[16,128]{1,0:T(8,128)S(1)} %get-tuple-element.131.top_ref, ...), custom_call_target="tpu_custom_call" | custom-call | tf_op jit(solution)/shard_map/last/pallas_call | solution.py:333
  (31 shorter events, 0.3 us)
Async XLA Ops:
  0.6 4.8 %collective-permute-start = (f32[16,1024]{1,0:T(8,128)}, f32[16,1024]{1,0:T(8,128)S(1)}, u32[]{:S(2)}, u32[]{:S(2)}) collective-permute-start(f32[16,1024]{1,0:T(8,128)} %bitcast.8), channel_id=1, source_target_pairs={{0,1},{1,0},{2,3},{3,2},{4,5},{5,4},{6,7},{7,6},{8,9},{9,8},{10,11... | collective-permute-start | bytes 196616 | tf_op jit(solution)/shard_map/ppermute | solution.py:256
  4.0 1.4 %copy-start.2 = (f32[1,3,128,128]{3,2,1,0:T(8,128)S(1)}, f32[1,3,128,128]{3,2,1,0:T(8,128)}, u32[]{:S(2)}) copy-start(f32[1,3,128,128]{3,2,1,0:T(8,128)} %param.10) | copy-start | bytes 589828
  4.0 1.4 %copy-start.3 = (f32[1,16,1024]{2,1,0:T(8,128)S(1)}, f32[1,16,1024]{2,1,0:T(8,128)}, u32[]{:S(2)}) copy-start(f32[1,16,1024]{2,1,0:T(8,128)} %param.7) | copy-start | bytes 196612
  4.0 1.5 %copy-start.5 = (s32[1,3,128]{2,0,1:T(1,128)S(1)}, s32[1,3,128]{2,0,1:T(1,128)}, u32[]{:S(2)}) copy-start(s32[1,3,128]{2,0,1:T(1,128)} %param.9) | copy-start | bytes 4612
  9.6 1.3 %collective-permute-start.1 = (f32[16,384]{1,0:T(8,128)S(1)}, f32[16,384]{1,0:T(8,128)S(1)}, u32[]{:S(2)}, u32[]{:S(2)}) collective-permute-start(f32[16,384]{1,0:T(8,128)S(1)} %get-tuple-element.78), channel_id=1, source_target_pairs={{0,1},{1,0},{2,3},{3,2},{4,5},{5,4},{6,7},{7,6},{8,9},{9,8},{10,11... | collective-permute-start | bytes 73736 | tf_op jit(solution)/shard_map/ppermute | solution.py:256
  10.9 8.1 %collective-permute-start.5 = (f32[16,384]{1,0:T(8,128)S(1)}, f32[16,384]{1,0:T(8,128)S(1)}, u32[]{:S(2)}, u32[]{:S(2)}) collective-permute-start(f32[16,384]{1,0:T(8,128)S(1)} %add.6.total_ref), channel_id=1, source_target_pairs={{0,18},{1,35},{2,16},{3,33},{4,22},{5,39},{6,20},{7,37},{8,26},{9,... | collective-permute-start | bytes 73736 | tf_op jit(solution)/shard_map/ppermute | solution.py:262
  13.4 5.6 %collective-permute-start.4 = (f32[16,384]{1,0:T(8,128)S(1)}, f32[16,384]{1,0:T(8,128)S(1)}, u32[]{:S(2)}, u32[]{:S(2)}) collective-permute-start(f32[16,384]{1,0:T(8,128)S(1)} %add.6.total_ref), channel_id=1, source_target_pairs={{0,50},{1,33},{2,48},{3,35},{4,54},{5,37},{6,52},{7,39},{8,58},{9,... | collective-permute-start | bytes 73736 | tf_op jit(solution)/shard_map/ppermute | solution.py:262
  13.4 5.5 %collective-permute-start.3 = (f32[16,384]{1,0:T(8,128)S(1)}, f32[16,384]{1,0:T(8,128)S(1)}, u32[]{:S(2)}, u32[]{:S(2)}) collective-permute-start(f32[16,384]{1,0:T(8,128)S(1)} %add.6.total_ref), channel_id=1, source_target_pairs={{0,16},{1,49},{2,18},{3,51},{4,20},{5,53},{6,22},{7,55},{8,24},{9,... | collective-permute-start | bytes 73736 | tf_op jit(solution)/shard_map/ppermute | solution.py:262
  16.2 2.8 %collective-permute-start.2 = (f32[16,384]{1,0:T(8,128)S(1)}, f32[16,384]{1,0:T(8,128)S(1)}, u32[]{:S(2)}, u32[]{:S(2)}) collective-permute-start(f32[16,384]{1,0:T(8,128)S(1)} %add.6.total_ref), channel_id=1, source_target_pairs={{0,2},{1,3},{2,0},{3,1},{4,6},{5,7},{6,4},{7,5},{8,10},{9,11},{10,... | collective-permute-start | bytes 73736 | tf_op jit(solution)/shard_map/ppermute | solution.py:262
  16.2 3.3 %copy-start = (f32[7,128,128]{2,1,0:T(8,128)S(1)}, f32[7,128,128]{2,1,0:T(8,128)}, u32[]{:S(2)}) copy-start(f32[7,128,128]{2,1,0:T(8,128)} %inverse_ref.1) | copy-start | bytes 1376260
  16.2 3.3 %copy-start.1 = (f32[6,128,128]{2,1,0:T(8,128)S(1)}, f32[6,128,128]{2,1,0:T(8,128)}, u32[]{:S(2)}) copy-start(f32[6,128,128]{2,1,0:T(8,128)} %parent_ref.1) | copy-start | bytes 1179652
  16.2 3.3 %copy-start.4 = (f32[7,16,128]{2,1,0:T(8,128)S(1)}, f32[7,16,128]{2,1,0:T(8,128)}, u32[]{:S(2)}) copy-start(f32[7,16,128]{2,1,0:T(8,128)} %rhs_ref) | copy-start | bytes 172036
  19.0 1.3 %collective-permute-start.6 = (f32[16,384]{1,0:T(8,128)S(1)}, f32[16,384]{1,0:T(8,128)S(1)}, u32[]{:S(2)}, u32[]{:S(2)}) collective-permute-start(f32[16,384]{1,0:T(8,128)S(1)} %octet.1), channel_id=1, source_target_pairs={{0,1},{1,0},{2,3},{3,2},{4,5},{5,4},{6,7},{7,6},{8,9},{9,8},{10,11... | collective-permute-start | bytes 73736 | tf_op jit(solution)/shard_map/ppermute | solution.py:256
  20.3 15.9 %collective-permute-start.12 = (f32[400,1024]{1,0:T(8,128)S(1)}, f32[400,1024]{1,0:T(8,128)S(1)}, u32[]{:S(2)}, u32[]{:S(2)}) collective-permute-start(f32[400,1024]{1,0:T(8,128)S(1)} %back.2), channel_id=1, source_target_pairs={{0,1},{1,0},{2,3},{3,2},{4,5},{5,4},{6,7},{7,6},{8,9},{9,8},{10,11... | collective-permute-start | bytes 4915208 | tf_op jit(solution)/shard_map/ppermute | solution.py:256
  20.6 12.2 %collective-permute-start.10 = (f32[16,384]{1,0:T(8,128)S(1)}, f32[16,384]{1,0:T(8,128)S(1)}, u32[]{:S(2)}, u32[]{:S(2)}) collective-permute-start(f32[16,384]{1,0:T(8,128)S(1)} %add.7.total_ref), channel_id=1, source_target_pairs={{0,10},{1,75},{2,8},{3,73},{4,14},{5,79},{6,12},{7,77},{8,2},{9,67... | collective-permute-start | bytes 73736 | tf_op jit(solution)/shard_map/ppermute | solution.py:262
  27.7 5.2 %collective-permute-start.9 = (f32[16,384]{1,0:T(8,128)S(1)}, f32[16,384]{1,0:T(8,128)S(1)}, u32[]{:S(2)}, u32[]{:S(2)}) collective-permute-start(f32[16,384]{1,0:T(8,128)S(1)} %add.7.total_ref), channel_id=1, source_target_pairs={{0,14},{1,79},{2,12},{3,77},{4,10},{5,75},{6,8},{7,73},{8,6},{9,71... | collective-permute-start | bytes 73736 | tf_op jit(solution)/shard_map/ppermute | solution.py:262
  27.7 5.2 %collective-permute-start.8 = (f32[16,384]{1,0:T(8,128)S(1)}, f32[16,384]{1,0:T(8,128)S(1)}, u32[]{:S(2)}, u32[]{:S(2)}) collective-permute-start(f32[16,384]{1,0:T(8,128)S(1)} %add.7.total_ref), channel_id=1, source_target_pairs={{0,4},{1,69},{2,6},{3,71},{4,0},{5,65},{6,2},{7,67},{8,12},{9,77},... | collective-permute-start | bytes 73736 | tf_op jit(solution)/shard_map/ppermute | solution.py:262
  28.9 4.0 %collective-permute-start.7 = (f32[16,384]{1,0:T(8,128)S(1)}, f32[16,384]{1,0:T(8,128)S(1)}, u32[]{:S(2)}, u32[]{:S(2)}) collective-permute-start(f32[16,384]{1,0:T(8,128)S(1)} %add.7.total_ref), channel_id=1, source_target_pairs={{0,2},{1,65},{2,0},{3,67},{4,6},{5,69},{6,4},{7,71},{8,10},{9,73},... | collective-permute-start | bytes 73736 | tf_op jit(solution)/shard_map/ppermute | solution.py:262
  32.9 1.3 %collective-permute-start.11 = (f32[16,384]{1,0:T(8,128)S(1)}, f32[16,384]{1,0:T(8,128)S(1)}, u32[]{:S(2)}, u32[]{:S(2)}) collective-permute-start(f32[16,384]{1,0:T(8,128)S(1)} %pair.1.part_ref), channel_id=1, source_target_pairs={{0,1},{1,0},{2,3},{3,2},{4,5},{5,4},{6,7},{7,6},{8,9},{9,8},{10,11... | collective-permute-start | bytes 73736 | tf_op jit(solution)/shard_map/ppermute | solution.py:256
  34.2 4.1 %collective-permute-start.13 = (f32[16,512]{1,0:T(8,128)S(1)}, f32[16,512]{1,0:T(8,128)S(1)}, u32[]{:S(2)}, u32[]{:S(2)}) collective-permute-start(f32[16,512]{1,0:T(8,128)S(1)} %source.1.source_ref), channel_id=1, source_target_pairs={{0,192},{1,193},{2,194},{3,195},{4,196},{5,197},{6,198},{7,199},{8... | collective-permute-start | bytes 98312 | tf_op jit(solution)/shard_map/ppermute | solution.py:262

commit v9 on v8

--- a/solution.py
+++ b/solution.py
@@ -123,7 +123,7 @@
         low_ref[level * k:(level + 1) * k, :] = moved[k:]
 
 
-def back_kernel(u_ref, high_ref, low_ref, *refs):
+def back_kernel(first, last, u_ref, high_ref, low_ref, *refs):
     *refs, out_ref = refs
     n = u_ref.shape[0]
     uh, ul = split(u_ref[...])
@@ -134,10 +134,11 @@
     highs, lows = [
         [ref.at[s] for ref in some for s in range(ref.shape[0])] for some in (refs[::2], refs[1::2])
     ]
-    for s in range(0, len(highs), 2):
-        cols = slice(s * chunk, (s + 2) * chunk)
-        ah = jnp.concatenate([ref[...] for ref in highs[s:s + 2]], axis=1)
-        al = jnp.concatenate([ref[...] for ref in lows[s:s + 2]], axis=1)
+    for s in range(first, last, 2):
+        end = min(s + 2, last)
+        cols = slice((s - first) * chunk, (end - first) * chunk)
+        ah = jnp.concatenate([ref[...] for ref in highs[s:end]], axis=1)
+        al = jnp.concatenate([ref[...] for ref in lows[s:end]], axis=1)
         one = dot(left, ah)
         three = dot(left[:m + n], al)
         out_ref[:m, cols] = one[:m] + dot(low, ah) + three[:m]
@@ -189,12 +190,12 @@
     return [ref.at[:, s:s + chunk] for ref in refs for s in range(0, ref.shape[1], chunk)]
 
 
-def join_kernel(chunk, mine_ref, got_ref, root_ref, base_ref, low_ref, qh_ref, ql_ref):
+def join_kernel(chunk, mine_ref, got0_ref, got1_ref, root_ref, base_ref, low_ref, qh_ref, ql_ref):
     k = root_ref.shape[0]
     root = root_ref[...]
     m = root.shape[1]
     width = base_ref.shape[1]
-    pairs = zip(columns_of((mine_ref,), chunk), columns_of((got_ref,), chunk))
+    pairs = zip(columns_of((mine_ref,), chunk), columns_of((got0_ref, got1_ref), chunk))
     for s, (mine_ref, got_ref) in enumerate(pairs):
         cols = slice(s * chunk, (s + 1) * chunk)
         b = mine_ref[:m, :] + got_ref[:m, :]
@@ -291,14 +292,14 @@
     term, high, low, got = ordered(term, high, low, got)
     total = term + got
 
-    def back(u, split_inverse):
-        out, = call("back", back_kernel, [shape(m + n, half)], [VMEM] * (3 + len(split_inverse)))(
-            u, high, low, *split_inverse)
+    def back(u, split_inverse, first, last):
+        out, = call("back", functools.partial(back_kernel, first, last), [shape(m + n, (last - first) * chunk)],
+                    [VMEM] * (3 + len(split_inverse)))(u, high, low, *split_inverse)
         return out
 
     total, u = ordered(total, u)
     heard = [swap_leaf(total, *masks) for masks in ((1, 1), (24, 8), (16, 25), (17, 9))]
-    sent0 = back(u, away)
+    sent0 = back(u, away, 0, steps - 1)
     total, sent0, *heard = ordered(total, sent0, *heard)
     total, = call("octet", octet_kernel, [shape(n, m)], [VMEM] * 5)(total, *heard)
     total, sep_inverse, sep_parent, sep_rhs = ordered(total, sep_inverse, sep_parent, sep_rhs)
@@ -312,8 +313,9 @@
     total, u, sent0 = ordered(total, u, sent0)
     received0 = swap_core(sent0)
     heard = [swap_leaf(total, *masks) for masks in ((32, 1), (34, 2), (39, 7), (37, 5))]
-    kept0 = back(u, home)
-    total, kept0, *heard = ordered(total, kept0, *heard)
+    sent1 = back(u, away, steps - 1, steps)
+    kept0 = back(u, home, 0, steps)
+    total, sent1, kept0, *heard = ordered(total, sent1, kept0, *heard)
     part, = call("pair", pair_kernel, [shape(n, m)], [VMEM] * 5)(total, *heard)
     part, own, sep_inverse, sep_parent = ordered(part, own, sep_inverse, sep_parent)
     got = swap_core(part)
@@ -322,11 +324,12 @@
     part, got, root = ordered(part, got, root)
     source, = call("source", source_kernel, [shape(n, m + k)], [VMEM] * 3)(part, got, chosen)
 
-    source, u, root = ordered(source, u, root)
+    source, sent1, root = ordered(source, sent1, root)
     other = swap_leaf(source, 96)
+    received1 = swap_core(sent1)
     base, lower, qh, ql = call("join", functools.partial(join_kernel, chunk),
                                [shape(n, half), shape(2 * k, half)] + [shape(k, half + m, dtype=BF16)] * 2,
-                               [VMEM] * 3)(kept0, received0, root)
+                               [VMEM] * 4)(kept0, received0, received1, root)
     pre, solved, top = call("lower", lower_kernel, [shape(n, half), shape(2, n, k), shape(n, k)], [VMEM] * 7)(
         source, chosen, wayh, wayl, own, base, lower)
     pre, other = ordered(pre, other)

time: 39.8 us -> 40 us (level)
  waiting for transfers between devices: 1.88 us -> 2.67 us
  starting transfers between devices: 21.1 us -> 20.6 us
    ppermute x9, waiting for transfers between devices: 0.55 us -> 1.03 us  [swap_leaf(): lax.ppermute(x, ('leaf', 'sep'), [(i, i ^ 2 * masks[i % 2]) for i in rang...]
    ppermute x5 -> x6, waiting for transfers between devices: 1.33 us -> 1.64 us  [swap_core(): return lax.ppermute(x, 'sep', [(0, 1), (1, 0)])]
    ppermute x5 -> x6, starting transfers between devices: 4.34 us -> 4.07 us  [swap_core(): return lax.ppermute(x, 'sep', [(0, 1), (1, 0)])]
    pallas_call x2 -> x3, Pallas kernels: 5.48 us -> 5.68 us  [back(): call('back', functools.partial(back_kernel, first, last), [shape(m + n, (...]
  transfers between devices with their start and end apart: 14 -> 15, of which waited for: 4 -> 5; matrix products, arithmetic and copies ran while one was open for 0% -> 0% of each run, Pallas kernels for 26% -> 26%
where the time goes in v9:
time: 40 us; the launch traced here: 39.9 us
  starting transfers between devices  20.6 us (52%)
  Pallas kernels  15.7 us (39%)
  waiting for transfers between devices  2.67 us (7%)
  between operations  0.85 us (2%)
    ppermute x9, starting transfers between devices, swap_leaf(): lax.ppermute(x, ('leaf', 'sep'), [(i, i ^ 2 * masks[i % 2]) for i in rang...  16.5 us
    pallas_call x3, Pallas kernels, back(): call('back', functools.partial(back_kernel, first, last), [shape(m + n, (...  5.68 us
    pallas_call x1, Pallas kernels, local(): call('leaf', functools.partial(leaf_kernel, chunk), [shape(n, m), shape(n...  4.14 us
    ppermute x6, starting transfers between devices, swap_core(): return lax.ppermute(x, 'sep', [(0, 1), (1, 0)])  4.07 us
    ppermute x6, waiting for transfers between devices, swap_core(): return lax.ppermute(x, 'sep', [(0, 1), (1, 0)])  1.64 us
    pallas_call x1, Pallas kernels, local(): call('load', functools.partial(load_kernel, chunk), parts(early), [HBM],...  1.41 us
    pallas_call x1, Pallas kernels, local(): call('last', last_kernel, [shape(n, half), shape(levels, n, k)], [VMEM] * 8)  1.09 us
    ppermute x9, waiting for transfers between devices, swap_leaf(): lax.ppermute(x, ('leaf', 'sep'), [(i, i ^ 2 * masks[i % 2]) for i in rang...  1.03 us
  transfers between devices with their start and end apart: 15, of which 5 were waited for; matrix products, arithmetic and copies ran while one was open for 0% of the time, Pallas kernels for 26%

profile of v9, /device:TPU:1, one launch (start us, length us, event | category | flops | bytes accessed | tf_op | source)
XLA Modules:
  0.0 39.9 jit_solution(1722536893886254946)
XLA Ops:
  0.6 3.3 %collective-permute-start = (f32[16,1024]{1,0:T(8,128)}, f32[16,1024]{1,0:T(8,128)S(1)}, u32[]{:S(2)}, u32[]{:S(2)}) collective-permute-start(f32[16,1024]{1,0:T(8,128)} %bitcast.8), channel_id=1, source_target_pairs={{0,1},{1,0},{2,3},{3,2},{4,5},{5,4},{6,7},{7,6},{8,9},{9,8},{10,11... | collective-permute-start | bytes 196616 | tf_op jit(solution)/shard_map/ppermute | solution.py:257
  4.0 1.4 %load.1 = (bf16[1,1024,256]{2,1,0:T(8,128)(2,1)S(1)}, bf16[1,1024,256]{2,1,0:T(8,128)(2,1)S(1)}) custom-call(f32[1024,2048]{1,0:T(8,128)} %bitcast.12), custom_call_target="tpu_custom_call" | custom-call | tf_op jit(solution)/shard_map/load/pallas_call | solution.py:283
  5.4 4.1 %leaf.1 = (f32[16,384]{1,0:T(8,128)S(1)}, f32[16,1024]{1,0:T(8,128)S(1)}, bf16[3,1024,256]{2,1,0:T(8,128)(2,1)S(1)}, bf16[3,1024,256]{2,1,0:T(8,128)(2,1)S(1)}, ...) custom-call(f32[16,1024]{1,0:T(8,128)S(1)} %bitcast.9, ...), custom_call_target="tpu_custom_call" | custom-call | tf_op jit(solution)/shard_map/leaf/pallas_call | solution.py:284
  9.7 0.6 %spread.1 = (bf16[384,1024]{1,0:T(8,128)(2,1)S(1)}, bf16[384,1024]{1,0:T(8,128)(2,1)S(1)}) custom-call(s32[3,1,128]{2,1,0:T(1,128)S(1)} %bitcast.11, f32[3,128,128]{2,1,0:T(8,128)S(1)} %bitcast.7), custom_call_target="tpu_custom_call" | custom-call | tf_op jit(solution)/shard_map/spread/pallas_call | solution.py:291
  10.3 0.6 %collective-permute-done.1 = f32[16,384]{1,0:T(8,128)S(1)} collective-permute-done((f32[16,384]{1,0:T(8,128)S(1)}, f32[16,384]{1,0:T(8,128)S(1)}, u32[]{:S(2)}, u32[]{:S(2)}) %collective-permute-start.1) | collective-permute-done | bytes 24608 | tf_op jit(solution)/shard_map/ppermute | solution.py:257
  10.9 2.5 %collective-permute-start.5 = (f32[16,384]{1,0:T(8,128)S(1)}, f32[16,384]{1,0:T(8,128)S(1)}, u32[]{:S(2)}, u32[]{:S(2)}) collective-permute-start(f32[16,384]{1,0:T(8,128)S(1)} %add.6.total_ref), channel_id=1, source_target_pairs={{0,18},{1,35},{2,16},{3,33},{4,22},{5,39},{6,20},{7,37},{8,26},{9,... | collective-permute-start | bytes 73736 | tf_op jit(solution)/shard_map/ppermute | solution.py:263
  13.4 2.7 %collective-permute-start.3 = (f32[16,384]{1,0:T(8,128)S(1)}, f32[16,384]{1,0:T(8,128)S(1)}, u32[]{:S(2)}, u32[]{:S(2)}) collective-permute-start(f32[16,384]{1,0:T(8,128)S(1)} %add.6.total_ref), channel_id=1, source_target_pairs={{0,16},{1,49},{2,18},{3,51},{4,20},{5,53},{6,22},{7,55},{8,24},{9,... | collective-permute-start | bytes 73736 | tf_op jit(solution)/shard_map/ppermute | solution.py:263
  16.2 2.1 %back.3 = f32[400,768]{1,0:T(8,128)S(1)} custom-call(f32[16,1024]{1,0:T(8,128)S(1)} %get-tuple-element.103.u_ref, bf16[384,1024]{1,0:T(8,128)(2,1)S(1)} %get-tuple-element.85.high_ref, bf16[384,1024]{1,0:T(8,128)(2,1)S(1)} %get-tuple-element.86.low_ref, bf16[4,1024,256]{2,1,0:T(8,128)(2,1)S(1)} %get-tuple-element.87.refs_0_, ...), custom_call_target="tpu_custom_call" | custom-call | tf_op jit(solution)/shard_map/back/pallas_call | solution.py:296
  18.4 0.5 %collective-permute-done.2.four_ref = f32[16,384]{1,0:T(8,128)S(1)} collective-permute-done((f32[16,384]{1,0:T(8,128)S(1)}, f32[16,384]{1,0:T(8,128)S(1)}, u32[]{:S(2)}, u32[]{:S(2)}) %collective-permute-start.2) | collective-permute-done | bytes 24608 | tf_op jit(solution)/shard_map/ppermute | solution.py:263
  19.0 0.5 %tree.1 = (bf16[128,384]{1,0:T(8,128)(2,1)S(1)}, bf16[128,384]{1,0:T(8,128)(2,1)S(1)}, f32[5,128,128]{2,1,0:T(8,128)S(1)}, f32[16,512]{1,0:T(8,128)S(1)}) custom-call(f32[7,128,128]{2,1,0:T(8,128)S(1)} %copy-done, f32[6,128,128]{2,1,0:T(8,128)S(1)} %copy-done.1, f32[7,16,128]{2,1,0:T(8,128)S(1)} %copy-done.4), custom_call_target="tpu_custom_call" | custom-call | tf_op jit(solution)/shard_map/tree/pallas_call | solution.py:307
  19.5 0.7 %collective-permute-done.6 = f32[16,384]{1,0:T(8,128)S(1)} collective-permute-done((f32[16,384]{1,0:T(8,128)S(1)}, f32[16,384]{1,0:T(8,128)S(1)}, u32[]{:S(2)}, u32[]{:S(2)}) %collective-permute-start.6) | collective-permute-done | bytes 24608 | tf_op jit(solution)/shard_map/ppermute | solution.py:257
  20.3 6.9 %collective-permute-start.10 = (f32[16,384]{1,0:T(8,128)S(1)}, f32[16,384]{1,0:T(8,128)S(1)}, u32[]{:S(2)}, u32[]{:S(2)}) collective-permute-start(f32[16,384]{1,0:T(8,128)S(1)} %add.7.total_ref), channel_id=1, source_target_pairs={{0,10},{1,75},{2,8},{3,73},{4,14},{5,79},{6,12},{7,77},{8,2},{9,67... | collective-permute-start | bytes 73736 | tf_op jit(solution)/shard_map/ppermute | solution.py:263
  27.2 1.2 %collective-permute-start.8 = (f32[16,384]{1,0:T(8,128)S(1)}, f32[16,384]{1,0:T(8,128)S(1)}, u32[]{:S(2)}, u32[]{:S(2)}) collective-permute-start(f32[16,384]{1,0:T(8,128)S(1)} %add.7.total_ref), channel_id=1, source_target_pairs={{0,4},{1,69},{2,6},{3,71},{4,0},{5,65},{6,2},{7,67},{8,12},{9,77},... | collective-permute-start | bytes 73736 | tf_op jit(solution)/shard_map/ppermute | solution.py:263
  28.4 1.2 %collective-permute-start.7 = (f32[16,384]{1,0:T(8,128)S(1)}, f32[16,384]{1,0:T(8,128)S(1)}, u32[]{:S(2)}, u32[]{:S(2)}) collective-permute-start(f32[16,384]{1,0:T(8,128)S(1)} %add.7.total_ref), channel_id=1, source_target_pairs={{0,2},{1,65},{2,0},{3,67},{4,6},{5,69},{6,4},{7,71},{8,10},{9,73},... | collective-permute-start | bytes 73736 | tf_op jit(solution)/shard_map/ppermute | solution.py:263
  29.6 0.8 %back.4 = f32[400,256]{1,0:T(8,128)S(1)} custom-call(f32[16,1024]{1,0:T(8,128)S(1)} %get-tuple-element.103.u_ref, bf16[384,1024]{1,0:T(8,128)(2,1)S(1)} %get-tuple-element.85.high_ref, bf16[384,1024]{1,0:T(8,128)(2,1)S(1)} %get-tuple-element.86.low_ref, bf16[4,1024,256]{2,1,0:T(8,128)(2,1)S(1)} %get-tuple-element.87.refs_0_, ...), custom_call_target="tpu_custom_call" | custom-call | tf_op jit(solution)/shard_map/back/pallas_call | solution.py:296
  30.4 2.7 %back.5.mine_ref = f32[400,1024]{1,0:T(8,128)S(1)} custom-call(f32[16,1024]{1,0:T(8,128)S(1)} %get-tuple-element.103.u_ref, bf16[384,1024]{1,0:T(8,128)(2,1)S(1)} %get-tuple-element.85.high_ref, bf16[384,1024]{1,0:T(8,128)(2,1)S(1)} %get-tuple-element.86.low_ref, bf16[1,1024,256]{2,1,0:T(8,128)(2,1)S(1)} %get-tuple-element.72.eh_ref.refs_0_, ...), custom_call_target="tpu_custom_call" | custom-call | tf_op jit(solution)/shard_map/back/pallas_call | solution.py:296
  33.3 0.8 %root.1 = (bf16[128,384]{1,0:T(8,128)(2,1)S(1)}, bf16[128,384]{1,0:T(8,128)(2,1)S(1)}, f32[128,384]{1,0:T(8,128)S(1)}) custom-call(f32[7,128,128]{2,1,0:T(8,128)S(1)} %copy-done, f32[6,128,128]{2,1,0:T(8,128)S(1)} %copy-done.1, f32[5,128,128]{2,1,0:T(8,128)S(1)} %get-tuple-element.115.own_ref), custom_call_target="tpu_custom_call" | custom-call | tf_op jit(solution)/shard_map/root/pallas_call | solution.py:322
  34.1 0.4 collective-permute-done.11.got_ref
  34.5 0.3 collective-permute-start.13
  34.8 2.0 %collective-permute-start.14 = (f32[16,512]{1,0:T(8,128)S(1)}, f32[16,512]{1,0:T(8,128)S(1)}, u32[]{:S(2)}, u32[]{:S(2)}) collective-permute-start(f32[16,512]{1,0:T(8,128)S(1)} %source.1.source_ref), channel_id=1, source_target_pairs={{0,192},{1,193},{2,194},{3,195},{4,196},{5,197},{6,198},{7,199},{8... | collective-permute-start | bytes 98312 | tf_op jit(solution)/shard_map/ppermute | solution.py:263
  36.7 0.7 %join.1 = (f32[16,1024]{1,0:T(8,128)S(1)}, f32[256,1024]{1,0:T(8,128)S(1)}, bf16[128,1408]{1,0:T(8,128)(2,1)S(1)}, bf16[128,1408]{1,0:T(8,128)(2,1)S(1)}) custom-call(f32[400,1024]{1,0:T(8,128)S(1)} %back.5.mine_ref, f32[400,768]{1,0:T(8,128)S(1)} %collective-permute-done.12.got0_ref, f32[400,256]{1,0:T(8,128)S(1)} %collective-permute-done.13.got1_ref, ...), custom_call_target="tpu_custom_call" | custom-call | tf_op jit(solution)/shard_map/join/pallas_call | solution.py:330
  37.4 0.8 %lower.1 = (f32[16,1024]{1,0:T(8,128)S(1)}, f32[2,16,128]{2,1,0:T(8,128)S(1)}, f32[16,128]{1,0:T(8,128)S(1)}) custom-call(f32[16,512]{1,0:T(8,128)S(1)} %source.1.source_ref, f32[16,512]{1,0:T(8,128)S(1)} %get-tuple-element.119.chosen_ref, bf16[128,384]{1,0:T(8,128)(2,1)S(1)} %get-tuple-element.123.wayh_ref, ...), custom_call_target="tpu_custom_call" | custom-call | tf_op jit(solution)/shard_map/lower/pallas_call | solution.py:333
  38.3 0.5 %collective-permute-done.14.other_ref = f32[16,512]{1,0:T(8,128)S(1)} collective-permute-done((f32[16,512]{1,0:T(8,128)S(1)}, f32[16,512]{1,0:T(8,128)S(1)}, u32[]{:S(2)}, u32[]{:S(2)}) %collective-permute-start.14) | collective-permute-done | bytes 32800 | tf_op jit(solution)/shard_map/ppermute | solution.py:263
  38.8 1.1 %last.1 = (f32[16,1024]{1,0:T(8,128)}, f32[3,16,128]{2,1,0:T(8,128)}) custom-call(f32[16,512]{1,0:T(8,128)S(1)} %collective-permute-done.14.other_ref, bf16[128,384]{1,0:T(8,128)(2,1)S(1)} %get-tuple-element.133.wayh_ref, bf16[128,384]{1,0:T(8,128)(2,1)S(1)} %get-tuple-element.134.wayl_ref, f32[16,128]{1,0:T(8,128)S(1)} %get-tuple-element.135.top_ref, ...), custom_call_target="tpu_custom_call" | custom-call | tf_op jit(solution)/shard_map/last/pallas_call | solution.py:336
  (34 shorter events, 0.6 us)
Async XLA Ops:
  0.6 4.8 %collective-permute-start = (f32[16,1024]{1,0:T(8,128)}, f32[16,1024]{1,0:T(8,128)S(1)}, u32[]{:S(2)}, u32[]{:S(2)}) collective-permute-start(f32[16,1024]{1,0:T(8,128)} %bitcast.8), channel_id=1, source_target_pairs={{0,1},{1,0},{2,3},{3,2},{4,5},{5,4},{6,7},{7,6},{8,9},{9,8},{10,11... | collective-permute-start | bytes 196616 | tf_op jit(solution)/shard_map/ppermute | solution.py:257
  4.0 1.4 %copy-start.2 = (f32[1,3,128,128]{3,2,1,0:T(8,128)S(1)}, f32[1,3,128,128]{3,2,1,0:T(8,128)}, u32[]{:S(2)}) copy-start(f32[1,3,128,128]{3,2,1,0:T(8,128)} %param.10) | copy-start | bytes 589828
  4.0 1.4 %copy-start.3 = (f32[1,16,1024]{2,1,0:T(8,128)S(1)}, f32[1,16,1024]{2,1,0:T(8,128)}, u32[]{:S(2)}) copy-start(f32[1,16,1024]{2,1,0:T(8,128)} %param.7) | copy-start | bytes 196612
  4.0 1.5 %copy-start.5 = (s32[1,3,128]{2,0,1:T(1,128)S(1)}, s32[1,3,128]{2,0,1:T(1,128)}, u32[]{:S(2)}) copy-start(s32[1,3,128]{2,0,1:T(1,128)} %param.9) | copy-start | bytes 4612
  9.6 1.3 %collective-permute-start.1 = (f32[16,384]{1,0:T(8,128)S(1)}, f32[16,384]{1,0:T(8,128)S(1)}, u32[]{:S(2)}, u32[]{:S(2)}) collective-permute-start(f32[16,384]{1,0:T(8,128)S(1)} %get-tuple-element.80), channel_id=1, source_target_pairs={{0,1},{1,0},{2,3},{3,2},{4,5},{5,4},{6,7},{7,6},{8,9},{9,8},{10,11... | collective-permute-start | bytes 73736 | tf_op jit(solution)/shard_map/ppermute | solution.py:257
  10.9 7.5 %collective-permute-start.5 = (f32[16,384]{1,0:T(8,128)S(1)}, f32[16,384]{1,0:T(8,128)S(1)}, u32[]{:S(2)}, u32[]{:S(2)}) collective-permute-start(f32[16,384]{1,0:T(8,128)S(1)} %add.6.total_ref), channel_id=1, source_target_pairs={{0,18},{1,35},{2,16},{3,33},{4,22},{5,39},{6,20},{7,37},{8,26},{9,... | collective-permute-start | bytes 73736 | tf_op jit(solution)/shard_map/ppermute | solution.py:263
  13.4 4.9 %collective-permute-start.4 = (f32[16,384]{1,0:T(8,128)S(1)}, f32[16,384]{1,0:T(8,128)S(1)}, u32[]{:S(2)}, u32[]{:S(2)}) collective-permute-start(f32[16,384]{1,0:T(8,128)S(1)} %add.6.total_ref), channel_id=1, source_target_pairs={{0,50},{1,33},{2,48},{3,35},{4,54},{5,37},{6,52},{7,39},{8,58},{9,... | collective-permute-start | bytes 73736 | tf_op jit(solution)/shard_map/ppermute | solution.py:263
  13.4 4.9 %collective-permute-start.3 = (f32[16,384]{1,0:T(8,128)S(1)}, f32[16,384]{1,0:T(8,128)S(1)}, u32[]{:S(2)}, u32[]{:S(2)}) collective-permute-start(f32[16,384]{1,0:T(8,128)S(1)} %add.6.total_ref), channel_id=1, source_target_pairs={{0,16},{1,49},{2,18},{3,51},{4,20},{5,53},{6,22},{7,55},{8,24},{9,... | collective-permute-start | bytes 73736 | tf_op jit(solution)/shard_map/ppermute | solution.py:263
  16.2 2.7 %collective-permute-start.2 = (f32[16,384]{1,0:T(8,128)S(1)}, f32[16,384]{1,0:T(8,128)S(1)}, u32[]{:S(2)}, u32[]{:S(2)}) collective-permute-start(f32[16,384]{1,0:T(8,128)S(1)} %add.6.total_ref), channel_id=1, source_target_pairs={{0,2},{1,3},{2,0},{3,1},{4,6},{5,7},{6,4},{7,5},{8,10},{9,11},{10,... | collective-permute-start | bytes 73736 | tf_op jit(solution)/shard_map/ppermute | solution.py:263
  16.2 2.8 %copy-start = (f32[7,128,128]{2,1,0:T(8,128)S(1)}, f32[7,128,128]{2,1,0:T(8,128)}, u32[]{:S(2)}) copy-start(f32[7,128,128]{2,1,0:T(8,128)} %inverse_ref.1) | copy-start | bytes 1376260
  16.2 2.8 %copy-start.1 = (f32[6,128,128]{2,1,0:T(8,128)S(1)}, f32[6,128,128]{2,1,0:T(8,128)}, u32[]{:S(2)}) copy-start(f32[6,128,128]{2,1,0:T(8,128)} %parent_ref.1) | copy-start | bytes 1179652
  16.2 2.8 %copy-start.4 = (f32[7,16,128]{2,1,0:T(8,128)S(1)}, f32[7,16,128]{2,1,0:T(8,128)}, u32[]{:S(2)}) copy-start(f32[7,16,128]{2,1,0:T(8,128)} %rhs_ref) | copy-start | bytes 172036
  18.9 1.3 %collective-permute-start.6 = (f32[16,384]{1,0:T(8,128)S(1)}, f32[16,384]{1,0:T(8,128)S(1)}, u32[]{:S(2)}, u32[]{:S(2)}) collective-permute-start(f32[16,384]{1,0:T(8,128)S(1)} %octet.1), channel_id=1, source_target_pairs={{0,1},{1,0},{2,3},{3,2},{4,5},{5,4},{6,7},{7,6},{8,9},{9,8},{10,11... | collective-permute-start | bytes 73736 | tf_op jit(solution)/shard_map/ppermute | solution.py:257
  20.2 16.6 %collective-permute-start.12 = (f32[400,768]{1,0:T(8,128)S(1)}, f32[400,768]{1,0:T(8,128)S(1)}, u32[]{:S(2)}, u32[]{:S(2)}) collective-permute-start(f32[400,768]{1,0:T(8,128)S(1)} %back.3), channel_id=1, source_target_pairs={{0,1},{1,0},{2,3},{3,2},{4,5},{5,4},{6,7},{7,6},{8,9},{9,8},{10,11... | collective-permute-start | bytes 3686408 | tf_op jit(solution)/shard_map/ppermute | solution.py:257
  20.3 12.8 %collective-permute-start.10 = (f32[16,384]{1,0:T(8,128)S(1)}, f32[16,384]{1,0:T(8,128)S(1)}, u32[]{:S(2)}, u32[]{:S(2)}) collective-permute-start(f32[16,384]{1,0:T(8,128)S(1)} %add.7.total_ref), channel_id=1, source_target_pairs={{0,10},{1,75},{2,8},{3,73},{4,14},{5,79},{6,12},{7,77},{8,2},{9,67... | collective-permute-start | bytes 73736 | tf_op jit(solution)/shard_map/ppermute | solution.py:263
  27.2 6.0 %collective-permute-start.9 = (f32[16,384]{1,0:T(8,128)S(1)}, f32[16,384]{1,0:T(8,128)S(1)}, u32[]{:S(2)}, u32[]{:S(2)}) collective-permute-start(f32[16,384]{1,0:T(8,128)S(1)} %add.7.total_ref), channel_id=1, source_target_pairs={{0,14},{1,79},{2,12},{3,77},{4,10},{5,75},{6,8},{7,73},{8,6},{9,71... | collective-permute-start | bytes 73736 | tf_op jit(solution)/shard_map/ppermute | solution.py:263
  27.2 6.0 %collective-permute-start.8 = (f32[16,384]{1,0:T(8,128)S(1)}, f32[16,384]{1,0:T(8,128)S(1)}, u32[]{:S(2)}, u32[]{:S(2)}) collective-permute-start(f32[16,384]{1,0:T(8,128)S(1)} %add.7.total_ref), channel_id=1, source_target_pairs={{0,4},{1,69},{2,6},{3,71},{4,0},{5,65},{6,2},{7,67},{8,12},{9,77},... | collective-permute-start | bytes 73736 | tf_op jit(solution)/shard_map/ppermute | solution.py:263
  28.4 4.8 %collective-permute-start.7 = (f32[16,384]{1,0:T(8,128)S(1)}, f32[16,384]{1,0:T(8,128)S(1)}, u32[]{:S(2)}, u32[]{:S(2)}) collective-permute-start(f32[16,384]{1,0:T(8,128)S(1)} %add.7.total_ref), channel_id=1, source_target_pairs={{0,2},{1,65},{2,0},{3,67},{4,6},{5,69},{6,4},{7,71},{8,10},{9,73},... | collective-permute-start | bytes 73736 | tf_op jit(solution)/shard_map/ppermute | solution.py:263
  33.2 1.3 %collective-permute-start.11 = (f32[16,384]{1,0:T(8,128)S(1)}, f32[16,384]{1,0:T(8,128)S(1)}, u32[]{:S(2)}, u32[]{:S(2)}) collective-permute-start(f32[16,384]{1,0:T(8,128)S(1)} %pair.1.part_ref), channel_id=1, source_target_pairs={{0,1},{1,0},{2,3},{3,2},{4,5},{5,4},{6,7},{7,6},{8,9},{9,8},{10,11... | collective-permute-start | bytes 73736 | tf_op jit(solution)/shard_map/ppermute | solution.py:257
  34.5 2.2 %collective-permute-start.13 = (f32[400,256]{1,0:T(8,128)S(1)}, f32[400,256]{1,0:T(8,128)S(1)}, u32[]{:S(2)}, u32[]{:S(2)}) collective-permute-start(f32[400,256]{1,0:T(8,128)S(1)} %back.4), channel_id=1, source_target_pairs={{0,1},{1,0},{2,3},{3,2},{4,5},{5,4},{6,7},{7,6},{8,9},{9,8},{10,11... | collective-permute-start | bytes 1228808 | tf_op jit(solution)/shard_map/ppermute | solution.py:257
  34.8 4.0 %collective-permute-start.14 = (f32[16,512]{1,0:T(8,128)S(1)}, f32[16,512]{1,0:T(8,128)S(1)}, u32[]{:S(2)}, u32[]{:S(2)}) collective-permute-start(f32[16,512]{1,0:T(8,128)S(1)} %source.1.source_ref), channel_id=1, source_target_pairs={{0,192},{1,193},{2,194},{3,195},{4,196},{5,197},{6,198},{7,199},{8... | collective-permute-start | bytes 98312 | tf_op jit(solution)/shard_map/ppermute | solution.py:263
